TPU v7x, 32 devices: a whole 2x2x4 slice. The times are simulated.
32 devices in a mesh: dp: 16 (over z, y, x), mp: 2 (over core).
Axes of the slice: x: 2, y: 2, z: 4, core: 2. Of those that a mesh axis runs over, the one named last changes fastest.
Arguments:
- features: bfloat16 [12288, 768], P('dp'), may hold values from -6 to 6
- lap_vectors: bfloat16 [12288, 16], P('dp'), may hold values from -5 to 5
- node_counts: int32 [96], P('dp'), may hold values from 2 to 51, as said below
- edge_counts: int32 [96], P('dp'), may hold values from 1 to 77, as said below
- endpoints: int32 [12288, 2], P('dp'), may hold values from 0 to 50, as said below
- w_ident: bfloat16 [32, 768], replicated, may hold values from -1 to 1
- type_table: bfloat16 [2, 768], replicated, may hold values from -3 to 3
- gain_one: bfloat16 [768], replicated, may hold values from 0.5 to 1.5
- shift_one: bfloat16 [768], replicated, may hold values from -2 to 2
- w_query: bfloat16 [768, 768], P(None, 'mp'), may hold values from -0.21875 to 0.21875
- w_key: bfloat16 [768, 768], P(None, 'mp'), may hold values from -0.21875 to 0.21875
- w_value: bfloat16 [768, 768], P(None, 'mp'), may hold values from -0.21875 to 0.21875
- bias_query: bfloat16 [768], P('mp'), may hold values from -3 to 3
- bias_value: bfloat16 [768], P('mp'), may hold values from -3 to 3
- w_out: bfloat16 [768, 768], P('mp'), may hold values from -0.875 to 0.875
- bias_out: bfloat16 [768], replicated, may hold values from -2 to 2
- gain_two: bfloat16 [768], replicated, may hold values from 0.5 to 1.5
- shift_two: bfloat16 [768], replicated, may hold values from -2 to 2
- w_up: bfloat16 [768, 768], P(None, 'mp'), may hold values from -0.21875 to 0.21875
- bias_up: bfloat16 [768], P('mp'), may hold values from -3 to 3
- w_down: bfloat16 [768, 768], P('mp'), may hold values from -0.21875 to 0.21875
- bias_down: bfloat16 [768], replicated, may hold values from -2 to 2
- cotangent: bfloat16 [12288, 768], P('dp'), may hold values from -6 to 6
Outputs:
- result: bfloat16 [12288, 768], P(('dp', 'mp'))
- grad_features: float32 [12288, 768], P(('dp', 'mp'))
- grad_w_ident: float32 [32, 768], replicated
- grad_type_table: float32 [2, 768], replicated
- grad_gain_one: float32 [768], replicated
- grad_shift_one: float32 [768], replicated
- grad_w_query: float32 [768, 768], P(None, 'mp')
- grad_w_key: float32 [768, 768], P(None, 'mp')
- grad_w_value: float32 [768, 768], P(None, 'mp')
- grad_bias_query: float32 [768], P('mp')
- grad_bias_value: float32 [768], P('mp')
- grad_w_out: float32 [768, 768], P('mp')
- grad_bias_out: float32 [768], replicated
- grad_gain_two: float32 [768], replicated
- grad_shift_two: float32 [768], replicated
- grad_w_up: float32 [768, 768], P(None, 'mp')
- grad_bias_up: float32 [768], P('mp')
- grad_w_down: float32 [768, 768], P('mp')
- grad_bias_down: float32 [768], replicated
Inputs may be any that keep to these rules, and one draw needn't show every extreme that they name: `node_counts`: some molecule has exactly 51 nodes and some has 2. edge_counts >= node_counts - 1 and node_counts + edge_counts <= 128 for every molecule; some molecule fills all 128 token slots. `endpoints`: in a molecule with n nodes and e edges, slot p < n holds (p, p), slots n to n + e - 1 hold two node indices below n, later slots hold (0, 0).
All inputs are finite; a program needn't handle non-finite values.
Results may differ from a plain program's by a relative error of at most 0.015.
Values may be sent and summed in bfloat16 or wider, within the bound.
No kernel may reach another device: no remote copies, remote signals or barrier semaphores. Data moves between devices by JAX's collectives and lax.ppermute only.
A program may use at most 128 MiB of HBM per device.

v0:
```python
import math

import jax
import jax.numpy as jnp
from jax import lax
from jax.experimental import pallas as pl
from jax.experimental.pallas import tpu as pltpu
from jax.sharding import PartitionSpec as P

HDIM = 24
SEQ = 128
LANES = 128
INNER = 4
OUTER = 4
EPSILON = 1e-05
SCALE = 1.0 / math.sqrt(HDIM)
LOG2_SCALE = SCALE * math.log2(math.e)
F32, BF16 = jnp.float32, jnp.bfloat16
MIB = 1024 * 1024


def dot(left, right):
    return jnp.dot(left, right, preferred_element_type=F32)


def dot_nt(left, right):
    return lax.dot_general(left, right, (((1,), (1,)), ((), ())), preferred_element_type=F32)


def dot_tn(left, right):
    return lax.dot_general(left, right, (((0,), (0,)), ((), ())), preferred_element_type=F32)


def norm_parts(hidden):
    average = jnp.mean(hidden, axis=-1, keepdims=True)
    centred = hidden - average
    inverse = lax.rsqrt(jnp.mean(centred * centred, axis=-1, keepdims=True) + EPSILON)
    return centred * inverse, inverse


def norm_back(unit, inverse, grad_hat):
    return inverse * (
        grad_hat
        - jnp.mean(grad_hat, axis=-1, keepdims=True)
        - unit * jnp.mean(grad_hat * unit, axis=-1, keepdims=True)
    )


def row_sum(block):
    return jnp.sum(block, axis=0, keepdims=True)


def positions(length):
    return lax.broadcasted_iota(jnp.int32, (length, 1), 0)


def whole():
    return pl.BlockSpec(memory_space=pltpu.VMEM)


def outside():
    return pl.BlockSpec(memory_space=pltpu.HBM)


def places():
    index = lax.axis_index("dp")
    return lax.axis_index("mp"), index % INNER, index // INNER % OUTER


def copy_in(sources, targets, sems):
    copies = [
        pltpu.make_async_copy(source, target, sems.at[place])
        for place, (source, target) in enumerate(zip(sources, targets))
    ]
    for copy in copies:
        copy.start()
    return copies


def row_of(ref):
    block = ref[...].astype(F32)
    return jnp.concatenate([block[r : r + 1, :] for r in range(block.shape[0])], axis=1)


def put_row(ref, row):
    for r in range(ref.shape[0]):
        ref[r : r + 1, :] = row[:, r * LANES : (r + 1) * LANES]


def call(kernel, args, specs, outs, scratch=(), micros=0, limit=24, in_place=None):
    return pl.pallas_call(
        kernel,
        out_shape=[jax.ShapeDtypeStruct(shape, kind) for shape, kind in outs],
        in_specs=specs,
        out_specs=[outside() if in_place else whole() for _ in outs],
        input_output_aliases=in_place or {},
        scratch_shapes=list(scratch),
        compiler_params=pltpu.CompilerParams(vmem_limit_bytes=limit * MIB),
        cost_estimate=pl.CostEstimate(
            flops=micros * 1_000_000_000, bytes_accessed=0, transcendentals=0
        ),
    )(*args)


def head_windows(width):
    windows = []
    for pair in range(width // (2 * HDIM)):
        low = pair * 2 * HDIM // LANES * LANES
        high = -(-(pair + 1) * 2 * HDIM // LANES) * LANES
        windows.append((low, high))
    return windows


def split_heads(block, pair, window):
    low, high = window
    part = block[:, low:high]
    column = low + lax.broadcasted_iota(jnp.int32, (16, high - low), 1)
    sides = []
    for head in (2 * pair, 2 * pair + 1):
        inside = (column >= head * HDIM) & (column < (head + 1) * HDIM)
        mask = jnp.where(inside, 1.0, 0.0).astype(BF16)
        sides.append(part * jnp.concatenate([mask] * (block.shape[0] // 16), axis=0))
    return jnp.concatenate(sides, axis=0)


def embed_rows(feats, lap, ends, w_ident, types, gain, shift, at, count):
    table = lap[:, at]
    slot = lax.broadcasted_iota(jnp.int32, (SEQ, SEQ), 0)
    picked = []
    for end in (0, 1):
        pick = jnp.where(ends[end : end + 1, at] == slot, 1.0, 0.0).astype(BF16)
        picked.append(dot(table, pick))
    ident = jnp.concatenate(picked, axis=0).astype(BF16)
    hidden = feats[at, :].astype(F32) + dot_tn(ident, w_ident[...])
    kinds = types[...].astype(F32)
    hidden = hidden + jnp.where(positions(SEQ) >= count, kinds[1:2, :], kinds[0:1, :])
    unit, _ = norm_parts(hidden)
    return hidden, ident, (unit * gain + shift).astype(BF16)


def embed_kernel(
    feats_in, lap_in, ends_in, nodes_in, w_ident_in, types_in, gain_in, shift_in,
    bias_q_in, bias_v_in, wq_in, wk_in, wv_in, edges_in,
    hidden_out, ident_out, normed_out, normed_t_out, q_out, k_out, v_out, keep_out,
    feats, lap, ends, nodes, w_ident, types, gain_rows, shift_rows, bias_q, bias_v,
    w_q, w_k, w_v, edges, sems,
):
    rows, dim = feats.shape
    mols = rows // SEQ
    core = places()[0]
    own_rows = pl.ds(pl.multiple_of(core * rows, SEQ), rows)
    copies = copy_in(
        (
            feats_in.at[own_rows, :], lap_in.at[:, own_rows], ends_in.at[:, own_rows], nodes_in,
            w_ident_in, types_in, gain_in, shift_in, bias_q_in, bias_v_in, wq_in, wk_in, wv_in,
            edges_in,
        ),
        (
            feats, lap, ends, nodes, w_ident, types, gain_rows, shift_rows, bias_q, bias_v,
            w_q, w_k, w_v, edges,
        ),
        sems,
    )
    for copy in copies[:10]:
        copy.wait()
    gain, shift = row_of(gain_rows), row_of(shift_rows)

    def molecule(m):
        at = slice(m * SEQ, (m + 1) * SEQ)
        count = nodes[core * mols + m]
        hidden, ident, normed = embed_rows(
            feats, lap, ends, w_ident, types, gain, shift, at, count
        )
        ident_out[:, at] = ident
        hidden_out[at, :] = hidden
        normed_out[at, :] = normed
        normed_t_out[:, at] = normed.T

    for m in range(mols):
        molecule(m)
    normed = normed_out[...]
    copies[10].wait()
    q_out[...] = (dot(normed, w_q[...]) + row_of(bias_q)).astype(BF16)
    copies[11].wait()
    k_out[...] = dot(normed, w_k[...]).astype(BF16)
    copies[12].wait()
    v_out[...] = (dot(normed, w_v[...]) + row_of(bias_v)).astype(BF16)
    copies[13].wait()
    for m in range(2 * mols):
        inside = lax.broadcasted_iota(jnp.int32, (SEQ, LANES), 0) < nodes[m] + edges[m]
        keep_out[m * SEQ : (m + 1) * SEQ, :] = jnp.where(inside, 1.0, 0.0)


def forward_kernel(
    hidden, normed, q_own, k_own, v_own, w_q, w_k, w_v, wo_own, wo, wu_own, wu,
    bias_q, bias_v, bias_u,
    nodes_in, edges_in, bias_u_own_in, bias_o_in, gain_in, shift_in,
    q_out, k_out, v_out, probs_out, keep_out, send_out, middle, active, slope,
    nodes, edges, bias_u_own, bias_o, gain_rows, shift_rows, sems,
    mixed, attended, normed_two,
):
    rows, dim = hidden.shape
    width = q_own.shape[1]
    mols = rows // SEQ
    pairs = width // (2 * HDIM)
    windows = head_windows(width)
    core = places()[0]
    copies = copy_in(
        (nodes_in, edges_in, bias_u_own_in, bias_o_in, gain_in, shift_in),
        (nodes, edges, bias_u_own, bias_o, gain_rows, shift_rows),
        sems,
    )

    for copy in copies:
        copy.wait()
    gain, shift, bias_out = row_of(gain_rows), row_of(shift_rows), row_of(bias_o)

    sides = ((q_own, k_own, v_own, keep_out), (q_out, k_out, v_out, send_out))
    units = [(m, side) for side in (0, 1) for m in range(mols)]

    def weigh(unit, pair):
        m, side = unit
        at = slice(m * SEQ, (m + 1) * SEQ)
        place = core * mols + m
        key_keep = positions(SEQ) < nodes[place] + edges[place]
        low, high = windows[pair]
        both = split_heads(sides[side][0][at, :], pair, windows[pair])
        scores = dot_nt(sides[side][1][at, low:high], both)
        scores = jnp.where(key_keep, scores, -1e30)
        top = jnp.max(scores, axis=0, keepdims=True)
        raised = jnp.exp2((scores - top) * LOG2_SCALE)
        probs_out[m, side * pairs + pair] = (raised * (1.0 / row_sum(raised))).astype(BF16)

    def mix(step, pair, values_t):
        m, side = units[step]
        first = pair * 2 * HDIM
        out = dot(values_t[first : first + 2 * HDIM], probs_out[m, side * pairs + pair])
        mixed[step % 2, first : first + HDIM, :] = out[:HDIM, :SEQ]
        mixed[step % 2, first + HDIM : first + 2 * HDIM, :] = out[HDIM:, SEQ:]

    def keep_mixed(step):
        m, side = units[step]
        at = slice(m * SEQ, (m + 1) * SEQ)
        place = core * mols + m
        query_keep = lax.broadcasted_iota(jnp.int32, (1, SEQ), 1) < nodes[place] + edges[place]
        kept = jnp.where(query_keep, mixed[step % 2], 0.0).astype(BF16)
        sides[side][3][dim : dim + width, at] = kept
        attended[at, side * width : (side + 1) * width] = kept.T

    partner = ((q_out, w_q, bias_q), (k_out, w_k, None), (v_out, w_v, bias_v))
    for pair in range(pairs):
        weigh(units[0], pair)
        if pair % 2 == 0 and pair // 2 < len(partner):
            out, weight, bias = partner[pair // 2]
            rows_of = dot(normed[...], weight[...])
            out[...] = (rows_of if bias is None else rows_of + row_of(bias)).astype(BF16)
    for step, task in enumerate(units):
        values_t = sides[task[1]][2][task[0] * SEQ : (task[0] + 1) * SEQ, :].T
        for pair in range(pairs):
            mix(step, pair, values_t)
            if step + 1 < len(units):
                weigh(units[step + 1], pair)
        keep_mixed(step)
    middle[...] = (
        hidden[...] + dot(attended[:, :width], wo_own[...]) + dot(attended[:, width:], wo[...])
    )

    for m in range(mols):
        at = slice(m * SEQ, (m + 1) * SEQ)
        total = middle[at, :] + bias_out
        middle[at, :] = total
        unit_rows, _ = norm_parts(total)
        rows_two = (unit_rows * gain + shift).astype(BF16)
        normed_two[at, :] = rows_two
        turned = rows_two.T
        keep_out[:dim, at] = turned
        send_out[:dim, at] = turned

    for side, (w_ref, b_ref, part_out) in enumerate(
        ((wu_own, bias_u_own, keep_out), (wu, bias_u, send_out))
    ):
        columns = slice(side * width, (side + 1) * width)
        slope[:, columns] = dot(normed_two[...], w_ref[...]) + row_of(b_ref)

        for m in range(mols):
            at = slice(m * SEQ, (m + 1) * SEQ)
            before = slope[at, columns]
            phi = 0.5 * (1.0 + lax.erf(before * math.sqrt(0.5)))
            out = (before * phi).astype(BF16)
            slope[at, columns] = phi + before * jnp.exp(before * before * -0.5) * (
                1.0 / math.sqrt(2.0 * math.pi)
            )
            active[at, columns] = out
            part_out[dim + width : dim + 2 * width, at] = out.T


def ffn_back_kernel(
    middle, slope, wu_own, wu, wd_own, wd, keep_rows, cots, gain_in,
    keep_out, send_out, gm_out, grad_branch,
    gain_rows, sems, grad_ffn,
):
    rows, dim = middle.shape
    width = wd.shape[0]
    mols = rows // SEQ
    core = places()[0]
    copies = copy_in((gain_in,), (gain_rows,), sems)

    def own_cots(m):
        at = pl.ds(pl.multiple_of(core * rows + m * SEQ, SEQ), SEQ)
        return jnp.where(keep_rows[at, 0:1] > 0.5, cots[at, :].astype(F32), 0.0)

    for m in range(mols):
        at = slice(m * SEQ, (m + 1) * SEQ)
        grad_ffn[at, :] = own_cots(m).astype(BF16)
    place_b = 0
    for side, (w_ref, part_out) in enumerate(((wd_own, keep_out), (wd, send_out))):
        columns = slice(side * width, (side + 1) * width)
        grad_before = slope[:, columns] * dot_nt(grad_ffn[...], w_ref[...])
        part_out[place_b : place_b + rows, :] = grad_before.astype(BF16)

    back = pl.ds(place_b, rows)
    gm_out[...] = dot_nt(keep_out[back, :], wu_own[...]) + dot_nt(send_out[back, :], wu[...])

    copies[0].wait()
    gain = row_of(gain_rows)
    nothing = jnp.zeros((1, dim), F32)
    sums = (nothing,) * 4
    for m in range(mols):
        at = slice(m * SEQ, (m + 1) * SEQ)
        grad_normed = gm_out[at, :]
        unit_rows, inverse = norm_parts(middle[at, :])
        grad_result = own_cots(m)
        grad = grad_result + norm_back(unit_rows, inverse, grad_normed * gain)
        gm_out[at, :] = grad
        grad_branch[at, :] = grad.astype(BF16)
        sums = (
            sums[0] + row_sum(grad),
            sums[1] + row_sum(grad_normed * unit_rows),
            sums[2] + row_sum(grad_normed),
            sums[3] + row_sum(grad_result),
        )

    place_m = place_b + rows
    for part_out in (keep_out, send_out):
        part_out[place_m : place_m + rows, :] = grad_branch[:, :width]
        part_out[place_m + rows : place_m + 2 * rows, :] = grad_branch[:, width:]
    small = jnp.concatenate(list(sums) + [nothing] * 12, axis=0)
    left, right = small[:, :width], small[:, width:]
    place_s = place_m + 2 * rows
    keep_out[place_s:, :] = jnp.where(core == 0, left, right).astype(BF16)
    send_out[place_s:, :] = jnp.where(core == 0, right, left).astype(BF16)


def result_kernel(middle, active, wd_own, wd, bias, result_out):
    width = wd.shape[0]
    result_out[...] = (
        middle[...]
        + dot(active[:, :width], wd_own[...])
        + dot(active[:, width:], wd[...])
        + row_of(bias)
    ).astype(BF16)


def branch_kernel(grad_branch, wo_own, wo, keep_rows, ga_own_out, ga_out):
    rows = grad_branch.shape[0]
    own_rows = pl.ds(pl.multiple_of(places()[0] * rows, SEQ), rows)
    keep = keep_rows[own_rows, 0:1] > 0.5
    for ref, weight in ((ga_own_out, wo_own), (ga_out, wo)):
        ref[...] = jnp.where(keep, dot_nt(grad_branch[...], weight[...]), 0.0).astype(BF16)


def attend_back_kernel(
    q_own, k_own, v_own, ga_own, q_got, k_got, v_got, ga_got, probs_all,
    keep_out, send_out, dq_t, dk, dv, slopes,
):
    rows, width = q_own.shape
    pairs = width // (2 * HDIM)
    windows = head_windows(width)
    sides = (
        (q_own, k_own, v_own, ga_own, keep_out),
        (q_got, k_got, v_got, ga_got, send_out),
    )
    units = [(m, side) for m in range(rows // SEQ) for side in (0, 1)]

    def score_back(unit, pair):
        m, side = unit
        at = slice(m * SEQ, (m + 1) * SEQ)
        low, high = windows[pair]
        both_g = split_heads(sides[side][3][at, :], pair, windows[pair])
        probs_low = probs_all[m, side * pairs + pair]
        probs = probs_low.astype(F32)
        grad_probs = dot_nt(sides[side][2][at, low:high], both_g)
        inner = row_sum(probs * grad_probs)
        slopes[side, pair] = (probs * (grad_probs - inner)).astype(BF16)
        dv[side, :, low:high] += dot(probs_low, both_g)

    def rows_back(unit, pair, keys_t):
        m, side = unit
        low, high = windows[pair]
        grad_scores = slopes[side, pair]
        both_q = split_heads(sides[side][0][m * SEQ : (m + 1) * SEQ, :], pair, windows[pair])
        dk[side, :, low:high] += dot(grad_scores, both_q)
        first = pair * 2 * HDIM
        out = dot(keys_t[first : first + 2 * HDIM], grad_scores)
        dq_t[side, first : first + HDIM, :] = out[:HDIM, :SEQ]
        dq_t[side, first + HDIM : first + 2 * HDIM, :] = out[HDIM:, SEQ:]

    def begin(unit):
        dk[unit[1]] = jnp.zeros_like(dk[unit[1]])
        dv[unit[1]] = jnp.zeros_like(dv[unit[1]])

    def finish(unit):
        m, side = unit
        part_out = sides[side][4]
        base = m * SEQ
        part_out[base : base + SEQ, :] = (dq_t[side] * SCALE).astype(BF16).T
        part_out[rows + base : rows + base + SEQ, :] = (dk[side] * SCALE).astype(BF16)
        part_out[2 * rows + base : 2 * rows + base + SEQ, :] = dv[side].astype(BF16)

    begin(units[0])
    for pair in range(pairs):
        score_back(units[0], pair)
    for step, unit in enumerate(units):
        keys_t = sides[unit[1]][1][unit[0] * SEQ : (unit[0] + 1) * SEQ, :].T
        if step + 1 < len(units):
            begin(units[step + 1])
        for pair in range(pairs):
            rows_back(unit, pair, keys_t)
            if step + 1 < len(units):
                score_back(units[step + 1], pair)
        finish(unit)


def embed_back_kernel(*refs):
    (
        grads_own, grads,
        wq_own, wk_own, wv_own, w_q, w_k, w_v, ident, grad_middle,
        feats_in, nodes_in, w_ident_in, types_in, gain_in,
        features_out, keep_out, send_out,
        feats, nodes, w_ident, types, gain_rows, sems, grad_normed, small,
    ) = refs
    core = places()[0]
    rows = feats.shape[0]
    copies = copy_in(
        (
            feats_in.at[pl.ds(pl.multiple_of(core * rows, SEQ), rows), :], nodes_in,
            w_ident_in, types_in, gain_in,
        ),
        (feats, nodes, w_ident, types, gain_rows),
        sems,
    )
    rows, dim = feats.shape
    width = wq_own.shape[1]
    idw = ident.shape[0]
    total = None
    for part, weights in ((grads_own, (wq_own, wk_own, wv_own)), (grads, (w_q, w_k, w_v))):
        for place, weight in enumerate(weights):
            term = dot_nt(part[place * rows : (place + 1) * rows, :], weight[...])
            total = term if total is None else total + term
    grad_normed[...] = total
    mols = rows // SEQ
    small[...] = jnp.zeros_like(small)
    for copy in copies:
        copy.wait()
    gain = row_of(gain_rows)
    kinds = types[...].astype(F32)

    def molecule(m, carry):
        at = pl.ds(pl.multiple_of(m * SEQ, SEQ), SEQ)
        is_edge = positions(SEQ) >= nodes[core * mols + m]
        hidden = feats[at, :].astype(F32) + dot_tn(ident[:, at], w_ident[...])
        hidden = hidden + jnp.where(is_edge, kinds[1:2, :], kinds[0:1, :])
        unit, inverse = norm_parts(hidden)
        grad_rows = grad_normed[at, :]
        grad = grad_middle[at, :] + norm_back(unit, inverse, grad_rows * gain)
        features_out[at, :] = grad
        high = grad.astype(BF16)
        rest = (grad - high.astype(F32)).astype(BF16)
        picked = ident[:, at]
        small[:idw, :] += dot(picked, high) + dot(picked, rest)
        edge_rows = jnp.where(is_edge, grad, 0.0)
        small[idw : idw + 1, :] += row_sum(grad - edge_rows)
        small[idw + 1 : idw + 2, :] += row_sum(edge_rows)
        small[idw + 2 : idw + 3, :] += row_sum(grad_rows * unit)
        small[idw + 3 : idw + 4, :] += row_sum(grad_rows)
        return carry

    lax.fori_loop(0, mols, molecule, 0)
    left, right = small[:, :width], small[:, width:]
    keep_out[...] = jnp.where(core == 0, left, right)
    send_out[...] = jnp.where(core == 0, right, left).astype(BF16)


def deal(unit, places_in, outs, block_at, small=None):
    _, inner, outer = places()
    first_kept, first_sent, second_kept, second_sent = outs
    for step in range(INNER):
        for turn in range(OUTER):
            if turn < 2:
                out, slot = (first_sent if step % 2 else first_kept), step // 2
            else:
                out, slot = (second_sent if step // 2 else second_kept), step % 2
            start = (slot * 2 + turn % 2) * places_in * unit
            for place in range(places_in):
                out[start + place * unit : start + (place + 1) * unit, :] = block_at(
                    inner ^ step, outer ^ turn, place
                )
    if small is not None:
        for out in (first_kept, first_sent):
            out[INNER * places_in * unit :, :] = small


def flat_block(flat, unit, dest, z):
    row = pl.multiple_of((dest * (OUTER // 2) + z // 2) * unit, 16)
    return flat[z % 2, pl.ds(row, unit), :]


def down_grads_kernel(kept, got, cots, keep_rows, *rest):
    outs, (flat, grad_ffn) = rest[:4], rest[4:]
    rows_all, dim = cots.shape
    rows, width = rows_all // 2, kept.shape[1]
    core = places()[0]
    for m in range(rows_all // SEQ):
        at = slice(m * SEQ, (m + 1) * SEQ)
        grad_ffn[at, :] = jnp.where(keep_rows[at, 0:1] > 0.5, cots[at, :].astype(F32), 0.0).astype(BF16)
    own_rows = pl.ds(pl.multiple_of(core * rows, SEQ), rows)
    other_rows = pl.ds(pl.multiple_of((1 - core) * rows, SEQ), rows)
    turned = slice(dim + width, dim + 2 * width)
    for half in (0, 1):
        columns = slice(half * width, (half + 1) * width)
        product = dot(kept[turned, :], grad_ffn[own_rows, columns])
        product = product + dot(got[turned, :], grad_ffn[other_rows, columns])
        flat[half] = product.astype(BF16)
    unit = dim // (INNER * OUTER)
    deal(unit, 1, outs, lambda dest, z, place: flat_block(flat, unit, dest, z))


def ffn_grads_kernel(kept, got, kept_back, got_back, *rest):
    outs, (tall, flat) = rest[:4], rest[4:]
    rows, width = kept.shape[1], kept.shape[1]
    dim = kept.shape[0] - 2 * width
    back, place_s = slice(0, rows), 3 * rows
    tall[...] = (
        dot(kept[:dim, :], kept_back[back, :]) + dot(got[:dim, :], got_back[back, :])
    ).astype(BF16)
    turned = slice(dim, dim + width)
    for half in (0, 1):
        mid = slice((1 + half) * rows, (2 + half) * rows)
        flat[half] = (
            dot(kept[turned, :], kept_back[mid, :]) + dot(got[turned, :], got_back[mid, :])
        ).astype(BF16)
    bias = row_sum(kept_back[back, :].astype(F32)) + row_sum(got_back[back, :].astype(F32))
    small = kept_back[place_s:, :].astype(F32) + got_back[place_s:, :].astype(F32)
    spot = lax.broadcasted_iota(jnp.int32, small.shape, 0)
    small = jnp.where(spot == 4, bias, small).astype(BF16)
    unit = dim // (INNER * OUTER)

    def block_at(dest, z, place):
        if place == 0:
            return tall[pl.ds(pl.multiple_of((dest * OUTER + z) * unit, 16), unit), :]
        return flat_block(flat, unit, dest, z)

    deal(unit, 2, outs, block_at, small)


def qkv_grads_kernel(normed_t, normed_t_got, kept, got, *refs):
    outs, small_out, (tall, normed, stacked) = refs[:4], refs[4], refs[5:]
    dim, rows = normed_t.shape
    unit = dim // (INNER * OUTER)
    normed[:, :rows] = normed_t[...]
    normed[:, rows:] = normed_t_got[...]
    spot = lax.broadcasted_iota(jnp.int32, small_out.shape, 0)
    small = jnp.zeros(small_out.shape, F32)
    for place in range(3):
        part = slice(place * rows, (place + 1) * rows)
        stacked[:rows, :] = kept[part, :]
        stacked[rows:, :] = got[part, :]
        tall[place] = dot(normed[...], stacked[...]).astype(BF16)
        if place != 1:
            small = jnp.where(spot == 36 + place // 2, row_sum(stacked[...].astype(F32)), small)
    small_out[...] = small

    def block_at(dest, z, place):
        return tall[place, pl.ds(pl.multiple_of((dest * OUTER + z) * unit, 16), unit), :]

    deal(unit, 3, outs, block_at)


def add(first, second):
    return (first.astype(F32) + second.astype(F32)).astype(BF16)


def plane_sum_kernel(first, first_got, second, second_got, *refs):
    late, (first_kept, first_sent, second_kept, second_sent) = refs[:-4], refs[-4:]
    pair = second_kept.shape[0]
    total = add(first[...], first_got[...])
    first_kept[:pair, :] = total[:pair]
    first_sent[:pair, :] = total[pair : 2 * pair]
    if late:
        small = (late[0][...] + late[1][...].astype(F32) + late[2][...]).astype(BF16)
    else:
        small = total[2 * pair :]
    first_kept[pair:, :] = small
    first_sent[pair:, :] = small
    total = add(second[...], second_got[...])
    second_kept[...] = total[:pair]
    second_sent[...] = total[pair:]


def plane_join_kernel(first, first_got, second, second_got, *refs):
    ahead, outs = refs[:4], refs[4:]
    unit = ahead[0].shape[0] // 4
    small = add(first[8 * unit :, :], first_got[8 * unit :, :])
    for place, (left, right, more, more_got) in enumerate(
        ((first, first_got, *ahead[:2]), (second, second_got, *ahead[2:]))
    ):
        total = add(left[: 8 * unit, :], right[: 8 * unit, :])
        late = add(more[...], more_got[...])
        for block in range(4):
            out = outs[2 * place + block // 2]
            start = block % 2 * 3 * unit
            out[start : start + 2 * unit, :] = total[2 * block * unit : 2 * (block + 1) * unit]
            out[start + 2 * unit : start + 3 * unit, :] = late[block * unit : (block + 1) * unit]
    for out in outs[:2]:
        out[6 * unit :, :] = small


def line_cut_kernel(first, first_got, second, second_got, own, near, middle, far):
    chunk = own.shape[0]
    total = add(first[...], first_got[...])
    own[...] = total[:chunk]
    near[...] = total[chunk:]
    total = add(second[...], second_got[...])
    middle[...] = total[:chunk]
    far[...] = total[chunk:]


def line_sum_kernel(own, near, near_got, middle_got, far_got, out, out_small):
    chunk = own.shape[0]
    total = own[...].astype(F32) + near_got[:chunk, :].astype(F32)
    total = total + middle_got[...].astype(F32) + far_got[...].astype(F32)
    out[...] = total.astype(BF16)
    out_small[:chunk, :] = total.astype(BF16)
    out_small[chunk:, :] = add(near[chunk:, :], near_got[chunk:, :])


def line_join_kernel(own, near, middle, far, line_x, line_y, small_out):
    chunk = near.shape[0]
    small = own[chunk:, :].astype(F32) + middle[chunk:, :].astype(F32)
    small_out[...] = small
    for out in (line_x, line_y):
        for turn, part in enumerate((own, near, middle, far)):
            out[turn * chunk : (turn + 1) * chunk, :] = part[:chunk, :]
    line_x[OUTER * chunk :, :] = small.astype(BF16)


def place_kernel(split_second, *refs):
    outs, parts = refs[-3:], refs[:-3]
    own = parts[0]
    steps = min(len(parts), INNER)
    _, inner, outer = places()
    unit = own.shape[0] // (3 * OUTER)
    width = own.shape[1]
    for step in range(steps):
        for turn in range(OUTER):
            ref, start = parts[step], turn * 3 * unit
            if step == 3 and turn >= 2:
                ref, start = parts[4], (turn - 2) * 3 * unit
            dest, z = inner ^ step, outer ^ turn
            tall = pl.ds(pl.multiple_of((dest * OUTER + z) * unit, 16), unit)
            flat = pl.ds(pl.multiple_of((dest * (OUTER // 2) + z // 2) * unit, 16), unit)
            columns = pl.ds(pl.multiple_of(z % 2 * width, LANES), width)
            for place in range(3):
                part = ref[start + place * unit : start + (place + 1) * unit, :].astype(F32)
                if split_second and place > 0:
                    outs[place][flat, columns] = part
                else:
                    outs[place][tall, :] = part


def corner_kernel(first, second, *refs):
    outs, blocks, sems = refs[3:6], refs[6], refs[7]
    _, inner, outer = places()
    unit = first.shape[0] // 6
    size = OUTER * unit
    for turn in range(OUTER):
        ref, start = (first, turn * 3 * unit) if turn < 2 else (second, (turn - 2) * 3 * unit)
        at = pl.ds(pl.multiple_of((outer ^ turn) * unit, 16), unit)
        for place in range(3):
            rows = slice(start + place * unit, start + (place + 1) * unit)
            blocks[place, at, :] = ref[rows, :].astype(F32)
    at = pl.ds(pl.multiple_of((inner ^ 3) * size, 64), size)
    copies = copy_in(
        [blocks.at[place] for place in range(3)], [out.at[at, :] for out in outs], sems
    )
    for copy in copies:
        copy.wait()


def finish_first_kernel(small, got, bias_out, gain, shift, bias_down, bias_up):
    core = places()[0]
    for place, ref in enumerate((bias_out, gain, shift, bias_down)):
        mine, other = small[place : place + 1, :], got[place : place + 1, :]
        left = jnp.where(core == 0, mine, other)
        put_row(ref, jnp.concatenate([left, jnp.where(core == 0, other, mine)], axis=1))
    put_row(bias_up, small[4:5, :])


def finish_second_kernel(small, extra, got, w_ident, types, gain, shift, bias_q, bias_v):
    idw = w_ident.shape[0]
    core = places()[0]
    mine, other = small[...] + extra[...].astype(F32), got[...]
    left = jnp.where(core == 0, mine, other)
    total = jnp.concatenate([left, jnp.where(core == 0, other, mine)], axis=1)
    w_ident[...] = total[:idw]
    types[...] = total[idw : idw + 2]
    put_row(gain, total[idw + 2 : idw + 3])
    put_row(shift, total[idw + 3 : idw + 4])
    put_row(bias_q, mine[idw + 4 : idw + 5])
    put_row(bias_v, mine[idw + 5 : idw + 6])


def per_device(
    features, lap_vectors, node_counts, edge_counts, endpoints, w_ident, type_table,
    gain_one, shift_one, w_query, w_key, w_value, bias_query, bias_value, w_out, bias_out,
    gain_two, shift_two, w_up, bias_up, w_down, bias_down, cotangent,
):
    dp_count = lax.axis_size("dp")
    dp_index = lax.axis_index("dp")
    mp_index = lax.axis_index("mp")
    block = INNER * OUTER
    rest_count = dp_count // block
    def swap(part):
        return lax.ppermute(part, "mp", [(0, 1), (1, 0)])

    def inner_move(part, step):
        return lax.ppermute(part, "dp", [(s, s ^ step) for s in range(dp_count)])

    def outer_move(part, step):
        return lax.ppermute(part, "dp", [(s, s ^ (step * INNER)) for s in range(dp_count)])

    rows_all, dim = features.shape
    rows = rows_all // 2
    mols = rows // SEQ
    width = w_query.shape[1]
    heads = width // HDIM
    lapk = lap_vectors.shape[1]
    idw = w_ident.shape[0]

    def pinned(part):
        return pltpu.with_memory_space_constraint(part, pltpu.HBM)

    def lanes(part):
        return pinned(part.reshape(-1, LANES))

    nodes, edges = pinned(node_counts), pinned(edge_counts)
    count_scratch = pltpu.SMEM(node_counts.shape, jnp.int32)
    wide_scratch = pltpu.VMEM((dim // LANES, LANES), BF16)
    half_scratch = pltpu.VMEM((width // LANES, LANES), BF16)
    def after(part, *others):
        return lax.optimization_barrier((part, *others))[0]

    embed_args = (
        pinned(features), pinned(lap_vectors.T), pinned(endpoints.T), nodes,
        pinned(w_ident), pinned(type_table), lanes(gain_one), lanes(shift_one),
    )
    embed_scratch = [
        pltpu.VMEM((rows, dim), BF16),
        pltpu.VMEM((lapk, rows), BF16),
        pltpu.VMEM((2, rows), jnp.int32),
        count_scratch,
        pltpu.VMEM((idw, dim), BF16),
        pltpu.VMEM((2, dim), BF16),
        wide_scratch,
        wide_scratch,
    ]

    wq_got, wk_got, wv_got = swap(w_query), swap(w_key), swap(w_value)
    bq_got, bv_got, bu_got = swap(bias_query), swap(bias_value), swap(bias_up)
    wo_got, wu_got = swap(w_out), swap(w_up)

    hidden, ident, normed, normed_t, q_own, k_own, v_own, keep_rows = call(
        embed_kernel,
        (
            *embed_args, lanes(bias_query), lanes(bias_value),
            pinned(w_query), pinned(w_key), pinned(w_value), edges,
        ),
        [outside()] * 14,
        [
            ((rows, dim), F32),
            ((idw, rows), BF16),
            ((rows, dim), BF16),
            ((dim, rows), BF16),
            ((rows, width), BF16),
            ((rows, width), BF16),
            ((rows, width), BF16),
            ((rows_all, LANES), F32),
        ],
        scratch=embed_scratch
        + [half_scratch] * 2
        + [pltpu.VMEM((dim, width), BF16)] * 3
        + [count_scratch, pltpu.SemaphoreType.DMA((14,))],
    )
    wd_got = swap(after(w_down, normed))
    ahead_rows, back_rows = dim + 2 * width, 3 * rows + 16
    q_got, k_got, v_got, probs, kept_a, sent_a, middle, active, slope = call(
        forward_kernel,
        (
            hidden, normed, q_own, k_own, v_own, wq_got, wk_got, wv_got,
            w_out, wo_got, w_up, wu_got,
            *(part.reshape(-1, LANES) for part in (bq_got, bv_got, bu_got)),
            nodes, edges,
            lanes(bias_up), lanes(bias_out), lanes(gain_two), lanes(shift_two),
        ),
        [whole()] * 15 + [outside()] * 6,
        [
            ((rows, width), BF16),
            ((rows, width), BF16),
            ((rows, width), BF16),
            ((mols, heads, SEQ, 2 * SEQ), BF16),
            ((ahead_rows, width), BF16),
            ((ahead_rows, width), BF16),
            ((rows, dim), F32),
            ((rows, dim), BF16),
            ((rows, dim), F32),
        ],
        scratch=[
            count_scratch,
            count_scratch,
            half_scratch,
            wide_scratch,
            wide_scratch,
            wide_scratch,
            pltpu.SemaphoreType.DMA((6,)),
            pltpu.VMEM((2, width, SEQ), F32),
            pltpu.VMEM((rows, dim), BF16),
            pltpu.VMEM((rows, dim), BF16),
        ],
        limit=30,
    )
    got_a = swap(sent_a)
    kept_back, sent_back, grad_middle, grad_branch = call(
        ffn_back_kernel,
        (
            middle, slope, w_up, wu_got, w_down, wd_got, keep_rows, cotangent,
            lanes(gain_two),
        ),
        [whole()] * 8 + [outside()],
        [
            ((back_rows, width), BF16),
            ((back_rows, width), BF16),
            ((rows, dim), F32),
            ((rows, dim), BF16),
        ],
        scratch=[wide_scratch, pltpu.SemaphoreType.DMA((1,)), pltpu.VMEM((rows, dim), BF16)],
    )
    got_back = swap(sent_back)

    unit = dim // block
    chunk = 3 * unit
    small_a, small_b = 16, 48

    def rest_sum(part):
        if rest_count == 1:
            return part
        groups = [[r * block + s for r in range(rest_count)] for s in range(block)]
        return lax.psum(part.astype(F32), "dp", axis_index_groups=groups).astype(part.dtype)

    pair = 2 * chunk

    def plane_step(parts, small_rows, late=(), others=(), micros=0):
        first, first_sent, second, second_sent = parts
        first_got = after(inner_move(first_sent, 1), *others)
        second_got = after(inner_move(second_sent, 2), *others)
        return call(
            plane_sum_kernel,
            (first, first_got, second, second_got, *late),
            [whole()] * (4 + len(late)),
            [((pair + small_rows, width), BF16)] * 2 + [((pair, width), BF16)] * 2,
            micros=micros,
        )

    def plane_turn(parts, others=(), micros=0):
        first, first_sent, second, second_sent = parts
        first_got = after(inner_move(first_sent, 2), *others)
        second_got = after(inner_move(second_sent, 1), *others)
        return call(
            line_cut_kernel,
            (first, first_got, second, second_got),
            [whole()] * 4,
            [
                ((chunk, width), BF16),
                ((first.shape[0] - chunk, width), BF16),
                ((chunk, width), BF16),
                ((chunk, width), BF16),
            ],
            micros=micros,
        )

    def line_step(parts, others=(), micros=0):
        got = [after(outer_move(parts[turn], turn), *others) for turn in range(1, OUTER)]
        mine, both = call(
            line_sum_kernel,
            (parts[0], parts[1], *got),
            [whole()] * 5,
            [((chunk, width), BF16), (parts[1].shape, BF16)],
            micros=micros,
        )
        if rest_count > 1:
            both = rest_sum(both)
            mine = both[:chunk]
        return mine, both

    def line_back(mine, both, others=(), micros=0):
        sent = (mine, both, mine)
        got = [after(outer_move(sent[turn - 1], turn), *others) for turn in range(1, OUTER)]
        small_rows = both.shape[0] - chunk
        return call(
            line_join_kernel,
            (both, *got),
            [whole()] * OUTER,
            [
                ((OUTER * chunk + small_rows, width), BF16),
                ((OUTER * chunk, width), BF16),
                ((small_rows, width), F32),
            ],
            micros=micros,
        )

    def plane_back(lines):
        return inner_move(lines[0], 1), inner_move(lines[1], 2)

    def plane_back_turn(side_x, side_y):
        return inner_move(side_y[:pair], 1), inner_move(side_x[pair : 2 * pair], 2)

    def placed(planes, split_second, micros=0):
        tall, flat = ((dim, width), F32), ((width, dim), F32)
        return call(
            lambda *refs: place_kernel(split_second, *refs),
            planes,
            [whole()] * len(planes),
            [tall, flat, flat] if split_second else [tall] * 3,
            micros=micros,
        )

    parts_down = call(
        down_grads_kernel,
        (after(kept_a, grad_branch), got_a, cotangent, keep_rows),
        [whole()] * 4,
        [((INNER * unit, width), BF16)] * 4,
        scratch=[pltpu.VMEM((2, width, width), BF16), pltpu.VMEM((rows_all, dim), BF16)],
    )
    parts_a = call(
        ffn_grads_kernel,
        (after(kept_a, parts_down[0]), got_a, kept_back, got_back),
        [whole()] * 4,
        [((2 * INNER * unit + small_a, width), BF16)] * 2 + [((2 * INNER * unit, width), BF16)] * 2,
        scratch=[pltpu.VMEM((dim, width), BF16), pltpu.VMEM((2, width, width), BF16)],
    )
    ahead = [
        after(inner_move(parts_down[1], 1), parts_a[0]),
        after(inner_move(parts_down[3], 2), parts_a[0]),
    ]
    ga_own, ga_got = call(
        branch_kernel,
        (after(grad_branch, parts_a[0], *ahead), w_out, wo_got, keep_rows),
        [whole()] * 4,
        [((rows, width), BF16), ((rows, width), BF16)],
    )

    kept_b, sent_b = call(
        attend_back_kernel,
        (q_own, k_own, v_own, ga_own, q_got, k_got, v_got, ga_got, probs),
        [whole()] * 9,
        [((3 * rows, width), BF16)] * 2,
        scratch=[
            pltpu.VMEM((2, width, SEQ), F32),
            pltpu.VMEM((2, SEQ, width), F32),
            pltpu.VMEM((2, SEQ, width), F32),
            pltpu.VMEM((2, heads // 2, SEQ, 2 * SEQ), BF16),
        ],
    )
    normed_t_got = swap(after(normed_t, parts_a[0]))
    got_b = swap(sent_b)
    moved = [after(inner_move(parts_a[1], 1), kept_b), after(inner_move(parts_a[3], 2), kept_b)]
    moved = moved + ahead
    steps_a = call(
        plane_join_kernel,
        (
            parts_a[0], moved[0], parts_a[2], moved[1],
            parts_down[0], moved[2], parts_down[2], moved[3],
        ),
        [whole()] * 8,
        [((pair + small_a, width), BF16)] * 2 + [((pair, width), BF16)] * 2,
        micros=6,
    )
    normed_t = after(normed_t, *steps_a)
    parts_b = call(
        qkv_grads_kernel,
        (normed_t, normed_t_got, kept_b, got_b),
        [whole()] * 4,
        [((INNER * chunk, width), BF16)] * 4 + [((small_b, width), F32)],
        scratch=[
            pltpu.VMEM((3, dim, width), BF16),
            pltpu.VMEM((dim, 2 * rows), BF16),
            pltpu.VMEM((2 * rows, width), BF16),
        ],
    )
    turned_a = plane_turn(steps_a, others=(parts_b[0],), micros=3)
    grad_middle = after(grad_middle, parts_b[0], *turned_a)
    grad_features, small_kept, small_sent = call(
        embed_back_kernel,
        (
            kept_b, sent_b, w_query, w_key, w_value, wq_got, wk_got, wv_got, ident,
            grad_middle, embed_args[0], nodes, *embed_args[4:7],
        ),
        [whole()] * 10 + [outside()] * 5,
        [((rows, dim), F32), ((small_b, width), F32), ((small_b, width), BF16)],
        scratch=[
            pltpu.VMEM((rows, dim), BF16),
            count_scratch,
            pltpu.VMEM((idw, dim), BF16),
            pltpu.VMEM((2, dim), BF16),
            wide_scratch,
            pltpu.SemaphoreType.DMA((5,)),
            pltpu.VMEM((rows, dim), F32),
            pltpu.VMEM((small_b, dim), F32),
        ],
        micros=0,
    )
    small_got = swap(small_sent)
    steps_b = plane_step(parts_b[:4], small_b, late=(small_kept, small_got, parts_b[4]))
    line_a = line_step(turned_a, others=steps_b, micros=3)
    turned_b = plane_turn(steps_b, others=line_a[:1])
    lines_a = line_back(*line_a, others=turned_b, micros=1)
    line_b = line_step(turned_b, micros=12)
    sides_a = plane_back((lines_a[1], lines_a[1]))
    far_a = plane_back_turn(*sides_a)
    planes_a = (lines_a[1], *sides_a, *far_a)
    lines_b = line_back(*line_b, micros=2)
    result = call(
        result_kernel,
        (middle, active, w_down, wd_got, lanes(after(bias_down, lines_b[1]))),
        [whole()] * 5,
        [((rows, dim), BF16)],
    )[0]
    wide, half = ((dim // LANES, LANES), F32), ((width // LANES, LANES), F32)
    sums_a = call(
        finish_first_kernel,
        (lines_a[2], swap(after(lines_a[2], lines_b[1]))),
        [whole()] * 2,
        [wide] * 4 + [half],
    )
    grad_w_up, grad_w_out, grad_w_down = placed(planes_a, True, micros=10)
    sides_b = plane_back(lines_b)
    sides_b, _ = lax.optimization_barrier((sides_b, (result, sums_a, grad_w_up)))
    near_b = placed((lines_b[1], sides_b[0], sides_b[1]), False)
    far_b = plane_back_turn(*sides_b)
    far_b, near_b = lax.optimization_barrier((far_b, near_b))
    extra = sides_b[0][OUTER * chunk :]
    own_b = lines_b[2] + extra.astype(F32)
    sums_b = call(
        finish_second_kernel,
        (lines_b[2], extra, swap(own_b)),
        [whole()] * 3,
        [((idw, dim), F32), ((2, dim), F32), wide, wide, half, half],
    )
    grad_w_query, grad_w_key, grad_w_value = call(
        corner_kernel,
        (*far_b, *near_b),
        [whole()] * 2 + [outside()] * 3,
        [((dim, width), F32)] * 3,
        scratch=[
            pltpu.VMEM((3, dim // INNER, width), F32),
            pltpu.SemaphoreType.DMA((3,)),
        ],
        in_place={2: 0, 3: 1, 4: 2},
    )
    return (
        result,
        grad_features,
        sums_b[0],
        sums_b[1],
        sums_b[2].reshape(-1),
        sums_b[3].reshape(-1),
        grad_w_query,
        grad_w_key,
        grad_w_value,
        sums_b[4].reshape(-1),
        sums_b[5].reshape(-1),
        grad_w_out,
        sums_a[0].reshape(-1),
        sums_a[1].reshape(-1),
        sums_a[2].reshape(-1),
        grad_w_up,
        sums_a[4].reshape(-1),
        grad_w_down,
        sums_a[3].reshape(-1),
    )


def solution(mesh):
    token, split = P("dp", None), P(("dp", "mp"), None)
    columns, lines, cut, copy = P(None, "mp"), P("mp", None), P("mp"), P()
    return jax.shard_map(
        per_device,
        mesh=mesh,
        in_specs=(
            token, token, P("dp"), P("dp"), token, copy, copy, copy, copy, columns, columns,
            columns, cut, cut, lines, copy, copy, copy, columns, cut, lines, copy, token,
        ),
        out_specs=(
            split, split, copy, copy, copy, copy, columns, columns, columns, cut, cut, lines,
            copy, copy, copy, columns, cut, lines, copy,
        ),
        check_vma=False,
    )
```

profile of v0, /device:TPU:0, one launch (start us, length us, event | category | flops | bytes accessed | tf_op | source)
XLA Modules:
  0.0 117.7 jit_solution(15317056331395111921)
XLA Ops:
  0.7 0.5 collective-permute-start
  1.3 0.4 collective-permute-start.6
  1.8 0.4 collective-permute-start.1
  2.2 0.8 collective-permute-done.5
  3.0 0.4 collective-permute-start.2
  3.5 0.4 collective-permute-start.4
  3.9 4.2 %shard_map.366 = (f32[384,768]{1,0:T(8,128)S(1)}, bf16[32,384]{1,0:T(8,128)(2,1)S(1)}, bf16[384,768]{1,0:T(8,128)(2,1)S(1)}, bf16[768,384]{1,0:T(8,128)(2,1)S(1)...) custom-call(bf16[768,768]{1,0:T(8,128)(2,1)} %refs_10_.1, ...), custom_call_target="tpu_custom_call" | custom-call | tf_op jit(solution)/shard_map/pallas_call | solution.py:91
  8.4 7.3 %shard_map.367 = (bf16[384,384]{1,0:T(8,128)(2,1)S(1)}, bf16[384,384]{1,0:T(8,128)(2,1)S(1)}, bf16[384,384]{1,0:T(8,128)(2,1)S(1)}, bf16[3,16,128,256]{3,2,1,0:T...) custom-call(f32[384,768]{1,0:T(8,128)S(1)} %get-tuple-element.135.hi, ...), custom_call_target="tpu_custom_call" | custom-call | tf_op jit(solution)/shard_map/pallas_call | solution.py:91
  15.7 0.4 collective-permute-start.9
  16.1 2.9 %shard_map.368 = (bf16[1168,384]{1,0:T(8,128)(2,1)S(1)}, bf16[1168,384]{1,0:T(8,128)(2,1)S(1)}, f32[384,768]{1,0:T(8,128)S(1)}, bf16[384,768]{1,0:T(8,128)(2,1)S(1)}) custom-call(f32[384,768]{1,0:T(8,128)S(1)} %get-tuple-element.140.middle, f32[384,768]{1,0:T(8,128)S(1)} %get-tuple-element.145.slope, bf16[768,384]{1,0:T(8,128)(2,1)S(1)} %copy-done.1, ...), custom_call_target="tpu_custom_call" | custom-call | tf_op jit(solution)/shard_map/pallas_call | solution.py:91
  19.2 1.2 %shard_map.369 = (bf16[192,384]{1,0:T(8,128)(2,1)S(1)}, bf16[192,384]{1,0:T(8,128)(2,1)S(1)}, bf16[192,384]{1,0:T(8,128)(2,1)S(1)}, bf16[192,384]{1,0:T(8,128)(2,1)S(1)}) custom-call(bf16[1536,384]{1,0:T(8,128)(2,1)S(1)} %get-tuple-element.151.kept, bf16[1536,384]{1,0:T(8,128)(2,1)S(1)} %collective-permute-done.9.got, bf16[768,768]{1,0:T(8,128)(2,1)S(1)} %copy-done, ...), custom_call_target="tpu_custom_call" | custom-call | tf_op jit(solution)/shard_map/pallas_call | solution.py:91
  20.4 2.9 %collective-permute-start.13 = (bf16[192,384]{1,0:T(8,128)(2,1)S(1)}, bf16[192,384]{1,0:T(8,128)(2,1)S(1)}, u32[]{:S(2)}, u32[]{:S(2)}) collective-permute-start(bf16[192,384]{1,0:T(8,128)(2,1)S(1)} %get-tuple-element.158), channel_id=1, source_target_pairs={{0,4},{2,6},{4,0},{6,2},{8,12},{10,14},{12,8},{14,10},{16,20},{18,... | collective-permute-start | bytes 442376 | tf_op jit(solution)/shard_map/ppermute | solution.py:737
  23.4 1.5 %collective-permute-start.12 = (bf16[192,384]{1,0:T(8,128)(2,1)S(1)}, bf16[192,384]{1,0:T(8,128)(2,1)S(1)}, u32[]{:S(2)}, u32[]{:S(2)}) collective-permute-start(bf16[192,384]{1,0:T(8,128)(2,1)S(1)} %get-tuple-element.156), channel_id=1, source_target_pairs={{0,2},{2,0},{4,6},{6,4},{8,10},{10,8},{12,14},{14,12},{16,18},{18,... | collective-permute-start | bytes 442376 | tf_op jit(solution)/shard_map/ppermute | solution.py:737
  24.9 1.9 %shard_map.370 = (bf16[400,384]{1,0:T(8,128)(2,1)S(1)}, bf16[400,384]{1,0:T(8,128)(2,1)S(1)}, bf16[384,384]{1,0:T(8,128)(2,1)S(1)}, bf16[384,384]{1,0:T(8,128)(2,1)S(1)}) custom-call(bf16[1536,384]{1,0:T(8,128)(2,1)S(1)} %get-tuple-element.151.kept, bf16[1536,384]{1,0:T(8,128)(2,1)S(1)} %collective-permute-done.9.got, ...), custom_call_target="tpu_custom_call" | custom-call | tf_op jit(solution)/shard_map/pallas_call | solution.py:91
  26.8 0.6 collective-permute-start.11
  27.4 0.3 collective-permute-start.14
  27.6 1.3 %collective-permute-done.12.refs_1_ = bf16[192,384]{1,0:T(8,128)(2,1)S(1)} collective-permute-done((bf16[192,384]{1,0:T(8,128)(2,1)S(1)}, bf16[192,384]{1,0:T(8,128)(2,1)S(1)}, u32[]{:S(2)}, u32[]{:S(2)}) %collective-permute-start.12) | collective-permute-done | bytes 147488 | tf_op jit(solution)/shard_map/ppermute | solution.py:737
  29.0 0.8 shard_map.371
  29.8 4.2 %shard_map.372 = (bf16[1152,384]{1,0:T(8,128)(2,1)S(1)}, bf16[1152,384]{1,0:T(8,128)(2,1)S(1)}) custom-call(bf16[384,384]{1,0:T(8,128)(2,1)S(1)} %get-tuple-element.137.q_own, bf16[384,384]{1,0:T(8,128)(2,1)S(1)} %get-tuple-element.138.k_own, bf16[384,384]{1,0:T(8,128)(2,1)S(1)} %get-tuple-element.139.v_own, bf16[384,384]{1,0:T(8,128)(2,1)S(1)} %get-tuple-element.161.ga_own, ...), custom_call_target="tpu_custom_call" | custom-call | tf_op jit(solution)/shard_map/pallas_call | solution.py:91
  34.1 0.5 collective-permute-start.15
  34.6 1.0 collective-permute-done.14.second_got
  35.8 1.1 collective-permute-start.19
  36.9 0.9 collective-permute-start.20
  37.9 2.2 %shard_map.374 = (bf16[576,384]{1,0:T(8,128)(2,1)S(1)}, bf16[576,384]{1,0:T(8,128)(2,1)S(1)}, bf16[576,384]{1,0:T(8,128)(2,1)S(1)}, bf16[576,384]{1,0:T(8,128)(2,1)S(1)}, f32[48,384]{1,0:T(8,128)S(1)}) custom-call(bf16[768,384]{1,0:T(8,128)(2,1)S(1)} %get-tuple-element.178.normed_t, bf16[768,384]{1,0:T(8,128)(2,1)S(1)} %collective-permute-done.15.normed_t_got, ...), custom_call_target="tpu_custom_call" | custom-call | tf_op jit(solution)/shard_map/pallas_call | solution.py:91
  40.1 2.0 %collective-permute-start.17 = (bf16[576,384]{1,0:T(8,128)(2,1)S(1)}, bf16[576,384]{1,0:T(8,128)(2,1)S(1)}, u32[]{:S(2)}, u32[]{:S(2)}) collective-permute-start(bf16[576,384]{1,0:T(8,128)(2,1)S(1)} %get-tuple-element.181), channel_id=1, source_target_pairs={{0,2},{2,0},{4,6},{6,4},{8,10},{10,8},{12,14},{14,12},{16,18},{18,... | collective-permute-start | bytes 1327112 | tf_op jit(solution)/shard_map/ppermute | solution.py:737
  42.2 1.1 collective-permute-done.20.second_got
  43.4 1.3 %collective-permute-start.23 = (bf16[160,384]{1,0:T(8,128)(2,1)S(1)}, bf16[160,384]{1,0:T(8,128)(2,1)S(1)}, u32[]{:S(2)}, u32[]{:S(2)}) collective-permute-start(bf16[160,384]{1,0:T(8,128)(2,1)S(1)} %get-tuple-element.189.near), channel_id=1, source_target_pairs={{0,8},{2,10},{4,12},{6,14},{8,0},{10,2},{12,4},{14,6},{16,24},{18,... | collective-permute-start | bytes 368648 | tf_op jit(solution)/shard_map/ppermute | solution.py:740
  44.8 2.5 %collective-permute-start.25 = (bf16[144,384]{1,0:T(8,128)(2,1)S(1)}, bf16[144,384]{1,0:T(8,128)(2,1)S(1)}, u32[]{:S(2)}, u32[]{:S(2)}) collective-permute-start(bf16[144,384]{1,0:T(8,128)(2,1)S(1)} %get-tuple-element.191), channel_id=1, source_target_pairs={{0,24},{2,26},{4,28},{6,30},{8,16},{10,18},{12,20},{14,22},{16,8},... | collective-permute-start | bytes 331784 | tf_op jit(solution)/shard_map/ppermute | solution.py:740
  47.4 6.6 %shard_map.376 = (f32[384,768]{1,0:T(8,128)}, f32[48,384]{1,0:T(8,128)S(1)}, bf16[48,384]{1,0:T(8,128)(2,1)S(1)}) custom-call(bf16[1152,384]{1,0:T(8,128)(2,1)S(1)} %get-tuple-element.167.kept.refs_0_, bf16[1152,384]{1,0:T(8,128)(2,1)S(1)} %get-tuple-element.179.refs_1_, bf16[768,384]{1,0:T(8,128)(2,1)S(1)} %copy-done.2, bf16[768,384]{1,0:T(8,128)(2,1)S(1)} %copy-done.3, ...), custom_call_target="tpu_custom_call" | custom-call | tf_op jit(solution)/shard_map/pallas_call | solution.py:91
  54.1 1.2 %collective-permute-done.21.refs_1_ = bf16[48,384]{1,0:T(8,128)(2,1)S(1)} collective-permute-done((bf16[48,384]{1,0:T(8,128)(2,1)S(1)}, bf16[48,384]{1,0:T(8,128)(2,1)S(1)}, u32[]{:S(2)}, u32[]{:S(2)}) %collective-permute-start.21) | collective-permute-done | bytes 36896 | tf_op jit(solution)/shard_map/ppermute | solution.py:734
  55.3 0.2 shard_map.377
  55.5 2.0 %collective-permute-start.26 = (bf16[288,384]{1,0:T(8,128)(2,1)S(1)}, bf16[288,384]{1,0:T(8,128)(2,1)S(1)}, u32[]{:S(2)}, u32[]{:S(2)}) collective-permute-start(bf16[288,384]{1,0:T(8,128)(2,1)S(1)} %get-tuple-element.199), channel_id=1, source_target_pairs={{0,2},{2,0},{4,6},{6,4},{8,10},{10,8},{12,14},{14,12},{16,18},{18,... | collective-permute-start | bytes 663560 | tf_op jit(solution)/shard_map/ppermute | solution.py:737
  57.5 2.7 %collective-permute-start.22 = (bf16[336,384]{1,0:T(8,128)(2,1)S(1)}, bf16[336,384]{1,0:T(8,128)(2,1)S(1)}, u32[]{:S(2)}, u32[]{:S(2)}) collective-permute-start(bf16[336,384]{1,0:T(8,128)(2,1)S(1)} %get-tuple-element.197), channel_id=1, source_target_pairs={{0,4},{2,6},{4,0},{6,2},{8,12},{10,14},{12,8},{14,10},{16,20},{18,... | collective-permute-start | bytes 774152 | tf_op jit(solution)/shard_map/ppermute | solution.py:737
  60.4 3.0 %collective-permute-start.37 = (bf16[144,384]{1,0:T(8,128)(2,1)S(1)}, bf16[144,384]{1,0:T(8,128)(2,1)S(1)}, u32[]{:S(2)}, u32[]{:S(2)}) collective-permute-start(bf16[144,384]{1,0:T(8,128)(2,1)S(1)} %get-tuple-element.203), channel_id=1, source_target_pairs={{0,24},{2,26},{4,28},{6,30},{8,16},{10,18},{12,20},{14,22},{16,8},... | collective-permute-start | bytes 331784 | tf_op jit(solution)/shard_map/ppermute | solution.py:740
  63.3 0.3 collective-permute-start.36
  63.7 1.1 collective-permute-start.35
  64.8 1.7 %collective-permute-done.22.first_got = bf16[336,384]{1,0:T(8,128)(2,1)S(1)} collective-permute-done((bf16[336,384]{1,0:T(8,128)(2,1)S(1)}, bf16[336,384]{1,0:T(8,128)(2,1)S(1)}, u32[]{:S(2)}, u32[]{:S(2)}) %collective-permute-start.22) | collective-permute-done | bytes 258080 | tf_op jit(solution)/shard_map/ppermute | solution.py:737
  66.7 1.8 %collective-permute-start.27 = (bf16[192,384]{1,0:T(8,128)(2,1)S(1)}, bf16[192,384]{1,0:T(8,128)(2,1)S(1)}, u32[]{:S(2)}, u32[]{:S(2)}) collective-permute-start(bf16[192,384]{1,0:T(8,128)(2,1)S(1)} %get-tuple-element.207.near), channel_id=1, source_target_pairs={{0,8},{2,10},{4,12},{6,14},{8,0},{10,2},{12,4},{14,6},{16,24},{18,... | collective-permute-start | bytes 442376 | tf_op jit(solution)/shard_map/ppermute | solution.py:740
  68.5 1.7 %collective-permute-start.28 = (bf16[144,384]{1,0:T(8,128)(2,1)S(1)}, bf16[144,384]{1,0:T(8,128)(2,1)S(1)}, u32[]{:S(2)}, u32[]{:S(2)}) collective-permute-start(bf16[144,384]{1,0:T(8,128)(2,1)S(1)} %get-tuple-element.208), channel_id=1, source_target_pairs={{0,16},{2,18},{4,20},{6,22},{8,24},{10,26},{12,28},{14,30},{16,0},... | collective-permute-start | bytes 331784 | tf_op jit(solution)/shard_map/ppermute | solution.py:740
  70.2 0.9 collective-permute-start.29
  71.1 3.9 %collective-permute-done.36.middle = bf16[160,384]{1,0:T(8,128)(2,1)S(1)} collective-permute-done((bf16[160,384]{1,0:T(8,128)(2,1)S(1)}, bf16[160,384]{1,0:T(8,128)(2,1)S(1)}, u32[]{:S(2)}, u32[]{:S(2)}) %collective-permute-start.36) | collective-permute-done | bytes 122912 | tf_op jit(solution)/shard_map/ppermute | solution.py:740
  75.0 0.8 shard_map.383
  75.9 1.4 %collective-permute-start.40 = (bf16[576,384]{1,0:T(8,128)(2,1)S(1)}, bf16[576,384]{1,0:T(8,128)(2,1)S(1)}, u32[]{:S(2)}, u32[]{:S(2)}) collective-permute-start(bf16[576,384]{1,0:T(8,128)(2,1)S(1)} %get-tuple-element.228.refs_0_), channel_id=1, source_target_pairs={{0,4},{2,6},{4,0},{6,2},{8,12},{10,14},{12,8},{14,10},{16,20},{18,... | collective-permute-start | bytes 1327112 | tf_op jit(solution)/shard_map/ppermute | solution.py:737
  77.2 4.5 %collective-permute-done.28.middle_got = bf16[144,384]{1,0:T(8,128)(2,1)S(1)} collective-permute-done((bf16[144,384]{1,0:T(8,128)(2,1)S(1)}, bf16[144,384]{1,0:T(8,128)(2,1)S(1)}, u32[]{:S(2)}, u32[]{:S(2)}) %collective-permute-start.28) | collective-permute-done | bytes 110624 | tf_op jit(solution)/shard_map/ppermute | solution.py:740
  81.8 3.3 %collective-permute-start.31 = (bf16[192,384]{1,0:T(8,128)(2,1)S(1)}, bf16[192,384]{1,0:T(8,128)(2,1)S(1)}, u32[]{:S(2)}, u32[]{:S(2)}) collective-permute-start(bf16[192,384]{1,0:T(8,128)(2,1)S(1)} %get-tuple-element.210.own), channel_id=1, source_target_pairs={{0,16},{2,18},{4,20},{6,22},{8,24},{10,26},{12,28},{14,30},{16,0},... | collective-permute-start | bytes 442376 | tf_op jit(solution)/shard_map/ppermute | solution.py:740
  85.1 1.4 %collective-permute-start.32 = (bf16[144,384]{1,0:T(8,128)(2,1)S(1)}, bf16[144,384]{1,0:T(8,128)(2,1)S(1)}, u32[]{:S(2)}, u32[]{:S(2)}) collective-permute-start(bf16[144,384]{1,0:T(8,128)(2,1)S(1)} %get-tuple-element.211), channel_id=1, source_target_pairs={{0,24},{2,26},{4,28},{6,30},{8,16},{10,18},{12,20},{14,22},{16,8},... | collective-permute-start | bytes 331784 | tf_op jit(solution)/shard_map/ppermute | solution.py:740
  86.5 0.4 collective-permute-start.41
  86.9 1.1 collective-permute-start.42
  88.0 5.1 %collective-permute-done.32.far = bf16[144,384]{1,0:T(8,128)(2,1)S(1)} collective-permute-done((bf16[144,384]{1,0:T(8,128)(2,1)S(1)}, bf16[144,384]{1,0:T(8,128)(2,1)S(1)}, u32[]{:S(2)}, u32[]{:S(2)}) %collective-permute-start.32) | collective-permute-done | bytes 110624 | tf_op jit(solution)/shard_map/ppermute | solution.py:740
  93.2 1.5 %collective-permute-done.31.middle = bf16[192,384]{1,0:T(8,128)(2,1)S(1)} collective-permute-done((bf16[192,384]{1,0:T(8,128)(2,1)S(1)}, bf16[192,384]{1,0:T(8,128)(2,1)S(1)}, u32[]{:S(2)}, u32[]{:S(2)}) %collective-permute-start.31) | collective-permute-done | bytes 147488 | tf_op jit(solution)/shard_map/ppermute | solution.py:740
  94.9 0.5 collective-permute-start.34
  95.4 0.7 collective-permute-start.33
  96.1 2.3 %shard_map.382 = bf16[384,768]{1,0:T(8,128)(2,1)} custom-call(f32[384,768]{1,0:T(8,128)S(1)} %get-tuple-element.140.middle, bf16[384,768]{1,0:T(8,128)(2,1)S(1)} %get-tuple-element.141.active, bf16[384,768]{1,0:T(8,128)(2,1)S(1)} %copy-done.5, bf16[384,768]{1,0:T(8,128)(2,1)S(1)} %collective-permute-done.8.wd, bf16[6,128]{1,0:T(8,128)(2,1)} %bitcast.35), custom_call_target="tpu_custom_call" | custom-call | tf_op jit(solution)/shard_map/pallas_call | solution.py:91
  98.4 0.6 shard_map.384
  99.0 2.1 %shard_map.385 = (f32[768,384]{1,0:T(8,128)}, f32[384,768]{1,0:T(8,128)}, f32[384,768]{1,0:T(8,128)}) custom-call(bf16[576,384]{1,0:T(8,128)(2,1)S(1)} %get-tuple-element.228.refs_0_, bf16[576,384]{1,0:T(8,128)(2,1)S(1)} %collective-permute-done.39.refs_1_, bf16[576,384]{1,0:T(8,128)(2,1)S(1)} %collective-permute-done.40.refs_2_, ...), custom_call_target="tpu_custom_call" | custom-call | flops 10000000000 | tf_op jit(solution)/shard_map/pallas_call | solution.py:91
  101.1 6.4 %collective-permute-done.34.refs_2_ = bf16[576,384]{1,0:T(8,128)(2,1)S(1)} collective-permute-done((bf16[576,384]{1,0:T(8,128)(2,1)S(1)}, bf16[576,384]{1,0:T(8,128)(2,1)S(1)}, u32[]{:S(2)}, u32[]{:S(2)}) %collective-permute-start.34) | collective-permute-done | bytes 442400 | tf_op jit(solution)/shard_map/ppermute | solution.py:737
  107.5 0.9 collective-permute-done.33.refs_1_
  108.5 1.7 %collective-permute-start.45 = (bf16[288,384]{1,0:T(8,128)(2,1)S(1)}, bf16[288,384]{1,0:T(8,128)(2,1)S(1)}, u32[]{:S(2)}, u32[]{:S(2)}) collective-permute-start(bf16[288,384]{1,0:T(8,128)(2,1)S(1)} %slice.19), channel_id=1, source_target_pairs={{0,4},{2,6},{4,0},{6,2},{8,12},{10,14},{12,8},{14,10},{16,20},{18,... | collective-permute-start | bytes 663560 | tf_op jit(solution)/shard_map/ppermute | solution.py:737
  110.2 0.5 collective-permute-start.44
  110.7 2.0 %shard_map.387 = (f32[768,384]{1,0:T(8,128)}, f32[768,384]{1,0:T(8,128)}, f32[768,384]{1,0:T(8,128)}) custom-call(bf16[576,384]{1,0:T(8,128)(2,1)S(1)} %get-tuple-element.212.refs_0_, bf16[624,384]{1,0:T(8,128)(2,1)S(1)} %collective-permute-done.33.refs_1_, bf16[576,384]{1,0:T(8,128)(2,1)S(1)} %collective-permute-done.34.refs_2_), custom_call_target="tpu_custom_call" | custom-call | tf_op jit(solution)/shard_map/pallas_call | solution.py:91
  112.7 0.7 shard_map.386
  113.4 1.8 %collective-permute-done.45.second = bf16[288,384]{1,0:T(8,128)(2,1)S(1)} collective-permute-done((bf16[288,384]{1,0:T(8,128)(2,1)S(1)}, bf16[288,384]{1,0:T(8,128)(2,1)S(1)}, u32[]{:S(2)}, u32[]{:S(2)}) %collective-permute-start.45) | collective-permute-done | bytes 221216 | tf_op jit(solution)/shard_map/ppermute | solution.py:737
  115.2 1.3 %collective-permute-done.44.first = bf16[288,384]{1,0:T(8,128)(2,1)S(1)} collective-permute-done((bf16[288,384]{1,0:T(8,128)(2,1)S(1)}, bf16[288,384]{1,0:T(8,128)(2,1)S(1)}, u32[]{:S(2)}, u32[]{:S(2)}) %collective-permute-start.44) | collective-permute-done | bytes 221216 | tf_op jit(solution)/shard_map/ppermute | solution.py:737
  116.5 1.0 shard_map.388
  (71 shorter events, 2.2 us)
Async XLA Ops:
  0.7 7.4 %collective-permute-start = (bf16[768,384]{1,0:T(8,128)(2,1)}, bf16[768,384]{1,0:T(8,128)(2,1)S(1)}, u32[]{:S(2)}, u32[]{:S(2)}) collective-permute-start(bf16[768,384]{1,0:T(8,128)(2,1)} %refs_2_.1), channel_id=1, source_target_pairs={{0,1},{1,0},{2,3},{3,2},{4,5},{5,4},{6,7},{7,6},{8,9},{9,8},{10,11... | collective-permute-start | bytes 1769480 | tf_op jit(solution)/shard_map/ppermute | solution.py:734
  1.2 1.8 %collective-permute-start.5 = (bf16[384]{0:T(512)(128)(2,1)}, bf16[384]{0:T(512)(128)(2,1)S(1)}, u32[]{:S(2)}, u32[]{:S(2)}) collective-permute-start(bf16[384]{0:T(512)(128)(2,1)} %param.35), channel_id=1, source_target_pairs={{0,1},{1,0},{2,3},{3,2},{4,5},{5,4},{6,7},{7,6},{8,9},{9,8},{10,11... | collective-permute-start | bytes 2312 | tf_op jit(solution)/shard_map/ppermute | solution.py:734
  1.3 2.1 %collective-permute-start.6 = (bf16[384]{0:T(512)(128)(2,1)}, bf16[384]{0:T(512)(128)(2,1)S(1)}, u32[]{:S(2)}, u32[]{:S(2)}) collective-permute-start(bf16[384]{0:T(512)(128)(2,1)} %param.36), channel_id=1, source_target_pairs={{0,1},{1,0},{2,3},{3,2},{4,5},{5,4},{6,7},{7,6},{8,9},{9,8},{10,11... | collective-permute-start | bytes 2312 | tf_op jit(solution)/shard_map/ppermute | solution.py:734
  1.7 1.8 %collective-permute-start.7 = (bf16[384]{0:T(512)(128)(2,1)}, bf16[384]{0:T(512)(128)(2,1)S(1)}, u32[]{:S(2)}, u32[]{:S(2)}) collective-permute-start(bf16[384]{0:T(512)(128)(2,1)} %param.42), channel_id=1, source_target_pairs={{0,1},{1,0},{2,3},{3,2},{4,5},{5,4},{6,7},{7,6},{8,9},{9,8},{10,11... | collective-permute-start | bytes 2312 | tf_op jit(solution)/shard_map/ppermute | solution.py:734
  1.8 6.5 %collective-permute-start.1 = (bf16[768,384]{1,0:T(8,128)(2,1)}, bf16[768,384]{1,0:T(8,128)(2,1)S(1)}, u32[]{:S(2)}, u32[]{:S(2)}) collective-permute-start(bf16[768,384]{1,0:T(8,128)(2,1)} %refs_3_.1), channel_id=1, source_target_pairs={{0,1},{1,0},{2,3},{3,2},{4,5},{5,4},{6,7},{7,6},{8,9},{9,8},{10,11... | collective-permute-start | bytes 1769480 | tf_op jit(solution)/shard_map/ppermute | solution.py:734
  3.0 5.3 %collective-permute-start.2 = (bf16[768,384]{1,0:T(8,128)(2,1)}, bf16[768,384]{1,0:T(8,128)(2,1)S(1)}, u32[]{:S(2)}, u32[]{:S(2)}) collective-permute-start(bf16[768,384]{1,0:T(8,128)(2,1)} %refs_4_.1), channel_id=1, source_target_pairs={{0,1},{1,0},{2,3},{3,2},{4,5},{5,4},{6,7},{7,6},{8,9},{9,8},{10,11... | collective-permute-start | bytes 1769480 | tf_op jit(solution)/shard_map/ppermute | solution.py:734
  3.4 4.9 %collective-permute-start.3 = (bf16[384,768]{1,0:T(8,128)(2,1)}, bf16[384,768]{1,0:T(8,128)(2,1)S(1)}, u32[]{:S(2)}, u32[]{:S(2)}) collective-permute-start(bf16[384,768]{1,0:T(8,128)(2,1)} %wo_own.3), channel_id=1, source_target_pairs={{0,1},{1,0},{2,3},{3,2},{4,5},{5,4},{6,7},{7,6},{8,9},{9,8},{10,11... | collective-permute-start | bytes 1769480 | tf_op jit(solution)/shard_map/ppermute | solution.py:734
  3.5 4.8 %collective-permute-start.4 = (bf16[768,384]{1,0:T(8,128)(2,1)}, bf16[768,384]{1,0:T(8,128)(2,1)S(1)}, u32[]{:S(2)}, u32[]{:S(2)}) collective-permute-start(bf16[768,384]{1,0:T(8,128)(2,1)} %wu_own.3), channel_id=1, source_target_pairs={{0,1},{1,0},{2,3},{3,2},{4,5},{5,4},{6,7},{7,6},{8,9},{9,8},{10,11... | collective-permute-start | bytes 1769480 | tf_op jit(solution)/shard_map/ppermute | solution.py:734
  3.9 4.2 %copy-start.5 = (bf16[384,768]{1,0:T(8,128)(2,1)S(1)}, bf16[384,768]{1,0:T(8,128)(2,1)}, u32[]{:S(2)}) copy-start(bf16[384,768]{1,0:T(8,128)(2,1)} %wd_own.3) | copy-start | bytes 1769476
  3.9 4.4 %copy-start.1 = (bf16[768,384]{1,0:T(8,128)(2,1)S(1)}, bf16[768,384]{1,0:T(8,128)(2,1)}, u32[]{:S(2)}) copy-start(bf16[768,384]{1,0:T(8,128)(2,1)} %wu_own.3) | copy-start | bytes 1769476
  3.9 4.4 %copy-start.6 = (bf16[384,768]{1,0:T(8,128)(2,1)S(1)}, bf16[384,768]{1,0:T(8,128)(2,1)}, u32[]{:S(2)}) copy-start(bf16[384,768]{1,0:T(8,128)(2,1)} %wo_own.3) | copy-start | bytes 1769476
  8.1 8.0 %collective-permute-start.8 = (bf16[384,768]{1,0:T(8,128)(2,1)S(1)}, bf16[384,768]{1,0:T(8,128)(2,1)S(1)}, u32[]{:S(2)}, u32[]{:S(2)}) collective-permute-start(bf16[384,768]{1,0:T(8,128)(2,1)S(1)} %copy-done.5), channel_id=1, source_target_pairs={{0,1},{1,0},{2,3},{3,2},{4,5},{5,4},{6,7},{7,6},{8,9},{9,8},{10,11... | collective-permute-start | bytes 1769480 | tf_op jit(solution)/shard_map/ppermute | solution.py:734
  8.4 7.7 %copy-start = (bf16[768,768]{1,0:T(8,128)(2,1)S(1)}, bf16[768,768]{1,0:T(8,128)(2,1)}, u32[]{:S(2)}) copy-start(bf16[768,768]{1,0:T(8,128)(2,1)} %cots.3) | copy-start | bytes 3538948
  15.7 3.6 %collective-permute-start.9 = (bf16[1536,384]{1,0:T(8,128)(2,1)S(1)}, bf16[1536,384]{1,0:T(8,128)(2,1)S(1)}, u32[]{:S(2)}, u32[]{:S(2)}) collective-permute-start(bf16[1536,384]{1,0:T(8,128)(2,1)S(1)} %get-tuple-element.149), channel_id=1, source_target_pairs={{0,1},{1,0},{2,3},{3,2},{4,5},{5,4},{6,7},{7,6},{8,9},{9,8},{10,11... | collective-permute-start | bytes 3538952 | tf_op jit(solution)/shard_map/ppermute | solution.py:734
  19.0 5.8 %collective-permute-start.10 = (bf16[1168,384]{1,0:T(8,128)(2,1)S(1)}, bf16[1168,384]{1,0:T(8,128)(2,1)S(1)}, u32[]{:S(2)}, u32[]{:S(2)}) collective-permute-start(bf16[1168,384]{1,0:T(8,128)(2,1)S(1)} %get-tuple-element.153), channel_id=1, source_target_pairs={{0,1},{1,0},{2,3},{3,2},{4,5},{5,4},{6,7},{7,6},{8,9},{9,8},{10,11... | collective-permute-start | bytes 2691080 | tf_op jit(solution)/shard_map/ppermute | solution.py:734
  20.4 7.2 %collective-permute-start.13 = (bf16[192,384]{1,0:T(8,128)(2,1)S(1)}, bf16[192,384]{1,0:T(8,128)(2,1)S(1)}, u32[]{:S(2)}, u32[]{:S(2)}) collective-permute-start(bf16[192,384]{1,0:T(8,128)(2,1)S(1)} %get-tuple-element.158), channel_id=1, source_target_pairs={{0,4},{2,6},{4,0},{6,2},{8,12},{10,14},{12,8},{14,10},{16,20},{18,... | collective-permute-start | bytes 442376 | tf_op jit(solution)/shard_map/ppermute | solution.py:737
  23.4 5.6 %collective-permute-start.12 = (bf16[192,384]{1,0:T(8,128)(2,1)S(1)}, bf16[192,384]{1,0:T(8,128)(2,1)S(1)}, u32[]{:S(2)}, u32[]{:S(2)}) collective-permute-start(bf16[192,384]{1,0:T(8,128)(2,1)S(1)} %get-tuple-element.156), channel_id=1, source_target_pairs={{0,2},{2,0},{4,6},{6,4},{8,10},{10,8},{12,14},{14,12},{16,18},{18,... | collective-permute-start | bytes 442376 | tf_op jit(solution)/shard_map/ppermute | solution.py:737
  26.8 8.8 %collective-permute-start.11 = (bf16[400,384]{1,0:T(8,128)(2,1)S(1)}, bf16[400,384]{1,0:T(8,128)(2,1)S(1)}, u32[]{:S(2)}, u32[]{:S(2)}) collective-permute-start(bf16[400,384]{1,0:T(8,128)(2,1)S(1)} %get-tuple-element.155), channel_id=1, source_target_pairs={{0,2},{2,0},{4,6},{6,4},{8,10},{10,8},{12,14},{14,12},{16,18},{18,... | collective-permute-start | bytes 921608 | tf_op jit(solution)/shard_map/ppermute | solution.py:737
  27.4 8.2 %collective-permute-start.14 = (bf16[384,384]{1,0:T(8,128)(2,1)S(1)}, bf16[384,384]{1,0:T(8,128)(2,1)S(1)}, u32[]{:S(2)}, u32[]{:S(2)}) collective-permute-start(bf16[384,384]{1,0:T(8,128)(2,1)S(1)} %get-tuple-element.170), channel_id=1, source_target_pairs={{0,4},{2,6},{4,0},{6,2},{8,12},{10,14},{12,8},{14,10},{16,20},{18,... | collective-permute-start | bytes 884744 | tf_op jit(solution)/shard_map/ppermute | solution.py:737
  34.0 3.9 %collective-permute-start.16 = (bf16[1152,384]{1,0:T(8,128)(2,1)S(1)}, bf16[1152,384]{1,0:T(8,128)(2,1)S(1)}, u32[]{:S(2)}, u32[]{:S(2)}) collective-permute-start(bf16[1152,384]{1,0:T(8,128)(2,1)S(1)} %get-tuple-element.179.refs_1_), channel_id=1, source_target_pairs={{0,1},{1,0},{2,3},{3,2},{4,5},{5,4},{6,7},{7,6},{8,9},{9,8},{10,11... | collective-permute-start | bytes 2654216 | tf_op jit(solution)/shard_map/ppermute | solution.py:734
  34.1 3.8 %collective-permute-start.15 = (bf16[768,384]{1,0:T(8,128)(2,1)S(1)}, bf16[768,384]{1,0:T(8,128)(2,1)S(1)}, u32[]{:S(2)}, u32[]{:S(2)}) collective-permute-start(bf16[768,384]{1,0:T(8,128)(2,1)S(1)} %get-tuple-element.178.normed_t), channel_id=1, source_target_pairs={{0,1},{1,0},{2,3},{3,2},{4,5},{5,4},{6,7},{7,6},{8,9},{9,8},{10,11... | collective-permute-start | bytes 1769480 | tf_op jit(solution)/shard_map/ppermute | solution.py:734
  35.8 7.5 %collective-permute-start.19 = (bf16[304,384]{1,0:T(8,128)(2,1)S(1)}, bf16[304,384]{1,0:T(8,128)(2,1)S(1)}, u32[]{:S(2)}, u32[]{:S(2)}) collective-permute-start(bf16[304,384]{1,0:T(8,128)(2,1)S(1)} %get-tuple-element.174), channel_id=1, source_target_pairs={{0,4},{2,6},{4,0},{6,2},{8,12},{10,14},{12,8},{14,10},{16,20},{18,... | collective-permute-start | bytes 700424 | tf_op jit(solution)/shard_map/ppermute | solution.py:737
  36.9 6.4 %collective-permute-start.20 = (bf16[288,384]{1,0:T(8,128)(2,1)S(1)}, bf16[288,384]{1,0:T(8,128)(2,1)S(1)}, u32[]{:S(2)}, u32[]{:S(2)}) collective-permute-start(bf16[288,384]{1,0:T(8,128)(2,1)S(1)} %get-tuple-element.176), channel_id=1, source_target_pairs={{0,2},{2,0},{4,6},{6,4},{8,10},{10,8},{12,14},{14,12},{16,18},{18,... | collective-permute-start | bytes 663560 | tf_op jit(solution)/shard_map/ppermute | solution.py:737
  40.1 13.9 %collective-permute-start.17 = (bf16[576,384]{1,0:T(8,128)(2,1)S(1)}, bf16[576,384]{1,0:T(8,128)(2,1)S(1)}, u32[]{:S(2)}, u32[]{:S(2)}) collective-permute-start(bf16[576,384]{1,0:T(8,128)(2,1)S(1)} %get-tuple-element.181), channel_id=1, source_target_pairs={{0,2},{2,0},{4,6},{6,4},{8,10},{10,8},{12,14},{14,12},{16,18},{18,... | collective-permute-start | bytes 1327112 | tf_op jit(solution)/shard_map/ppermute | solution.py:737
  42.0 12.0 %collective-permute-start.18 = (bf16[576,384]{1,0:T(8,128)(2,1)S(1)}, bf16[576,384]{1,0:T(8,128)(2,1)S(1)}, u32[]{:S(2)}, u32[]{:S(2)}) collective-permute-start(bf16[576,384]{1,0:T(8,128)(2,1)S(1)} %get-tuple-element.183), channel_id=1, source_target_pairs={{0,4},{2,6},{4,0},{6,2},{8,12},{10,14},{12,8},{14,10},{16,20},{18,... | collective-permute-start | bytes 1327112 | tf_op jit(solution)/shard_map/ppermute | solution.py:737
  43.3 4.1 %copy-start.2 = (bf16[768,384]{1,0:T(8,128)(2,1)S(1)}, bf16[768,384]{1,0:T(8,128)(2,1)}, u32[]{:S(2)}) copy-start(bf16[768,384]{1,0:T(8,128)(2,1)} %refs_2_.1) | copy-start | bytes 1769476
  43.3 4.1 %copy-start.3 = (bf16[768,384]{1,0:T(8,128)(2,1)S(1)}, bf16[768,384]{1,0:T(8,128)(2,1)}, u32[]{:S(2)}) copy-start(bf16[768,384]{1,0:T(8,128)(2,1)} %refs_3_.1) | copy-start | bytes 1769476
  43.3 4.1 %copy-start.4 = (bf16[768,384]{1,0:T(8,128)(2,1)S(1)}, bf16[768,384]{1,0:T(8,128)(2,1)}, u32[]{:S(2)}) copy-start(bf16[768,384]{1,0:T(8,128)(2,1)} %refs_4_.1) | copy-start | bytes 1769476
  43.4 16.8 %collective-permute-start.23 = (bf16[160,384]{1,0:T(8,128)(2,1)S(1)}, bf16[160,384]{1,0:T(8,128)(2,1)S(1)}, u32[]{:S(2)}, u32[]{:S(2)}) collective-permute-start(bf16[160,384]{1,0:T(8,128)(2,1)S(1)} %get-tuple-element.189.near), channel_id=1, source_target_pairs={{0,8},{2,10},{4,12},{6,14},{8,0},{10,2},{12,4},{14,6},{16,24},{18,... | collective-permute-start | bytes 368648 | tf_op jit(solution)/shard_map/ppermute | solution.py:740
  44.8 15.5 %collective-permute-start.25 = (bf16[144,384]{1,0:T(8,128)(2,1)S(1)}, bf16[144,384]{1,0:T(8,128)(2,1)S(1)}, u32[]{:S(2)}, u32[]{:S(2)}) collective-permute-start(bf16[144,384]{1,0:T(8,128)(2,1)S(1)} %get-tuple-element.191), channel_id=1, source_target_pairs={{0,24},{2,26},{4,28},{6,30},{8,16},{10,18},{12,20},{14,22},{16,8},... | collective-permute-start | bytes 331784 | tf_op jit(solution)/shard_map/ppermute | solution.py:740
  47.3 13.0 %collective-permute-start.24 = (bf16[144,384]{1,0:T(8,128)(2,1)S(1)}, bf16[144,384]{1,0:T(8,128)(2,1)S(1)}, u32[]{:S(2)}, u32[]{:S(2)}) collective-permute-start(bf16[144,384]{1,0:T(8,128)(2,1)S(1)} %get-tuple-element.190), channel_id=1, source_target_pairs={{0,16},{2,18},{4,20},{6,22},{8,24},{10,26},{12,28},{14,30},{16,0},... | collective-permute-start | bytes 331784 | tf_op jit(solution)/shard_map/ppermute | solution.py:740
  54.0 1.3 %collective-permute-start.21 = (bf16[48,384]{1,0:T(8,128)(2,1)S(1)}, bf16[48,384]{1,0:T(8,128)(2,1)S(1)}, u32[]{:S(2)}, u32[]{:S(2)}) collective-permute-start(bf16[48,384]{1,0:T(8,128)(2,1)S(1)} %get-tuple-element.194), channel_id=1, source_target_pairs={{0,1},{1,0},{2,3},{3,2},{4,5},{5,4},{6,7},{7,6},{8,9},{9,8},{10,11... | collective-permute-start | bytes 110600 | tf_op jit(solution)/shard_map/ppermute | solution.py:734
  55.5 9.3 %collective-permute-start.26 = (bf16[288,384]{1,0:T(8,128)(2,1)S(1)}, bf16[288,384]{1,0:T(8,128)(2,1)S(1)}, u32[]{:S(2)}, u32[]{:S(2)}) collective-permute-start(bf16[288,384]{1,0:T(8,128)(2,1)S(1)} %get-tuple-element.199), channel_id=1, source_target_pairs={{0,2},{2,0},{4,6},{6,4},{8,10},{10,8},{12,14},{14,12},{16,18},{18,... | collective-permute-start | bytes 663560 | tf_op jit(solution)/shard_map/ppermute | solution.py:737
  57.5 9.0 %collective-permute-start.22 = (bf16[336,384]{1,0:T(8,128)(2,1)S(1)}, bf16[336,384]{1,0:T(8,128)(2,1)S(1)}, u32[]{:S(2)}, u32[]{:S(2)}) collective-permute-start(bf16[336,384]{1,0:T(8,128)(2,1)S(1)} %get-tuple-element.197), channel_id=1, source_target_pairs={{0,4},{2,6},{4,0},{6,2},{8,12},{10,14},{12,8},{14,10},{16,20},{18,... | collective-permute-start | bytes 774152 | tf_op jit(solution)/shard_map/ppermute | solution.py:737
  60.4 9.9 %collective-permute-start.37 = (bf16[144,384]{1,0:T(8,128)(2,1)S(1)}, bf16[144,384]{1,0:T(8,128)(2,1)S(1)}, u32[]{:S(2)}, u32[]{:S(2)}) collective-permute-start(bf16[144,384]{1,0:T(8,128)(2,1)S(1)} %get-tuple-element.203), channel_id=1, source_target_pairs={{0,24},{2,26},{4,28},{6,30},{8,16},{10,18},{12,20},{14,22},{16,8},... | collective-permute-start | bytes 331784 | tf_op jit(solution)/shard_map/ppermute | solution.py:740
  63.3 11.7 %collective-permute-start.36 = (bf16[160,384]{1,0:T(8,128)(2,1)S(1)}, bf16[160,384]{1,0:T(8,128)(2,1)S(1)}, u32[]{:S(2)}, u32[]{:S(2)}) collective-permute-start(bf16[160,384]{1,0:T(8,128)(2,1)S(1)} %get-tuple-element.217.own), channel_id=1, source_target_pairs={{0,16},{2,18},{4,20},{6,22},{8,24},{10,26},{12,28},{14,30},{16,0},... | collective-permute-start | bytes 368648 | tf_op jit(solution)/shard_map/ppermute | solution.py:740
  63.7 11.4 %collective-permute-start.35 = (bf16[144,384]{1,0:T(8,128)(2,1)S(1)}, bf16[144,384]{1,0:T(8,128)(2,1)S(1)}, u32[]{:S(2)}, u32[]{:S(2)}) collective-permute-start(bf16[144,384]{1,0:T(8,128)(2,1)S(1)} %get-tuple-element.203), channel_id=1, source_target_pairs={{0,8},{2,10},{4,12},{6,14},{8,0},{10,2},{12,4},{14,6},{16,24},{18,... | collective-permute-start | bytes 331784 | tf_op jit(solution)/shard_map/ppermute | solution.py:740
  66.7 15.1 %collective-permute-start.27 = (bf16[192,384]{1,0:T(8,128)(2,1)S(1)}, bf16[192,384]{1,0:T(8,128)(2,1)S(1)}, u32[]{:S(2)}, u32[]{:S(2)}) collective-permute-start(bf16[192,384]{1,0:T(8,128)(2,1)S(1)} %get-tuple-element.207.near), channel_id=1, source_target_pairs={{0,8},{2,10},{4,12},{6,14},{8,0},{10,2},{12,4},{14,6},{16,24},{18,... | collective-permute-start | bytes 442376 | tf_op jit(solution)/shard_map/ppermute | solution.py:740
  68.5 13.2 %collective-permute-start.28 = (bf16[144,384]{1,0:T(8,128)(2,1)S(1)}, bf16[144,384]{1,0:T(8,128)(2,1)S(1)}, u32[]{:S(2)}, u32[]{:S(2)}) collective-permute-start(bf16[144,384]{1,0:T(8,128)(2,1)S(1)} %get-tuple-element.208), channel_id=1, source_target_pairs={{0,16},{2,18},{4,20},{6,22},{8,24},{10,26},{12,28},{14,30},{16,0},... | collective-permute-start | bytes 331784 | tf_op jit(solution)/shard_map/ppermute | solution.py:740
  70.2 11.5 %collective-permute-start.29 = (bf16[144,384]{1,0:T(8,128)(2,1)S(1)}, bf16[144,384]{1,0:T(8,128)(2,1)S(1)}, u32[]{:S(2)}, u32[]{:S(2)}) collective-permute-start(bf16[144,384]{1,0:T(8,128)(2,1)S(1)} %get-tuple-element.209), channel_id=1, source_target_pairs={{0,24},{2,26},{4,28},{6,30},{8,16},{10,18},{12,20},{14,22},{16,8},... | collective-permute-start | bytes 331784 | tf_op jit(solution)/shard_map/ppermute | solution.py:740
  75.9 10.6 %collective-permute-start.40 = (bf16[576,384]{1,0:T(8,128)(2,1)S(1)}, bf16[576,384]{1,0:T(8,128)(2,1)S(1)}, u32[]{:S(2)}, u32[]{:S(2)}) collective-permute-start(bf16[576,384]{1,0:T(8,128)(2,1)S(1)} %get-tuple-element.228.refs_0_), channel_id=1, source_target_pairs={{0,4},{2,6},{4,0},{6,2},{8,12},{10,14},{12,8},{14,10},{16,20},{18,... | collective-permute-start | bytes 1327112 | tf_op jit(solution)/shard_map/ppermute | solution.py:737
  77.2 9.7 %collective-permute-start.39 = (bf16[576,384]{1,0:T(8,128)(2,1)S(1)}, bf16[576,384]{1,0:T(8,128)(2,1)S(1)}, u32[]{:S(2)}, u32[]{:S(2)}) collective-permute-start(bf16[576,384]{1,0:T(8,128)(2,1)S(1)} %get-tuple-element.228.refs_0_), channel_id=1, source_target_pairs={{0,2},{2,0},{4,6},{6,4},{8,10},{10,8},{12,14},{14,12},{16,18},{18,... | collective-permute-start | bytes 1327112 | tf_op jit(solution)/shard_map/ppermute | solution.py:737
  81.8 12.9 %collective-permute-start.31 = (bf16[192,384]{1,0:T(8,128)(2,1)S(1)}, bf16[192,384]{1,0:T(8,128)(2,1)S(1)}, u32[]{:S(2)}, u32[]{:S(2)}) collective-permute-start(bf16[192,384]{1,0:T(8,128)(2,1)S(1)} %get-tuple-element.210.own), channel_id=1, source_target_pairs={{0,16},{2,18},{4,20},{6,22},{8,24},{10,26},{12,28},{14,30},{16,0},... | collective-permute-start | bytes 442376 | tf_op jit(solution)/shard_map/ppermute | solution.py:740
  85.1 8.1 %collective-permute-start.32 = (bf16[144,384]{1,0:T(8,128)(2,1)S(1)}, bf16[144,384]{1,0:T(8,128)(2,1)S(1)}, u32[]{:S(2)}, u32[]{:S(2)}) collective-permute-start(bf16[144,384]{1,0:T(8,128)(2,1)S(1)} %get-tuple-element.211), channel_id=1, source_target_pairs={{0,24},{2,26},{4,28},{6,30},{8,16},{10,18},{12,20},{14,22},{16,8},... | collective-permute-start | bytes 331784 | tf_op jit(solution)/shard_map/ppermute | solution.py:740
  86.4 6.8 %collective-permute-start.30 = (bf16[144,384]{1,0:T(8,128)(2,1)S(1)}, bf16[144,384]{1,0:T(8,128)(2,1)S(1)}, u32[]{:S(2)}, u32[]{:S(2)}) collective-permute-start(bf16[144,384]{1,0:T(8,128)(2,1)S(1)} %get-tuple-element.211), channel_id=1, source_target_pairs={{0,8},{2,10},{4,12},{6,14},{8,0},{10,2},{12,4},{14,6},{16,24},{18,... | collective-permute-start | bytes 331784 | tf_op jit(solution)/shard_map/ppermute | solution.py:740
  86.5 12.5 %collective-permute-start.41 = (bf16[288,384]{1,0:T(8,128)(2,1)S(1)}, bf16[288,384]{1,0:T(8,128)(2,1)S(1)}, u32[]{:S(2)}, u32[]{:S(2)}) collective-permute-start(bf16[288,384]{1,0:T(8,128)(2,1)S(1)} %slice.20), channel_id=1, source_target_pairs={{0,2},{2,0},{4,6},{6,4},{8,10},{10,8},{12,14},{14,12},{16,18},{18,... | collective-permute-start | bytes 663560 | tf_op jit(solution)/shard_map/ppermute | solution.py:737
  86.9 12.1 %collective-permute-start.42 = (bf16[288,384]{1,0:T(8,128)(2,1)S(1)}, bf16[288,384]{1,0:T(8,128)(2,1)S(1)}, u32[]{:S(2)}, u32[]{:S(2)}) collective-permute-start(bf16[288,384]{1,0:T(8,128)(2,1)S(1)} %slice.21), channel_id=1, source_target_pairs={{0,4},{2,6},{4,0},{6,2},{8,12},{10,14},{12,8},{14,10},{16,20},{18,... | collective-permute-start | bytes 663560 | tf_op jit(solution)/shard_map/ppermute | solution.py:737
  94.8 3.5 %collective-permute-start.38 = (f32[16,384]{1,0:T(8,128)S(1)}, f32[16,384]{1,0:T(8,128)S(1)}, u32[]{:S(2)}, u32[]{:S(2)}) collective-permute-start(f32[16,384]{1,0:T(8,128)S(1)} %get-tuple-element.222.small), channel_id=1, source_target_pairs={{0,1},{1,0},{2,3},{3,2},{4,5},{5,4},{6,7},{7,6},{8,9},{9,8},{10,11... | collective-permute-start | bytes 73736 | tf_op jit(solution)/shard_map/ppermute | solution.py:734
  94.9 12.6 %collective-permute-start.34 = (bf16[576,384]{1,0:T(8,128)(2,1)S(1)}, bf16[576,384]{1,0:T(8,128)(2,1)S(1)}, u32[]{:S(2)}, u32[]{:S(2)}) collective-permute-start(bf16[576,384]{1,0:T(8,128)(2,1)S(1)} %get-tuple-element.212.refs_0_), channel_id=1, source_target_pairs={{0,4},{2,6},{4,0},{6,2},{8,12},{10,14},{12,8},{14,10},{16,20},{18,... | collective-permute-start | bytes 1327112 | tf_op jit(solution)/shard_map/ppermute | solution.py:737
  95.4 13.0 %collective-permute-start.33 = (bf16[624,384]{1,0:T(8,128)(2,1)S(1)}, bf16[624,384]{1,0:T(8,128)(2,1)S(1)}, u32[]{:S(2)}, u32[]{:S(2)}) collective-permute-start(bf16[624,384]{1,0:T(8,128)(2,1)S(1)} %get-tuple-element.216), channel_id=1, source_target_pairs={{0,2},{2,0},{4,6},{6,4},{8,10},{10,8},{12,14},{14,12},{16,18},{18,... | collective-permute-start | bytes 1437704 | tf_op jit(solution)/shard_map/ppermute | solution.py:737
  108.5 6.7 %collective-permute-start.45 = (bf16[288,384]{1,0:T(8,128)(2,1)S(1)}, bf16[288,384]{1,0:T(8,128)(2,1)S(1)}, u32[]{:S(2)}, u32[]{:S(2)}) collective-permute-start(bf16[288,384]{1,0:T(8,128)(2,1)S(1)} %slice.19), channel_id=1, source_target_pairs={{0,4},{2,6},{4,0},{6,2},{8,12},{10,14},{12,8},{14,10},{16,20},{18,... | collective-permute-start | bytes 663560 | tf_op jit(solution)/shard_map/ppermute | solution.py:737
  110.2 6.4 %collective-permute-start.44 = (bf16[288,384]{1,0:T(8,128)(2,1)S(1)}, bf16[288,384]{1,0:T(8,128)(2,1)S(1)}, u32[]{:S(2)}, u32[]{:S(2)}) collective-permute-start(bf16[288,384]{1,0:T(8,128)(2,1)S(1)} %slice.18), channel_id=1, source_target_pairs={{0,2},{2,0},{4,6},{6,4},{8,10},{10,8},{12,14},{14,12},{16,18},{18,... | collective-permute-start | bytes 663560 | tf_op jit(solution)/shard_map/ppermute | solution.py:737
  110.6 2.1 %collective-permute-start.43 = (f32[48,384]{1,0:T(8,128)S(1)}, f32[48,384]{1,0:T(8,128)S(1)}, u32[]{:S(2)}, u32[]{:S(2)}) collective-permute-start(f32[48,384]{1,0:T(8,128)S(1)} %convert_add_fusion), channel_id=1, source_target_pairs={{0,1},{1,0},{2,3},{3,2},{4,5},{5,4},{6,7},{7,6},{8,9},{9,8},{10,11... | collective-permute-start | bytes 221192 | tf_op jit(solution)/shard_map/ppermute | solution.py:734
where the time goes:
time: 118 us
  starting transfers between devices  42 us (36%)
  Pallas kernels  41.7 us (35%)
  waiting for transfers between devices  32.8 us (28%)
    pallas_call x23, Pallas kernels, call(): pl.pallas_call(kernel, out_shape=[jax.ShapeDtypeStruct(shape, kind) for s...  41.7 us
    ppermute x18, starting transfers between devices, inner_move(): return lax.ppermute(part, 'dp', [(s, s ^ step) for s in range(dp_count)])  20.5 us
    ppermute x12, starting transfers between devices, outer_move(): lax.ppermute(part, 'dp', [(s, s ^ step * INNER) for s in range(dp_count)])  17.5 us
    ppermute x18, waiting for transfers between devices, inner_move(): return lax.ppermute(part, 'dp', [(s, s ^ step) for s in range(dp_count)])  15.7 us
    ppermute x12, waiting for transfers between devices, outer_move(): lax.ppermute(part, 'dp', [(s, s ^ step * INNER) for s in range(dp_count)])  15.1 us
    ppermute x16, starting transfers between devices, swap(): return lax.ppermute(part, 'mp', [(0, 1), (1, 0)])  4.04 us
  transfers between devices with their start and end apart: 46, of which 14 were waited for; matrix products, arithmetic and copies ran while one was open for 0% of the time, Pallas kernels for 35%

commit v1 on v0

--- a/solution.py
+++ b/solution.py
@@ -111,16 +111,27 @@
     return windows
 
 
-def split_heads(block, pair, window):
-    low, high = window
-    part = block[:, low:high]
-    column = low + lax.broadcasted_iota(jnp.int32, (16, high - low), 1)
-    sides = []
-    for head in (2 * pair, 2 * pair + 1):
-        inside = (column >= head * HDIM) & (column < (head + 1) * HDIM)
-        mask = jnp.where(inside, 1.0, 0.0).astype(BF16)
-        sides.append(part * jnp.concatenate([mask] * (block.shape[0] // 16), axis=0))
-    return jnp.concatenate(sides, axis=0)
+def head_masks(windows):
+    masks = []
+    for pair, (low, high) in enumerate(windows):
+        column = low + lax.broadcasted_iota(jnp.int32, (16, high - low), 1)
+        masks.append(
+            [
+                jnp.where(
+                    (column >= head * HDIM) & (column < (head + 1) * HDIM), 1.0, 0.0
+                ).astype(BF16)
+                for head in (2 * pair, 2 * pair + 1)
+            ]
+        )
+    return masks
+
+
+def split_heads(block, masks, window):
+    part = block[:, window[0] : window[1]]
+    tiles = block.shape[0] // 16
+    return jnp.concatenate(
+        [part * jnp.concatenate([mask] * tiles, axis=0) for mask in masks], axis=0
+    )
 
 
 def embed_rows(feats, lap, ends, w_ident, types, gain, shift, at, count):
@@ -204,6 +215,7 @@
     mols = rows // SEQ
     pairs = width // (2 * HDIM)
     windows = head_windows(width)
+    masks = head_masks(windows)
     core = places()[0]
     copies = copy_in(
         (nodes_in, edges_in, bias_u_own_in, bias_o_in, gain_in, shift_in),
@@ -224,7 +236,7 @@
         place = core * mols + m
         key_keep = positions(SEQ) < nodes[place] + edges[place]
         low, high = windows[pair]
-        both = split_heads(sides[side][0][at, :], pair, windows[pair])
+        both = split_heads(sides[side][0][at, :], masks[pair], windows[pair])
         scores = dot_nt(sides[side][1][at, low:high], both)
         scores = jnp.where(key_keep, scores, -1e30)
         top = jnp.max(scores, axis=0, keepdims=True)
@@ -376,6 +388,7 @@
     rows, width = q_own.shape
     pairs = width // (2 * HDIM)
     windows = head_windows(width)
+    masks = head_masks(windows)
     sides = (
         (q_own, k_own, v_own, ga_own, keep_out),
         (q_got, k_got, v_got, ga_got, send_out),
@@ -386,7 +399,7 @@
         m, side = unit
         at = slice(m * SEQ, (m + 1) * SEQ)
         low, high = windows[pair]
-        both_g = split_heads(sides[side][3][at, :], pair, windows[pair])
+        both_g = split_heads(sides[side][3][at, :], masks[pair], windows[pair])
         probs_low = probs_all[m, side * pairs + pair]
         probs = probs_low.astype(F32)
         grad_probs = dot_nt(sides[side][2][at, low:high], both_g)
@@ -398,7 +411,7 @@
         m, side = unit
         low, high = windows[pair]
         grad_scores = slopes[side, pair]
-        both_q = split_heads(sides[side][0][m * SEQ : (m + 1) * SEQ, :], pair, windows[pair])
+        both_q = split_heads(sides[side][0][m * SEQ : (m + 1) * SEQ, :], masks[pair], windows[pair])
         dk[side, :, low:high] += dot(grad_scores, both_q)
         first = pair * 2 * HDIM
         out = dot(keys_t[first : first + 2 * HDIM], grad_scores)

time: 118 us -> 118 us (level)
  no operation moved by 1% of the time
where the time goes in v1:
time: 118 us
  starting transfers between devices  42 us (36%)
  Pallas kernels  41.7 us (35%)
  waiting for transfers between devices  32.8 us (28%)
    pallas_call x23, Pallas kernels, call(): pl.pallas_call(kernel, out_shape=[jax.ShapeDtypeStruct(shape, kind) for s...  41.7 us
    ppermute x18, starting transfers between devices, inner_move(): return lax.ppermute(part, 'dp', [(s, s ^ step) for s in range(dp_count)])  20.5 us
    ppermute x12, starting transfers between devices, outer_move(): lax.ppermute(part, 'dp', [(s, s ^ step * INNER) for s in range(dp_count)])  17.5 us
    ppermute x18, waiting for transfers between devices, inner_move(): return lax.ppermute(part, 'dp', [(s, s ^ step) for s in range(dp_count)])  15.7 us
    ppermute x12, waiting for transfers between devices, outer_move(): lax.ppermute(part, 'dp', [(s, s ^ step * INNER) for s in range(dp_count)])  15.1 us
    ppermute x16, starting transfers between devices, swap(): return lax.ppermute(part, 'mp', [(0, 1), (1, 0)])  4.05 us
  transfers between devices with their start and end apart: 46, of which 14 were waited for; matrix products, arithmetic and copies ran while one was open for 0% of the time, Pallas kernels for 35%

profile of v1, /device:TPU:0, one launch (start us, length us, event | category | flops | bytes accessed | tf_op | source)
XLA Modules:
  0.0 117.7 jit_solution(13680019115761552424)
XLA Ops:
  0.7 0.5 collective-permute-start
  1.3 0.4 collective-permute-start.6
  1.8 0.4 collective-permute-start.1
  2.2 0.8 collective-permute-done.5
  3.0 0.4 collective-permute-start.2
  3.5 0.4 collective-permute-start.4
  3.9 4.2 %shard_map.366 = (f32[384,768]{1,0:T(8,128)S(1)}, bf16[32,384]{1,0:T(8,128)(2,1)S(1)}, bf16[384,768]{1,0:T(8,128)(2,1)S(1)}, bf16[768,384]{1,0:T(8,128)(2,1)S(1)...) custom-call(bf16[768,768]{1,0:T(8,128)(2,1)} %refs_10_.1, ...), custom_call_target="tpu_custom_call" | custom-call | tf_op jit(solution)/shard_map/pallas_call | solution.py:91
  8.4 7.3 %shard_map.367 = (bf16[384,384]{1,0:T(8,128)(2,1)S(1)}, bf16[384,384]{1,0:T(8,128)(2,1)S(1)}, bf16[384,384]{1,0:T(8,128)(2,1)S(1)}, bf16[3,16,128,256]{3,2,1,0:T...) custom-call(f32[384,768]{1,0:T(8,128)S(1)} %get-tuple-element.135.hi, ...), custom_call_target="tpu_custom_call" | custom-call | tf_op jit(solution)/shard_map/pallas_call | solution.py:91
  15.6 0.4 collective-permute-start.9
  16.1 2.9 %shard_map.368 = (bf16[1168,384]{1,0:T(8,128)(2,1)S(1)}, bf16[1168,384]{1,0:T(8,128)(2,1)S(1)}, f32[384,768]{1,0:T(8,128)S(1)}, bf16[384,768]{1,0:T(8,128)(2,1)S(1)}) custom-call(f32[384,768]{1,0:T(8,128)S(1)} %get-tuple-element.140.middle, f32[384,768]{1,0:T(8,128)S(1)} %get-tuple-element.145.slope, bf16[768,384]{1,0:T(8,128)(2,1)S(1)} %copy-done.1, ...), custom_call_target="tpu_custom_call" | custom-call | tf_op jit(solution)/shard_map/pallas_call | solution.py:91
  19.2 1.2 %shard_map.369 = (bf16[192,384]{1,0:T(8,128)(2,1)S(1)}, bf16[192,384]{1,0:T(8,128)(2,1)S(1)}, bf16[192,384]{1,0:T(8,128)(2,1)S(1)}, bf16[192,384]{1,0:T(8,128)(2,1)S(1)}) custom-call(bf16[1536,384]{1,0:T(8,128)(2,1)S(1)} %get-tuple-element.151.kept, bf16[1536,384]{1,0:T(8,128)(2,1)S(1)} %collective-permute-done.9.got, bf16[768,768]{1,0:T(8,128)(2,1)S(1)} %copy-done, ...), custom_call_target="tpu_custom_call" | custom-call | tf_op jit(solution)/shard_map/pallas_call | solution.py:91
  20.4 2.9 %collective-permute-start.13 = (bf16[192,384]{1,0:T(8,128)(2,1)S(1)}, bf16[192,384]{1,0:T(8,128)(2,1)S(1)}, u32[]{:S(2)}, u32[]{:S(2)}) collective-permute-start(bf16[192,384]{1,0:T(8,128)(2,1)S(1)} %get-tuple-element.158), channel_id=1, source_target_pairs={{0,4},{2,6},{4,0},{6,2},{8,12},{10,14},{12,8},{14,10},{16,20},{18,... | collective-permute-start | bytes 442376 | tf_op jit(solution)/shard_map/ppermute | solution.py:750
  23.4 1.5 %collective-permute-start.12 = (bf16[192,384]{1,0:T(8,128)(2,1)S(1)}, bf16[192,384]{1,0:T(8,128)(2,1)S(1)}, u32[]{:S(2)}, u32[]{:S(2)}) collective-permute-start(bf16[192,384]{1,0:T(8,128)(2,1)S(1)} %get-tuple-element.156), channel_id=1, source_target_pairs={{0,2},{2,0},{4,6},{6,4},{8,10},{10,8},{12,14},{14,12},{16,18},{18,... | collective-permute-start | bytes 442376 | tf_op jit(solution)/shard_map/ppermute | solution.py:750
  24.9 1.9 %shard_map.370 = (bf16[400,384]{1,0:T(8,128)(2,1)S(1)}, bf16[400,384]{1,0:T(8,128)(2,1)S(1)}, bf16[384,384]{1,0:T(8,128)(2,1)S(1)}, bf16[384,384]{1,0:T(8,128)(2,1)S(1)}) custom-call(bf16[1536,384]{1,0:T(8,128)(2,1)S(1)} %get-tuple-element.151.kept, bf16[1536,384]{1,0:T(8,128)(2,1)S(1)} %collective-permute-done.9.got, ...), custom_call_target="tpu_custom_call" | custom-call | tf_op jit(solution)/shard_map/pallas_call | solution.py:91
  26.7 0.6 collective-permute-start.11
  27.3 0.3 collective-permute-start.14
  27.6 1.3 %collective-permute-done.12.refs_1_ = bf16[192,384]{1,0:T(8,128)(2,1)S(1)} collective-permute-done((bf16[192,384]{1,0:T(8,128)(2,1)S(1)}, bf16[192,384]{1,0:T(8,128)(2,1)S(1)}, u32[]{:S(2)}, u32[]{:S(2)}) %collective-permute-start.12) | collective-permute-done | bytes 147488 | tf_op jit(solution)/shard_map/ppermute | solution.py:750
  29.0 0.8 shard_map.371
  29.8 4.2 %shard_map.372 = (bf16[1152,384]{1,0:T(8,128)(2,1)S(1)}, bf16[1152,384]{1,0:T(8,128)(2,1)S(1)}) custom-call(bf16[384,384]{1,0:T(8,128)(2,1)S(1)} %get-tuple-element.137.q_own, bf16[384,384]{1,0:T(8,128)(2,1)S(1)} %get-tuple-element.138.k_own, bf16[384,384]{1,0:T(8,128)(2,1)S(1)} %get-tuple-element.139.v_own, bf16[384,384]{1,0:T(8,128)(2,1)S(1)} %get-tuple-element.161.ga_own, ...), custom_call_target="tpu_custom_call" | custom-call | tf_op jit(solution)/shard_map/pallas_call | solution.py:91
  34.1 0.5 collective-permute-start.15
  34.6 1.0 collective-permute-done.14.second_got
  35.8 1.1 collective-permute-start.19
  36.9 0.9 collective-permute-start.20
  37.8 2.2 %shard_map.374 = (bf16[576,384]{1,0:T(8,128)(2,1)S(1)}, bf16[576,384]{1,0:T(8,128)(2,1)S(1)}, bf16[576,384]{1,0:T(8,128)(2,1)S(1)}, bf16[576,384]{1,0:T(8,128)(2,1)S(1)}, f32[48,384]{1,0:T(8,128)S(1)}) custom-call(bf16[768,384]{1,0:T(8,128)(2,1)S(1)} %get-tuple-element.178.normed_t, bf16[768,384]{1,0:T(8,128)(2,1)S(1)} %collective-permute-done.15.normed_t_got, ...), custom_call_target="tpu_custom_call" | custom-call | tf_op jit(solution)/shard_map/pallas_call | solution.py:91
  40.1 1.9 %collective-permute-start.17 = (bf16[576,384]{1,0:T(8,128)(2,1)S(1)}, bf16[576,384]{1,0:T(8,128)(2,1)S(1)}, u32[]{:S(2)}, u32[]{:S(2)}) collective-permute-start(bf16[576,384]{1,0:T(8,128)(2,1)S(1)} %get-tuple-element.181), channel_id=1, source_target_pairs={{0,2},{2,0},{4,6},{6,4},{8,10},{10,8},{12,14},{14,12},{16,18},{18,... | collective-permute-start | bytes 1327112 | tf_op jit(solution)/shard_map/ppermute | solution.py:750
  42.2 1.1 collective-permute-done.20.second_got
  43.4 1.3 %collective-permute-start.23 = (bf16[160,384]{1,0:T(8,128)(2,1)S(1)}, bf16[160,384]{1,0:T(8,128)(2,1)S(1)}, u32[]{:S(2)}, u32[]{:S(2)}) collective-permute-start(bf16[160,384]{1,0:T(8,128)(2,1)S(1)} %get-tuple-element.189.near), channel_id=1, source_target_pairs={{0,8},{2,10},{4,12},{6,14},{8,0},{10,2},{12,4},{14,6},{16,24},{18,... | collective-permute-start | bytes 368648 | tf_op jit(solution)/shard_map/ppermute | solution.py:753
  44.8 2.5 %collective-permute-start.25 = (bf16[144,384]{1,0:T(8,128)(2,1)S(1)}, bf16[144,384]{1,0:T(8,128)(2,1)S(1)}, u32[]{:S(2)}, u32[]{:S(2)}) collective-permute-start(bf16[144,384]{1,0:T(8,128)(2,1)S(1)} %get-tuple-element.191), channel_id=1, source_target_pairs={{0,24},{2,26},{4,28},{6,30},{8,16},{10,18},{12,20},{14,22},{16,8},... | collective-permute-start | bytes 331784 | tf_op jit(solution)/shard_map/ppermute | solution.py:753
  47.4 6.6 %shard_map.376 = (f32[384,768]{1,0:T(8,128)}, f32[48,384]{1,0:T(8,128)S(1)}, bf16[48,384]{1,0:T(8,128)(2,1)S(1)}) custom-call(bf16[1152,384]{1,0:T(8,128)(2,1)S(1)} %get-tuple-element.167.kept.refs_0_, bf16[1152,384]{1,0:T(8,128)(2,1)S(1)} %get-tuple-element.179.refs_1_, bf16[768,384]{1,0:T(8,128)(2,1)S(1)} %copy-done.2, bf16[768,384]{1,0:T(8,128)(2,1)S(1)} %copy-done.3, ...), custom_call_target="tpu_custom_call" | custom-call | tf_op jit(solution)/shard_map/pallas_call | solution.py:91
  54.1 1.2 %collective-permute-done.21.refs_1_ = bf16[48,384]{1,0:T(8,128)(2,1)S(1)} collective-permute-done((bf16[48,384]{1,0:T(8,128)(2,1)S(1)}, bf16[48,384]{1,0:T(8,128)(2,1)S(1)}, u32[]{:S(2)}, u32[]{:S(2)}) %collective-permute-start.21) | collective-permute-done | bytes 36896 | tf_op jit(solution)/shard_map/ppermute | solution.py:747
  55.3 0.2 shard_map.377
  55.5 2.0 %collective-permute-start.26 = (bf16[288,384]{1,0:T(8,128)(2,1)S(1)}, bf16[288,384]{1,0:T(8,128)(2,1)S(1)}, u32[]{:S(2)}, u32[]{:S(2)}) collective-permute-start(bf16[288,384]{1,0:T(8,128)(2,1)S(1)} %get-tuple-element.199), channel_id=1, source_target_pairs={{0,2},{2,0},{4,6},{6,4},{8,10},{10,8},{12,14},{14,12},{16,18},{18,... | collective-permute-start | bytes 663560 | tf_op jit(solution)/shard_map/ppermute | solution.py:750
  57.5 2.7 %collective-permute-start.22 = (bf16[336,384]{1,0:T(8,128)(2,1)S(1)}, bf16[336,384]{1,0:T(8,128)(2,1)S(1)}, u32[]{:S(2)}, u32[]{:S(2)}) collective-permute-start(bf16[336,384]{1,0:T(8,128)(2,1)S(1)} %get-tuple-element.197), channel_id=1, source_target_pairs={{0,4},{2,6},{4,0},{6,2},{8,12},{10,14},{12,8},{14,10},{16,20},{18,... | collective-permute-start | bytes 774152 | tf_op jit(solution)/shard_map/ppermute | solution.py:750
  60.3 3.0 %collective-permute-start.37 = (bf16[144,384]{1,0:T(8,128)(2,1)S(1)}, bf16[144,384]{1,0:T(8,128)(2,1)S(1)}, u32[]{:S(2)}, u32[]{:S(2)}) collective-permute-start(bf16[144,384]{1,0:T(8,128)(2,1)S(1)} %get-tuple-element.203), channel_id=1, source_target_pairs={{0,24},{2,26},{4,28},{6,30},{8,16},{10,18},{12,20},{14,22},{16,8},... | collective-permute-start | bytes 331784 | tf_op jit(solution)/shard_map/ppermute | solution.py:753
  63.3 0.3 collective-permute-start.36
  63.7 1.1 collective-permute-start.35
  64.8 1.7 %collective-permute-done.22.first_got = bf16[336,384]{1,0:T(8,128)(2,1)S(1)} collective-permute-done((bf16[336,384]{1,0:T(8,128)(2,1)S(1)}, bf16[336,384]{1,0:T(8,128)(2,1)S(1)}, u32[]{:S(2)}, u32[]{:S(2)}) %collective-permute-start.22) | collective-permute-done | bytes 258080 | tf_op jit(solution)/shard_map/ppermute | solution.py:750
  66.6 1.9 %collective-permute-start.27 = (bf16[192,384]{1,0:T(8,128)(2,1)S(1)}, bf16[192,384]{1,0:T(8,128)(2,1)S(1)}, u32[]{:S(2)}, u32[]{:S(2)}) collective-permute-start(bf16[192,384]{1,0:T(8,128)(2,1)S(1)} %get-tuple-element.207.near), channel_id=1, source_target_pairs={{0,8},{2,10},{4,12},{6,14},{8,0},{10,2},{12,4},{14,6},{16,24},{18,... | collective-permute-start | bytes 442376 | tf_op jit(solution)/shard_map/ppermute | solution.py:753
  68.5 1.7 %collective-permute-start.28 = (bf16[144,384]{1,0:T(8,128)(2,1)S(1)}, bf16[144,384]{1,0:T(8,128)(2,1)S(1)}, u32[]{:S(2)}, u32[]{:S(2)}) collective-permute-start(bf16[144,384]{1,0:T(8,128)(2,1)S(1)} %get-tuple-element.208), channel_id=1, source_target_pairs={{0,16},{2,18},{4,20},{6,22},{8,24},{10,26},{12,28},{14,30},{16,0},... | collective-permute-start | bytes 331784 | tf_op jit(solution)/shard_map/ppermute | solution.py:753
  70.2 0.9 collective-permute-start.29
  71.1 3.9 %collective-permute-done.36.middle = bf16[160,384]{1,0:T(8,128)(2,1)S(1)} collective-permute-done((bf16[160,384]{1,0:T(8,128)(2,1)S(1)}, bf16[160,384]{1,0:T(8,128)(2,1)S(1)}, u32[]{:S(2)}, u32[]{:S(2)}) %collective-permute-start.36) | collective-permute-done | bytes 122912 | tf_op jit(solution)/shard_map/ppermute | solution.py:753
  75.0 0.8 shard_map.383
  75.8 1.4 %collective-permute-start.40 = (bf16[576,384]{1,0:T(8,128)(2,1)S(1)}, bf16[576,384]{1,0:T(8,128)(2,1)S(1)}, u32[]{:S(2)}, u32[]{:S(2)}) collective-permute-start(bf16[576,384]{1,0:T(8,128)(2,1)S(1)} %get-tuple-element.228.refs_0_), channel_id=1, source_target_pairs={{0,4},{2,6},{4,0},{6,2},{8,12},{10,14},{12,8},{14,10},{16,20},{18,... | collective-permute-start | bytes 1327112 | tf_op jit(solution)/shard_map/ppermute | solution.py:750
  77.2 4.5 %collective-permute-done.28.middle_got = bf16[144,384]{1,0:T(8,128)(2,1)S(1)} collective-permute-done((bf16[144,384]{1,0:T(8,128)(2,1)S(1)}, bf16[144,384]{1,0:T(8,128)(2,1)S(1)}, u32[]{:S(2)}, u32[]{:S(2)}) %collective-permute-start.28) | collective-permute-done | bytes 110624 | tf_op jit(solution)/shard_map/ppermute | solution.py:753
  81.8 3.3 %collective-permute-start.31 = (bf16[192,384]{1,0:T(8,128)(2,1)S(1)}, bf16[192,384]{1,0:T(8,128)(2,1)S(1)}, u32[]{:S(2)}, u32[]{:S(2)}) collective-permute-start(bf16[192,384]{1,0:T(8,128)(2,1)S(1)} %get-tuple-element.210.own), channel_id=1, source_target_pairs={{0,16},{2,18},{4,20},{6,22},{8,24},{10,26},{12,28},{14,30},{16,0},... | collective-permute-start | bytes 442376 | tf_op jit(solution)/shard_map/ppermute | solution.py:753
  85.0 1.4 %collective-permute-start.32 = (bf16[144,384]{1,0:T(8,128)(2,1)S(1)}, bf16[144,384]{1,0:T(8,128)(2,1)S(1)}, u32[]{:S(2)}, u32[]{:S(2)}) collective-permute-start(bf16[144,384]{1,0:T(8,128)(2,1)S(1)} %get-tuple-element.211), channel_id=1, source_target_pairs={{0,24},{2,26},{4,28},{6,30},{8,16},{10,18},{12,20},{14,22},{16,8},... | collective-permute-start | bytes 331784 | tf_op jit(solution)/shard_map/ppermute | solution.py:753
  86.5 0.4 collective-permute-start.41
  86.9 1.1 collective-permute-start.42
  88.0 5.1 %collective-permute-done.32.far = bf16[144,384]{1,0:T(8,128)(2,1)S(1)} collective-permute-done((bf16[144,384]{1,0:T(8,128)(2,1)S(1)}, bf16[144,384]{1,0:T(8,128)(2,1)S(1)}, u32[]{:S(2)}, u32[]{:S(2)}) %collective-permute-start.32) | collective-permute-done | bytes 110624 | tf_op jit(solution)/shard_map/ppermute | solution.py:753
  93.2 1.6 %collective-permute-done.31.middle = bf16[192,384]{1,0:T(8,128)(2,1)S(1)} collective-permute-done((bf16[192,384]{1,0:T(8,128)(2,1)S(1)}, bf16[192,384]{1,0:T(8,128)(2,1)S(1)}, u32[]{:S(2)}, u32[]{:S(2)}) %collective-permute-start.31) | collective-permute-done | bytes 147488 | tf_op jit(solution)/shard_map/ppermute | solution.py:753
  94.9 0.5 collective-permute-start.34
  95.4 0.7 collective-permute-start.33
  96.0 2.3 %shard_map.382 = bf16[384,768]{1,0:T(8,128)(2,1)} custom-call(f32[384,768]{1,0:T(8,128)S(1)} %get-tuple-element.140.middle, bf16[384,768]{1,0:T(8,128)(2,1)S(1)} %get-tuple-element.141.active, bf16[384,768]{1,0:T(8,128)(2,1)S(1)} %copy-done.5, bf16[384,768]{1,0:T(8,128)(2,1)S(1)} %collective-permute-done.8.wd, bf16[6,128]{1,0:T(8,128)(2,1)} %bitcast.35), custom_call_target="tpu_custom_call" | custom-call | tf_op jit(solution)/shard_map/pallas_call | solution.py:91
  98.3 0.6 shard_map.384
  99.0 2.1 %shard_map.385 = (f32[768,384]{1,0:T(8,128)}, f32[384,768]{1,0:T(8,128)}, f32[384,768]{1,0:T(8,128)}) custom-call(bf16[576,384]{1,0:T(8,128)(2,1)S(1)} %get-tuple-element.228.refs_0_, bf16[576,384]{1,0:T(8,128)(2,1)S(1)} %collective-permute-done.39.refs_1_, bf16[576,384]{1,0:T(8,128)(2,1)S(1)} %collective-permute-done.40.refs_2_, ...), custom_call_target="tpu_custom_call" | custom-call | flops 10000000000 | tf_op jit(solution)/shard_map/pallas_call | solution.py:91
  101.0 6.4 %collective-permute-done.34.refs_2_ = bf16[576,384]{1,0:T(8,128)(2,1)S(1)} collective-permute-done((bf16[576,384]{1,0:T(8,128)(2,1)S(1)}, bf16[576,384]{1,0:T(8,128)(2,1)S(1)}, u32[]{:S(2)}, u32[]{:S(2)}) %collective-permute-start.34) | collective-permute-done | bytes 442400 | tf_op jit(solution)/shard_map/ppermute | solution.py:750
  107.5 0.9 collective-permute-done.33.refs_1_
  108.4 1.7 %collective-permute-start.45 = (bf16[288,384]{1,0:T(8,128)(2,1)S(1)}, bf16[288,384]{1,0:T(8,128)(2,1)S(1)}, u32[]{:S(2)}, u32[]{:S(2)}) collective-permute-start(bf16[288,384]{1,0:T(8,128)(2,1)S(1)} %slice.19), channel_id=1, source_target_pairs={{0,4},{2,6},{4,0},{6,2},{8,12},{10,14},{12,8},{14,10},{16,20},{18,... | collective-permute-start | bytes 663560 | tf_op jit(solution)/shard_map/ppermute | solution.py:750
  110.1 0.5 collective-permute-start.44
  110.7 2.0 %shard_map.387 = (f32[768,384]{1,0:T(8,128)}, f32[768,384]{1,0:T(8,128)}, f32[768,384]{1,0:T(8,128)}) custom-call(bf16[576,384]{1,0:T(8,128)(2,1)S(1)} %get-tuple-element.212.refs_0_, bf16[624,384]{1,0:T(8,128)(2,1)S(1)} %collective-permute-done.33.refs_1_, bf16[576,384]{1,0:T(8,128)(2,1)S(1)} %collective-permute-done.34.refs_2_), custom_call_target="tpu_custom_call" | custom-call | tf_op jit(solution)/shard_map/pallas_call | solution.py:91
  112.7 0.7 shard_map.386
  113.4 1.8 %collective-permute-done.45.second = bf16[288,384]{1,0:T(8,128)(2,1)S(1)} collective-permute-done((bf16[288,384]{1,0:T(8,128)(2,1)S(1)}, bf16[288,384]{1,0:T(8,128)(2,1)S(1)}, u32[]{:S(2)}, u32[]{:S(2)}) %collective-permute-start.45) | collective-permute-done | bytes 221216 | tf_op jit(solution)/shard_map/ppermute | solution.py:750
  115.2 1.3 %collective-permute-done.44.first = bf16[288,384]{1,0:T(8,128)(2,1)S(1)} collective-permute-done((bf16[288,384]{1,0:T(8,128)(2,1)S(1)}, bf16[288,384]{1,0:T(8,128)(2,1)S(1)}, u32[]{:S(2)}, u32[]{:S(2)}) %collective-permute-start.44) | collective-permute-done | bytes 221216 | tf_op jit(solution)/shard_map/ppermute | solution.py:750
  116.5 1.0 shard_map.388
  (71 shorter events, 2.2 us)
Async XLA Ops:
  0.7 7.4 %collective-permute-start = (bf16[768,384]{1,0:T(8,128)(2,1)}, bf16[768,384]{1,0:T(8,128)(2,1)S(1)}, u32[]{:S(2)}, u32[]{:S(2)}) collective-permute-start(bf16[768,384]{1,0:T(8,128)(2,1)} %refs_2_.1), channel_id=1, source_target_pairs={{0,1},{1,0},{2,3},{3,2},{4,5},{5,4},{6,7},{7,6},{8,9},{9,8},{10,11... | collective-permute-start | bytes 1769480 | tf_op jit(solution)/shard_map/ppermute | solution.py:747
  1.2 1.8 %collective-permute-start.5 = (bf16[384]{0:T(512)(128)(2,1)}, bf16[384]{0:T(512)(128)(2,1)S(1)}, u32[]{:S(2)}, u32[]{:S(2)}) collective-permute-start(bf16[384]{0:T(512)(128)(2,1)} %param.35), channel_id=1, source_target_pairs={{0,1},{1,0},{2,3},{3,2},{4,5},{5,4},{6,7},{7,6},{8,9},{9,8},{10,11... | collective-permute-start | bytes 2312 | tf_op jit(solution)/shard_map/ppermute | solution.py:747
  1.3 2.1 %collective-permute-start.6 = (bf16[384]{0:T(512)(128)(2,1)}, bf16[384]{0:T(512)(128)(2,1)S(1)}, u32[]{:S(2)}, u32[]{:S(2)}) collective-permute-start(bf16[384]{0:T(512)(128)(2,1)} %param.36), channel_id=1, source_target_pairs={{0,1},{1,0},{2,3},{3,2},{4,5},{5,4},{6,7},{7,6},{8,9},{9,8},{10,11... | collective-permute-start | bytes 2312 | tf_op jit(solution)/shard_map/ppermute | solution.py:747
  1.7 1.8 %collective-permute-start.7 = (bf16[384]{0:T(512)(128)(2,1)}, bf16[384]{0:T(512)(128)(2,1)S(1)}, u32[]{:S(2)}, u32[]{:S(2)}) collective-permute-start(bf16[384]{0:T(512)(128)(2,1)} %param.42), channel_id=1, source_target_pairs={{0,1},{1,0},{2,3},{3,2},{4,5},{5,4},{6,7},{7,6},{8,9},{9,8},{10,11... | collective-permute-start | bytes 2312 | tf_op jit(solution)/shard_map/ppermute | solution.py:747
  1.8 6.5 %collective-permute-start.1 = (bf16[768,384]{1,0:T(8,128)(2,1)}, bf16[768,384]{1,0:T(8,128)(2,1)S(1)}, u32[]{:S(2)}, u32[]{:S(2)}) collective-permute-start(bf16[768,384]{1,0:T(8,128)(2,1)} %refs_3_.1), channel_id=1, source_target_pairs={{0,1},{1,0},{2,3},{3,2},{4,5},{5,4},{6,7},{7,6},{8,9},{9,8},{10,11... | collective-permute-start | bytes 1769480 | tf_op jit(solution)/shard_map/ppermute | solution.py:747
  3.0 5.3 %collective-permute-start.2 = (bf16[768,384]{1,0:T(8,128)(2,1)}, bf16[768,384]{1,0:T(8,128)(2,1)S(1)}, u32[]{:S(2)}, u32[]{:S(2)}) collective-permute-start(bf16[768,384]{1,0:T(8,128)(2,1)} %refs_4_.1), channel_id=1, source_target_pairs={{0,1},{1,0},{2,3},{3,2},{4,5},{5,4},{6,7},{7,6},{8,9},{9,8},{10,11... | collective-permute-start | bytes 1769480 | tf_op jit(solution)/shard_map/ppermute | solution.py:747
  3.4 4.9 %collective-permute-start.3 = (bf16[384,768]{1,0:T(8,128)(2,1)}, bf16[384,768]{1,0:T(8,128)(2,1)S(1)}, u32[]{:S(2)}, u32[]{:S(2)}) collective-permute-start(bf16[384,768]{1,0:T(8,128)(2,1)} %wo_own.3), channel_id=1, source_target_pairs={{0,1},{1,0},{2,3},{3,2},{4,5},{5,4},{6,7},{7,6},{8,9},{9,8},{10,11... | collective-permute-start | bytes 1769480 | tf_op jit(solution)/shard_map/ppermute | solution.py:747
  3.5 4.8 %collective-permute-start.4 = (bf16[768,384]{1,0:T(8,128)(2,1)}, bf16[768,384]{1,0:T(8,128)(2,1)S(1)}, u32[]{:S(2)}, u32[]{:S(2)}) collective-permute-start(bf16[768,384]{1,0:T(8,128)(2,1)} %wu_own.3), channel_id=1, source_target_pairs={{0,1},{1,0},{2,3},{3,2},{4,5},{5,4},{6,7},{7,6},{8,9},{9,8},{10,11... | collective-permute-start | bytes 1769480 | tf_op jit(solution)/shard_map/ppermute | solution.py:747
  3.9 4.2 %copy-start.5 = (bf16[384,768]{1,0:T(8,128)(2,1)S(1)}, bf16[384,768]{1,0:T(8,128)(2,1)}, u32[]{:S(2)}) copy-start(bf16[384,768]{1,0:T(8,128)(2,1)} %wd_own.3) | copy-start | bytes 1769476
  3.9 4.4 %copy-start.1 = (bf16[768,384]{1,0:T(8,128)(2,1)S(1)}, bf16[768,384]{1,0:T(8,128)(2,1)}, u32[]{:S(2)}) copy-start(bf16[768,384]{1,0:T(8,128)(2,1)} %wu_own.3) | copy-start | bytes 1769476
  3.9 4.4 %copy-start.6 = (bf16[384,768]{1,0:T(8,128)(2,1)S(1)}, bf16[384,768]{1,0:T(8,128)(2,1)}, u32[]{:S(2)}) copy-start(bf16[384,768]{1,0:T(8,128)(2,1)} %wo_own.3) | copy-start | bytes 1769476
  8.1 8.0 %collective-permute-start.8 = (bf16[384,768]{1,0:T(8,128)(2,1)S(1)}, bf16[384,768]{1,0:T(8,128)(2,1)S(1)}, u32[]{:S(2)}, u32[]{:S(2)}) collective-permute-start(bf16[384,768]{1,0:T(8,128)(2,1)S(1)} %copy-done.5), channel_id=1, source_target_pairs={{0,1},{1,0},{2,3},{3,2},{4,5},{5,4},{6,7},{7,6},{8,9},{9,8},{10,11... | collective-permute-start | bytes 1769480 | tf_op jit(solution)/shard_map/ppermute | solution.py:747
  8.4 7.7 %copy-start = (bf16[768,768]{1,0:T(8,128)(2,1)S(1)}, bf16[768,768]{1,0:T(8,128)(2,1)}, u32[]{:S(2)}) copy-start(bf16[768,768]{1,0:T(8,128)(2,1)} %cots.3) | copy-start | bytes 3538948
  15.6 3.6 %collective-permute-start.9 = (bf16[1536,384]{1,0:T(8,128)(2,1)S(1)}, bf16[1536,384]{1,0:T(8,128)(2,1)S(1)}, u32[]{:S(2)}, u32[]{:S(2)}) collective-permute-start(bf16[1536,384]{1,0:T(8,128)(2,1)S(1)} %get-tuple-element.149), channel_id=1, source_target_pairs={{0,1},{1,0},{2,3},{3,2},{4,5},{5,4},{6,7},{7,6},{8,9},{9,8},{10,11... | collective-permute-start | bytes 3538952 | tf_op jit(solution)/shard_map/ppermute | solution.py:747
  19.0 5.9 %collective-permute-start.10 = (bf16[1168,384]{1,0:T(8,128)(2,1)S(1)}, bf16[1168,384]{1,0:T(8,128)(2,1)S(1)}, u32[]{:S(2)}, u32[]{:S(2)}) collective-permute-start(bf16[1168,384]{1,0:T(8,128)(2,1)S(1)} %get-tuple-element.153), channel_id=1, source_target_pairs={{0,1},{1,0},{2,3},{3,2},{4,5},{5,4},{6,7},{7,6},{8,9},{9,8},{10,11... | collective-permute-start | bytes 2691080 | tf_op jit(solution)/shard_map/ppermute | solution.py:747
  20.4 7.2 %collective-permute-start.13 = (bf16[192,384]{1,0:T(8,128)(2,1)S(1)}, bf16[192,384]{1,0:T(8,128)(2,1)S(1)}, u32[]{:S(2)}, u32[]{:S(2)}) collective-permute-start(bf16[192,384]{1,0:T(8,128)(2,1)S(1)} %get-tuple-element.158), channel_id=1, source_target_pairs={{0,4},{2,6},{4,0},{6,2},{8,12},{10,14},{12,8},{14,10},{16,20},{18,... | collective-permute-start | bytes 442376 | tf_op jit(solution)/shard_map/ppermute | solution.py:750
  23.4 5.6 %collective-permute-start.12 = (bf16[192,384]{1,0:T(8,128)(2,1)S(1)}, bf16[192,384]{1,0:T(8,128)(2,1)S(1)}, u32[]{:S(2)}, u32[]{:S(2)}) collective-permute-start(bf16[192,384]{1,0:T(8,128)(2,1)S(1)} %get-tuple-element.156), channel_id=1, source_target_pairs={{0,2},{2,0},{4,6},{6,4},{8,10},{10,8},{12,14},{14,12},{16,18},{18,... | collective-permute-start | bytes 442376 | tf_op jit(solution)/shard_map/ppermute | solution.py:750
  26.7 8.8 %collective-permute-start.11 = (bf16[400,384]{1,0:T(8,128)(2,1)S(1)}, bf16[400,384]{1,0:T(8,128)(2,1)S(1)}, u32[]{:S(2)}, u32[]{:S(2)}) collective-permute-start(bf16[400,384]{1,0:T(8,128)(2,1)S(1)} %get-tuple-element.155), channel_id=1, source_target_pairs={{0,2},{2,0},{4,6},{6,4},{8,10},{10,8},{12,14},{14,12},{16,18},{18,... | collective-permute-start | bytes 921608 | tf_op jit(solution)/shard_map/ppermute | solution.py:750
  27.3 8.2 %collective-permute-start.14 = (bf16[384,384]{1,0:T(8,128)(2,1)S(1)}, bf16[384,384]{1,0:T(8,128)(2,1)S(1)}, u32[]{:S(2)}, u32[]{:S(2)}) collective-permute-start(bf16[384,384]{1,0:T(8,128)(2,1)S(1)} %get-tuple-element.170), channel_id=1, source_target_pairs={{0,4},{2,6},{4,0},{6,2},{8,12},{10,14},{12,8},{14,10},{16,20},{18,... | collective-permute-start | bytes 884744 | tf_op jit(solution)/shard_map/ppermute | solution.py:750
  34.0 3.9 %collective-permute-start.16 = (bf16[1152,384]{1,0:T(8,128)(2,1)S(1)}, bf16[1152,384]{1,0:T(8,128)(2,1)S(1)}, u32[]{:S(2)}, u32[]{:S(2)}) collective-permute-start(bf16[1152,384]{1,0:T(8,128)(2,1)S(1)} %get-tuple-element.179.refs_1_), channel_id=1, source_target_pairs={{0,1},{1,0},{2,3},{3,2},{4,5},{5,4},{6,7},{7,6},{8,9},{9,8},{10,11... | collective-permute-start | bytes 2654216 | tf_op jit(solution)/shard_map/ppermute | solution.py:747
  34.1 3.8 %collective-permute-start.15 = (bf16[768,384]{1,0:T(8,128)(2,1)S(1)}, bf16[768,384]{1,0:T(8,128)(2,1)S(1)}, u32[]{:S(2)}, u32[]{:S(2)}) collective-permute-start(bf16[768,384]{1,0:T(8,128)(2,1)S(1)} %get-tuple-element.178.normed_t), channel_id=1, source_target_pairs={{0,1},{1,0},{2,3},{3,2},{4,5},{5,4},{6,7},{7,6},{8,9},{9,8},{10,11... | collective-permute-start | bytes 1769480 | tf_op jit(solution)/shard_map/ppermute | solution.py:747
  35.8 7.5 %collective-permute-start.19 = (bf16[304,384]{1,0:T(8,128)(2,1)S(1)}, bf16[304,384]{1,0:T(8,128)(2,1)S(1)}, u32[]{:S(2)}, u32[]{:S(2)}) collective-permute-start(bf16[304,384]{1,0:T(8,128)(2,1)S(1)} %get-tuple-element.174), channel_id=1, source_target_pairs={{0,4},{2,6},{4,0},{6,2},{8,12},{10,14},{12,8},{14,10},{16,20},{18,... | collective-permute-start | bytes 700424 | tf_op jit(solution)/shard_map/ppermute | solution.py:750
  36.9 6.4 %collective-permute-start.20 = (bf16[288,384]{1,0:T(8,128)(2,1)S(1)}, bf16[288,384]{1,0:T(8,128)(2,1)S(1)}, u32[]{:S(2)}, u32[]{:S(2)}) collective-permute-start(bf16[288,384]{1,0:T(8,128)(2,1)S(1)} %get-tuple-element.176), channel_id=1, source_target_pairs={{0,2},{2,0},{4,6},{6,4},{8,10},{10,8},{12,14},{14,12},{16,18},{18,... | collective-permute-start | bytes 663560 | tf_op jit(solution)/shard_map/ppermute | solution.py:750
  40.1 13.9 %collective-permute-start.17 = (bf16[576,384]{1,0:T(8,128)(2,1)S(1)}, bf16[576,384]{1,0:T(8,128)(2,1)S(1)}, u32[]{:S(2)}, u32[]{:S(2)}) collective-permute-start(bf16[576,384]{1,0:T(8,128)(2,1)S(1)} %get-tuple-element.181), channel_id=1, source_target_pairs={{0,2},{2,0},{4,6},{6,4},{8,10},{10,8},{12,14},{14,12},{16,18},{18,... | collective-permute-start | bytes 1327112 | tf_op jit(solution)/shard_map/ppermute | solution.py:750
  42.0 12.0 %collective-permute-start.18 = (bf16[576,384]{1,0:T(8,128)(2,1)S(1)}, bf16[576,384]{1,0:T(8,128)(2,1)S(1)}, u32[]{:S(2)}, u32[]{:S(2)}) collective-permute-start(bf16[576,384]{1,0:T(8,128)(2,1)S(1)} %get-tuple-element.183), channel_id=1, source_target_pairs={{0,4},{2,6},{4,0},{6,2},{8,12},{10,14},{12,8},{14,10},{16,20},{18,... | collective-permute-start | bytes 1327112 | tf_op jit(solution)/shard_map/ppermute | solution.py:750
  43.3 4.1 %copy-start.2 = (bf16[768,384]{1,0:T(8,128)(2,1)S(1)}, bf16[768,384]{1,0:T(8,128)(2,1)}, u32[]{:S(2)}) copy-start(bf16[768,384]{1,0:T(8,128)(2,1)} %refs_2_.1) | copy-start | bytes 1769476
  43.3 4.1 %copy-start.3 = (bf16[768,384]{1,0:T(8,128)(2,1)S(1)}, bf16[768,384]{1,0:T(8,128)(2,1)}, u32[]{:S(2)}) copy-start(bf16[768,384]{1,0:T(8,128)(2,1)} %refs_3_.1) | copy-start | bytes 1769476
  43.3 4.1 %copy-start.4 = (bf16[768,384]{1,0:T(8,128)(2,1)S(1)}, bf16[768,384]{1,0:T(8,128)(2,1)}, u32[]{:S(2)}) copy-start(bf16[768,384]{1,0:T(8,128)(2,1)} %refs_4_.1) | copy-start | bytes 1769476
  43.4 16.8 %collective-permute-start.23 = (bf16[160,384]{1,0:T(8,128)(2,1)S(1)}, bf16[160,384]{1,0:T(8,128)(2,1)S(1)}, u32[]{:S(2)}, u32[]{:S(2)}) collective-permute-start(bf16[160,384]{1,0:T(8,128)(2,1)S(1)} %get-tuple-element.189.near), channel_id=1, source_target_pairs={{0,8},{2,10},{4,12},{6,14},{8,0},{10,2},{12,4},{14,6},{16,24},{18,... | collective-permute-start | bytes 368648 | tf_op jit(solution)/shard_map/ppermute | solution.py:753
  44.8 15.5 %collective-permute-start.25 = (bf16[144,384]{1,0:T(8,128)(2,1)S(1)}, bf16[144,384]{1,0:T(8,128)(2,1)S(1)}, u32[]{:S(2)}, u32[]{:S(2)}) collective-permute-start(bf16[144,384]{1,0:T(8,128)(2,1)S(1)} %get-tuple-element.191), channel_id=1, source_target_pairs={{0,24},{2,26},{4,28},{6,30},{8,16},{10,18},{12,20},{14,22},{16,8},... | collective-permute-start | bytes 331784 | tf_op jit(solution)/shard_map/ppermute | solution.py:753
  47.3 13.0 %collective-permute-start.24 = (bf16[144,384]{1,0:T(8,128)(2,1)S(1)}, bf16[144,384]{1,0:T(8,128)(2,1)S(1)}, u32[]{:S(2)}, u32[]{:S(2)}) collective-permute-start(bf16[144,384]{1,0:T(8,128)(2,1)S(1)} %get-tuple-element.190), channel_id=1, source_target_pairs={{0,16},{2,18},{4,20},{6,22},{8,24},{10,26},{12,28},{14,30},{16,0},... | collective-permute-start | bytes 331784 | tf_op jit(solution)/shard_map/ppermute | solution.py:753
  54.0 1.3 %collective-permute-start.21 = (bf16[48,384]{1,0:T(8,128)(2,1)S(1)}, bf16[48,384]{1,0:T(8,128)(2,1)S(1)}, u32[]{:S(2)}, u32[]{:S(2)}) collective-permute-start(bf16[48,384]{1,0:T(8,128)(2,1)S(1)} %get-tuple-element.194), channel_id=1, source_target_pairs={{0,1},{1,0},{2,3},{3,2},{4,5},{5,4},{6,7},{7,6},{8,9},{9,8},{10,11... | collective-permute-start | bytes 110600 | tf_op jit(solution)/shard_map/ppermute | solution.py:747
  55.5 9.3 %collective-permute-start.26 = (bf16[288,384]{1,0:T(8,128)(2,1)S(1)}, bf16[288,384]{1,0:T(8,128)(2,1)S(1)}, u32[]{:S(2)}, u32[]{:S(2)}) collective-permute-start(bf16[288,384]{1,0:T(8,128)(2,1)S(1)} %get-tuple-element.199), channel_id=1, source_target_pairs={{0,2},{2,0},{4,6},{6,4},{8,10},{10,8},{12,14},{14,12},{16,18},{18,... | collective-permute-start | bytes 663560 | tf_op jit(solution)/shard_map/ppermute | solution.py:750
  57.5 9.0 %collective-permute-start.22 = (bf16[336,384]{1,0:T(8,128)(2,1)S(1)}, bf16[336,384]{1,0:T(8,128)(2,1)S(1)}, u32[]{:S(2)}, u32[]{:S(2)}) collective-permute-start(bf16[336,384]{1,0:T(8,128)(2,1)S(1)} %get-tuple-element.197), channel_id=1, source_target_pairs={{0,4},{2,6},{4,0},{6,2},{8,12},{10,14},{12,8},{14,10},{16,20},{18,... | collective-permute-start | bytes 774152 | tf_op jit(solution)/shard_map/ppermute | solution.py:750
  60.3 9.9 %collective-permute-start.37 = (bf16[144,384]{1,0:T(8,128)(2,1)S(1)}, bf16[144,384]{1,0:T(8,128)(2,1)S(1)}, u32[]{:S(2)}, u32[]{:S(2)}) collective-permute-start(bf16[144,384]{1,0:T(8,128)(2,1)S(1)} %get-tuple-element.203), channel_id=1, source_target_pairs={{0,24},{2,26},{4,28},{6,30},{8,16},{10,18},{12,20},{14,22},{16,8},... | collective-permute-start | bytes 331784 | tf_op jit(solution)/shard_map/ppermute | solution.py:753
  63.3 11.7 %collective-permute-start.36 = (bf16[160,384]{1,0:T(8,128)(2,1)S(1)}, bf16[160,384]{1,0:T(8,128)(2,1)S(1)}, u32[]{:S(2)}, u32[]{:S(2)}) collective-permute-start(bf16[160,384]{1,0:T(8,128)(2,1)S(1)} %get-tuple-element.217.own), channel_id=1, source_target_pairs={{0,16},{2,18},{4,20},{6,22},{8,24},{10,26},{12,28},{14,30},{16,0},... | collective-permute-start | bytes 368648 | tf_op jit(solution)/shard_map/ppermute | solution.py:753
  63.7 11.3 %collective-permute-start.35 = (bf16[144,384]{1,0:T(8,128)(2,1)S(1)}, bf16[144,384]{1,0:T(8,128)(2,1)S(1)}, u32[]{:S(2)}, u32[]{:S(2)}) collective-permute-start(bf16[144,384]{1,0:T(8,128)(2,1)S(1)} %get-tuple-element.203), channel_id=1, source_target_pairs={{0,8},{2,10},{4,12},{6,14},{8,0},{10,2},{12,4},{14,6},{16,24},{18,... | collective-permute-start | bytes 331784 | tf_op jit(solution)/shard_map/ppermute | solution.py:753
  66.6 15.1 %collective-permute-start.27 = (bf16[192,384]{1,0:T(8,128)(2,1)S(1)}, bf16[192,384]{1,0:T(8,128)(2,1)S(1)}, u32[]{:S(2)}, u32[]{:S(2)}) collective-permute-start(bf16[192,384]{1,0:T(8,128)(2,1)S(1)} %get-tuple-element.207.near), channel_id=1, source_target_pairs={{0,8},{2,10},{4,12},{6,14},{8,0},{10,2},{12,4},{14,6},{16,24},{18,... | collective-permute-start | bytes 442376 | tf_op jit(solution)/shard_map/ppermute | solution.py:753
  68.5 13.2 %collective-permute-start.28 = (bf16[144,384]{1,0:T(8,128)(2,1)S(1)}, bf16[144,384]{1,0:T(8,128)(2,1)S(1)}, u32[]{:S(2)}, u32[]{:S(2)}) collective-permute-start(bf16[144,384]{1,0:T(8,128)(2,1)S(1)} %get-tuple-element.208), channel_id=1, source_target_pairs={{0,16},{2,18},{4,20},{6,22},{8,24},{10,26},{12,28},{14,30},{16,0},... | collective-permute-start | bytes 331784 | tf_op jit(solution)/shard_map/ppermute | solution.py:753
  70.2 11.5 %collective-permute-start.29 = (bf16[144,384]{1,0:T(8,128)(2,1)S(1)}, bf16[144,384]{1,0:T(8,128)(2,1)S(1)}, u32[]{:S(2)}, u32[]{:S(2)}) collective-permute-start(bf16[144,384]{1,0:T(8,128)(2,1)S(1)} %get-tuple-element.209), channel_id=1, source_target_pairs={{0,24},{2,26},{4,28},{6,30},{8,16},{10,18},{12,20},{14,22},{16,8},... | collective-permute-start | bytes 331784 | tf_op jit(solution)/shard_map/ppermute | solution.py:753
  75.8 10.6 %collective-permute-start.40 = (bf16[576,384]{1,0:T(8,128)(2,1)S(1)}, bf16[576,384]{1,0:T(8,128)(2,1)S(1)}, u32[]{:S(2)}, u32[]{:S(2)}) collective-permute-start(bf16[576,384]{1,0:T(8,128)(2,1)S(1)} %get-tuple-element.228.refs_0_), channel_id=1, source_target_pairs={{0,4},{2,6},{4,0},{6,2},{8,12},{10,14},{12,8},{14,10},{16,20},{18,... | collective-permute-start | bytes 1327112 | tf_op jit(solution)/shard_map/ppermute | solution.py:750
  77.2 9.7 %collective-permute-start.39 = (bf16[576,384]{1,0:T(8,128)(2,1)S(1)}, bf16[576,384]{1,0:T(8,128)(2,1)S(1)}, u32[]{:S(2)}, u32[]{:S(2)}) collective-permute-start(bf16[576,384]{1,0:T(8,128)(2,1)S(1)} %get-tuple-element.228.refs_0_), channel_id=1, source_target_pairs={{0,2},{2,0},{4,6},{6,4},{8,10},{10,8},{12,14},{14,12},{16,18},{18,... | collective-permute-start | bytes 1327112 | tf_op jit(solution)/shard_map/ppermute | solution.py:750
  81.8 12.9 %collective-permute-start.31 = (bf16[192,384]{1,0:T(8,128)(2,1)S(1)}, bf16[192,384]{1,0:T(8,128)(2,1)S(1)}, u32[]{:S(2)}, u32[]{:S(2)}) collective-permute-start(bf16[192,384]{1,0:T(8,128)(2,1)S(1)} %get-tuple-element.210.own), channel_id=1, source_target_pairs={{0,16},{2,18},{4,20},{6,22},{8,24},{10,26},{12,28},{14,30},{16,0},... | collective-permute-start | bytes 442376 | tf_op jit(solution)/shard_map/ppermute | solution.py:753
  85.0 8.1 %collective-permute-start.32 = (bf16[144,384]{1,0:T(8,128)(2,1)S(1)}, bf16[144,384]{1,0:T(8,128)(2,1)S(1)}, u32[]{:S(2)}, u32[]{:S(2)}) collective-permute-start(bf16[144,384]{1,0:T(8,128)(2,1)S(1)} %get-tuple-element.211), channel_id=1, source_target_pairs={{0,24},{2,26},{4,28},{6,30},{8,16},{10,18},{12,20},{14,22},{16,8},... | collective-permute-start | bytes 331784 | tf_op jit(solution)/shard_map/ppermute | solution.py:753
  86.4 6.7 %collective-permute-start.30 = (bf16[144,384]{1,0:T(8,128)(2,1)S(1)}, bf16[144,384]{1,0:T(8,128)(2,1)S(1)}, u32[]{:S(2)}, u32[]{:S(2)}) collective-permute-start(bf16[144,384]{1,0:T(8,128)(2,1)S(1)} %get-tuple-element.211), channel_id=1, source_target_pairs={{0,8},{2,10},{4,12},{6,14},{8,0},{10,2},{12,4},{14,6},{16,24},{18,... | collective-permute-start | bytes 331784 | tf_op jit(solution)/shard_map/ppermute | solution.py:753
  86.5 12.5 %collective-permute-start.41 = (bf16[288,384]{1,0:T(8,128)(2,1)S(1)}, bf16[288,384]{1,0:T(8,128)(2,1)S(1)}, u32[]{:S(2)}, u32[]{:S(2)}) collective-permute-start(bf16[288,384]{1,0:T(8,128)(2,1)S(1)} %slice.20), channel_id=1, source_target_pairs={{0,2},{2,0},{4,6},{6,4},{8,10},{10,8},{12,14},{14,12},{16,18},{18,... | collective-permute-start | bytes 663560 | tf_op jit(solution)/shard_map/ppermute | solution.py:750
  86.9 12.0 %collective-permute-start.42 = (bf16[288,384]{1,0:T(8,128)(2,1)S(1)}, bf16[288,384]{1,0:T(8,128)(2,1)S(1)}, u32[]{:S(2)}, u32[]{:S(2)}) collective-permute-start(bf16[288,384]{1,0:T(8,128)(2,1)S(1)} %slice.21), channel_id=1, source_target_pairs={{0,4},{2,6},{4,0},{6,2},{8,12},{10,14},{12,8},{14,10},{16,20},{18,... | collective-permute-start | bytes 663560 | tf_op jit(solution)/shard_map/ppermute | solution.py:750
  94.8 3.5 %collective-permute-start.38 = (f32[16,384]{1,0:T(8,128)S(1)}, f32[16,384]{1,0:T(8,128)S(1)}, u32[]{:S(2)}, u32[]{:S(2)}) collective-permute-start(f32[16,384]{1,0:T(8,128)S(1)} %get-tuple-element.222.small), channel_id=1, source_target_pairs={{0,1},{1,0},{2,3},{3,2},{4,5},{5,4},{6,7},{7,6},{8,9},{9,8},{10,11... | collective-permute-start | bytes 73736 | tf_op jit(solution)/shard_map/ppermute | solution.py:747
  94.9 12.6 %collective-permute-start.34 = (bf16[576,384]{1,0:T(8,128)(2,1)S(1)}, bf16[576,384]{1,0:T(8,128)(2,1)S(1)}, u32[]{:S(2)}, u32[]{:S(2)}) collective-permute-start(bf16[576,384]{1,0:T(8,128)(2,1)S(1)} %get-tuple-element.212.refs_0_), channel_id=1, source_target_pairs={{0,4},{2,6},{4,0},{6,2},{8,12},{10,14},{12,8},{14,10},{16,20},{18,... | collective-permute-start | bytes 1327112 | tf_op jit(solution)/shard_map/ppermute | solution.py:750
  95.4 13.0 %collective-permute-start.33 = (bf16[624,384]{1,0:T(8,128)(2,1)S(1)}, bf16[624,384]{1,0:T(8,128)(2,1)S(1)}, u32[]{:S(2)}, u32[]{:S(2)}) collective-permute-start(bf16[624,384]{1,0:T(8,128)(2,1)S(1)} %get-tuple-element.216), channel_id=1, source_target_pairs={{0,2},{2,0},{4,6},{6,4},{8,10},{10,8},{12,14},{14,12},{16,18},{18,... | collective-permute-start | bytes 1437704 | tf_op jit(solution)/shard_map/ppermute | solution.py:750
  108.4 6.7 %collective-permute-start.45 = (bf16[288,384]{1,0:T(8,128)(2,1)S(1)}, bf16[288,384]{1,0:T(8,128)(2,1)S(1)}, u32[]{:S(2)}, u32[]{:S(2)}) collective-permute-start(bf16[288,384]{1,0:T(8,128)(2,1)S(1)} %slice.19), channel_id=1, source_target_pairs={{0,4},{2,6},{4,0},{6,2},{8,12},{10,14},{12,8},{14,10},{16,20},{18,... | collective-permute-start | bytes 663560 | tf_op jit(solution)/shard_map/ppermute | solution.py:750
  110.1 6.4 %collective-permute-start.44 = (bf16[288,384]{1,0:T(8,128)(2,1)S(1)}, bf16[288,384]{1,0:T(8,128)(2,1)S(1)}, u32[]{:S(2)}, u32[]{:S(2)}) collective-permute-start(bf16[288,384]{1,0:T(8,128)(2,1)S(1)} %slice.18), channel_id=1, source_target_pairs={{0,2},{2,0},{4,6},{6,4},{8,10},{10,8},{12,14},{14,12},{16,18},{18,... | collective-permute-start | bytes 663560 | tf_op jit(solution)/shard_map/ppermute | solution.py:750
  110.6 2.1 %collective-permute-start.43 = (f32[48,384]{1,0:T(8,128)S(1)}, f32[48,384]{1,0:T(8,128)S(1)}, u32[]{:S(2)}, u32[]{:S(2)}) collective-permute-start(f32[48,384]{1,0:T(8,128)S(1)} %convert_add_fusion), channel_id=1, source_target_pairs={{0,1},{1,0},{2,3},{3,2},{4,5},{5,4},{6,7},{7,6},{8,9},{9,8},{10,11... | collective-permute-start | bytes 221192 | tf_op jit(solution)/shard_map/ppermute | solution.py:747

commit v2 on v1

--- a/solution.py
+++ b/solution.py
@@ -160,15 +160,17 @@
     mols = rows // SEQ
     core = places()[0]
     own_rows = pl.ds(pl.multiple_of(core * rows, SEQ), rows)
+    parts = [pl.ds(pl.multiple_of(core * rows + m * SEQ, SEQ), SEQ) for m in range(mols)]
     copies = copy_in(
         (
-            feats_in.at[own_rows, :], lap_in.at[:, own_rows], ends_in.at[:, own_rows], nodes_in,
+            feats_in.at[parts[0], :], lap_in.at[:, own_rows], ends_in.at[:, own_rows], nodes_in,
             w_ident_in, types_in, gain_in, shift_in, bias_q_in, bias_v_in, wq_in, wk_in, wv_in,
-            edges_in,
+            edges_in, *(feats_in.at[part, :] for part in parts[1:]),
         ),
         (
-            feats, lap, ends, nodes, w_ident, types, gain_rows, shift_rows, bias_q, bias_v,
+            feats.at[pl.ds(0, SEQ), :], lap, ends, nodes, w_ident, types, gain_rows, shift_rows, bias_q, bias_v,
             w_q, w_k, w_v, edges,
+            *(feats.at[pl.ds(m * SEQ, SEQ), :] for m in range(1, mols)),
         ),
         sems,
     )
@@ -177,6 +179,8 @@
     gain, shift = row_of(gain_rows), row_of(shift_rows)
 
     def molecule(m):
+        if m > 0:
+            copies[13 + m].wait()
         at = slice(m * SEQ, (m + 1) * SEQ)
         count = nodes[core * mols + m]
         hidden, ident, normed = embed_rows(
@@ -696,16 +700,18 @@
     _, inner, outer = places()
     unit = first.shape[0] // 6
     size = OUTER * unit
-    for turn in range(OUTER):
-        ref, start = (first, turn * 3 * unit) if turn < 2 else (second, (turn - 2) * 3 * unit)
-        at = pl.ds(pl.multiple_of((outer ^ turn) * unit, 16), unit)
-        for place in range(3):
+    target = pl.ds(pl.multiple_of((inner ^ 3) * size, 64), size)
+    copies = []
+    for place in range(3):
+        for turn in range(OUTER):
+            ref, start = (first, turn * 3 * unit) if turn < 2 else (second, (turn - 2) * 3 * unit)
+            at = pl.ds(pl.multiple_of((outer ^ turn) * unit, 16), unit)
             rows = slice(start + place * unit, start + (place + 1) * unit)
             blocks[place, at, :] = ref[rows, :].astype(F32)
-    at = pl.ds(pl.multiple_of((inner ^ 3) * size, 64), size)
-    copies = copy_in(
-        [blocks.at[place] for place in range(3)], [out.at[at, :] for out in outs], sems
-    )
+        copies.append(
+            pltpu.make_async_copy(blocks.at[place], outs[place].at[target, :], sems.at[place])
+        )
+        copies[-1].start()
     for copy in copies:
         copy.wait()
 
@@ -812,7 +818,7 @@
         scratch=embed_scratch
         + [half_scratch] * 2
         + [pltpu.VMEM((dim, width), BF16)] * 3
-        + [count_scratch, pltpu.SemaphoreType.DMA((14,))],
+        + [count_scratch, pltpu.SemaphoreType.DMA((13 + mols,))],
     )
     wd_got = swap(after(w_down, normed))
     ahead_rows, back_rows = dim + 2 * width, 3 * rows + 16

time: 118 us -> 119 us (level)
  transfers between devices with their start and end apart: 46 -> 46, of which waited for: 14 -> 16; matrix products, arithmetic and copies ran while one was open for 0% -> 0% of each run, Pallas kernels for 35% -> 35%
where the time goes in v2:
time: 119 us
  starting transfers between devices  42.4 us (36%)
  Pallas kernels  42 us (35%)
  waiting for transfers between devices  32.9 us (28%)
    pallas_call x23, Pallas kernels, call(): pl.pallas_call(kernel, out_shape=[jax.ShapeDtypeStruct(shape, kind) for s...  42 us
    ppermute x18, starting transfers between devices, inner_move(): return lax.ppermute(part, 'dp', [(s, s ^ step) for s in range(dp_count)])  20.5 us
    ppermute x12, starting transfers between devices, outer_move(): lax.ppermute(part, 'dp', [(s, s ^ step * INNER) for s in range(dp_count)])  17.8 us
    ppermute x18, waiting for transfers between devices, inner_move(): return lax.ppermute(part, 'dp', [(s, s ^ step) for s in range(dp_count)])  15.8 us
    ppermute x12, waiting for transfers between devices, outer_move(): lax.ppermute(part, 'dp', [(s, s ^ step * INNER) for s in range(dp_count)])  15.1 us
    ppermute x16, starting transfers between devices, swap(): return lax.ppermute(part, 'mp', [(0, 1), (1, 0)])  4.04 us
  transfers between devices with their start and end apart: 46, of which 16 were waited for; matrix products, arithmetic and copies ran while one was open for 0% of the time, Pallas kernels for 35%

profile of v2, /device:TPU:0, one launch (start us, length us, event | category | flops | bytes accessed | tf_op | source)
XLA Modules:
  0.0 118.5 jit_solution(7523904962245638694)
XLA Ops:
  0.7 0.5 collective-permute-start
  1.3 0.4 collective-permute-start.6
  1.8 0.4 collective-permute-start.1
  2.2 0.8 collective-permute-done.5
  3.0 0.4 collective-permute-start.2
  3.5 0.4 collective-permute-start.4
  3.9 4.8 %shard_map.366 = (f32[384,768]{1,0:T(8,128)S(1)}, bf16[32,384]{1,0:T(8,128)(2,1)S(1)}, bf16[384,768]{1,0:T(8,128)(2,1)S(1)}, bf16[768,384]{1,0:T(8,128)(2,1)S(1)...) custom-call(bf16[768,768]{1,0:T(8,128)(2,1)} %refs_10_.1, ...), custom_call_target="tpu_custom_call" | custom-call | tf_op jit(solution)/shard_map/pallas_call | solution.py:91
  9.0 7.3 %shard_map.367 = (bf16[384,384]{1,0:T(8,128)(2,1)S(1)}, bf16[384,384]{1,0:T(8,128)(2,1)S(1)}, bf16[384,384]{1,0:T(8,128)(2,1)S(1)}, bf16[3,16,128,256]{3,2,1,0:T...) custom-call(f32[384,768]{1,0:T(8,128)S(1)} %get-tuple-element.135.hi, ...), custom_call_target="tpu_custom_call" | custom-call | tf_op jit(solution)/shard_map/pallas_call | solution.py:91
  16.2 0.4 collective-permute-start.9
  16.7 2.9 %shard_map.368 = (bf16[1168,384]{1,0:T(8,128)(2,1)S(1)}, bf16[1168,384]{1,0:T(8,128)(2,1)S(1)}, f32[384,768]{1,0:T(8,128)S(1)}, bf16[384,768]{1,0:T(8,128)(2,1)S(1)}) custom-call(f32[384,768]{1,0:T(8,128)S(1)} %get-tuple-element.140.middle, f32[384,768]{1,0:T(8,128)S(1)} %get-tuple-element.145.slope, bf16[768,384]{1,0:T(8,128)(2,1)S(1)} %copy-done.1, ...), custom_call_target="tpu_custom_call" | custom-call | tf_op jit(solution)/shard_map/pallas_call | solution.py:91
  19.8 1.2 %shard_map.369 = (bf16[192,384]{1,0:T(8,128)(2,1)S(1)}, bf16[192,384]{1,0:T(8,128)(2,1)S(1)}, bf16[192,384]{1,0:T(8,128)(2,1)S(1)}, bf16[192,384]{1,0:T(8,128)(2,1)S(1)}) custom-call(bf16[1536,384]{1,0:T(8,128)(2,1)S(1)} %get-tuple-element.151.kept, bf16[1536,384]{1,0:T(8,128)(2,1)S(1)} %collective-permute-done.9.got, bf16[768,768]{1,0:T(8,128)(2,1)S(1)} %copy-done, ...), custom_call_target="tpu_custom_call" | custom-call | tf_op jit(solution)/shard_map/pallas_call | solution.py:91
  21.0 3.1 %collective-permute-start.13 = (bf16[192,384]{1,0:T(8,128)(2,1)S(1)}, bf16[192,384]{1,0:T(8,128)(2,1)S(1)}, u32[]{:S(2)}, u32[]{:S(2)}) collective-permute-start(bf16[192,384]{1,0:T(8,128)(2,1)S(1)} %get-tuple-element.158), channel_id=1, source_target_pairs={{0,4},{2,6},{4,0},{6,2},{8,12},{10,14},{12,8},{14,10},{16,20},{18,... | collective-permute-start | bytes 442376 | tf_op jit(solution)/shard_map/ppermute | solution.py:756
  24.1 1.5 %collective-permute-start.12 = (bf16[192,384]{1,0:T(8,128)(2,1)S(1)}, bf16[192,384]{1,0:T(8,128)(2,1)S(1)}, u32[]{:S(2)}, u32[]{:S(2)}) collective-permute-start(bf16[192,384]{1,0:T(8,128)(2,1)S(1)} %get-tuple-element.156), channel_id=1, source_target_pairs={{0,2},{2,0},{4,6},{6,4},{8,10},{10,8},{12,14},{14,12},{16,18},{18,... | collective-permute-start | bytes 442376 | tf_op jit(solution)/shard_map/ppermute | solution.py:756
  25.6 1.7 %shard_map.370 = (bf16[400,384]{1,0:T(8,128)(2,1)S(1)}, bf16[400,384]{1,0:T(8,128)(2,1)S(1)}, bf16[384,384]{1,0:T(8,128)(2,1)S(1)}, bf16[384,384]{1,0:T(8,128)(2,1)S(1)}) custom-call(bf16[1536,384]{1,0:T(8,128)(2,1)S(1)} %get-tuple-element.151.kept, bf16[1536,384]{1,0:T(8,128)(2,1)S(1)} %collective-permute-done.9.got, ...), custom_call_target="tpu_custom_call" | custom-call | tf_op jit(solution)/shard_map/pallas_call | solution.py:91
  27.3 0.6 collective-permute-start.11
  28.1 0.2 collective-permute-done.13.refs_3_
  28.3 1.6 %collective-permute-done.12.refs_1_ = bf16[192,384]{1,0:T(8,128)(2,1)S(1)} collective-permute-done((bf16[192,384]{1,0:T(8,128)(2,1)S(1)}, bf16[192,384]{1,0:T(8,128)(2,1)S(1)}, u32[]{:S(2)}, u32[]{:S(2)}) %collective-permute-start.12) | collective-permute-done | bytes 147488 | tf_op jit(solution)/shard_map/ppermute | solution.py:756
  29.9 0.8 shard_map.371
  30.7 4.2 %shard_map.372 = (bf16[1152,384]{1,0:T(8,128)(2,1)S(1)}, bf16[1152,384]{1,0:T(8,128)(2,1)S(1)}) custom-call(bf16[384,384]{1,0:T(8,128)(2,1)S(1)} %get-tuple-element.137.q_own, bf16[384,384]{1,0:T(8,128)(2,1)S(1)} %get-tuple-element.138.k_own, bf16[384,384]{1,0:T(8,128)(2,1)S(1)} %get-tuple-element.139.v_own, bf16[384,384]{1,0:T(8,128)(2,1)S(1)} %get-tuple-element.161.ga_own, ...), custom_call_target="tpu_custom_call" | custom-call | tf_op jit(solution)/shard_map/pallas_call | solution.py:91
  35.0 0.5 collective-permute-start.15
  35.5 0.7 collective-permute-done.14.second_got
  36.6 0.8 collective-permute-start.19
  37.3 1.3 %collective-permute-start.20 = (bf16[288,384]{1,0:T(8,128)(2,1)S(1)}, bf16[288,384]{1,0:T(8,128)(2,1)S(1)}, u32[]{:S(2)}, u32[]{:S(2)}) collective-permute-start(bf16[288,384]{1,0:T(8,128)(2,1)S(1)} %get-tuple-element.176), channel_id=1, source_target_pairs={{0,2},{2,0},{4,6},{6,4},{8,10},{10,8},{12,14},{14,12},{16,18},{18,... | collective-permute-start | bytes 663560 | tf_op jit(solution)/shard_map/ppermute | solution.py:756
  38.6 2.2 %shard_map.374 = (bf16[576,384]{1,0:T(8,128)(2,1)S(1)}, bf16[576,384]{1,0:T(8,128)(2,1)S(1)}, bf16[576,384]{1,0:T(8,128)(2,1)S(1)}, bf16[576,384]{1,0:T(8,128)(2,1)S(1)}, f32[48,384]{1,0:T(8,128)S(1)}) custom-call(bf16[768,384]{1,0:T(8,128)(2,1)S(1)} %get-tuple-element.178.normed_t, bf16[768,384]{1,0:T(8,128)(2,1)S(1)} %collective-permute-done.15.normed_t_got, ...), custom_call_target="tpu_custom_call" | custom-call | tf_op jit(solution)/shard_map/pallas_call | solution.py:91
  40.9 2.1 %collective-permute-start.17 = (bf16[576,384]{1,0:T(8,128)(2,1)S(1)}, bf16[576,384]{1,0:T(8,128)(2,1)S(1)}, u32[]{:S(2)}, u32[]{:S(2)}) collective-permute-start(bf16[576,384]{1,0:T(8,128)(2,1)S(1)} %get-tuple-element.181), channel_id=1, source_target_pairs={{0,2},{2,0},{4,6},{6,4},{8,10},{10,8},{12,14},{14,12},{16,18},{18,... | collective-permute-start | bytes 1327112 | tf_op jit(solution)/shard_map/ppermute | solution.py:756
  43.1 0.9 collective-permute-done.20.second_got
  44.1 1.6 %collective-permute-start.23 = (bf16[160,384]{1,0:T(8,128)(2,1)S(1)}, bf16[160,384]{1,0:T(8,128)(2,1)S(1)}, u32[]{:S(2)}, u32[]{:S(2)}) collective-permute-start(bf16[160,384]{1,0:T(8,128)(2,1)S(1)} %get-tuple-element.189.near), channel_id=1, source_target_pairs={{0,8},{2,10},{4,12},{6,14},{8,0},{10,2},{12,4},{14,6},{16,24},{18,... | collective-permute-start | bytes 368648 | tf_op jit(solution)/shard_map/ppermute | solution.py:759
  45.8 2.5 %collective-permute-start.25 = (bf16[144,384]{1,0:T(8,128)(2,1)S(1)}, bf16[144,384]{1,0:T(8,128)(2,1)S(1)}, u32[]{:S(2)}, u32[]{:S(2)}) collective-permute-start(bf16[144,384]{1,0:T(8,128)(2,1)S(1)} %get-tuple-element.191), channel_id=1, source_target_pairs={{0,24},{2,26},{4,28},{6,30},{8,16},{10,18},{12,20},{14,22},{16,8},... | collective-permute-start | bytes 331784 | tf_op jit(solution)/shard_map/ppermute | solution.py:759
  48.4 6.6 %shard_map.376 = (f32[384,768]{1,0:T(8,128)}, f32[48,384]{1,0:T(8,128)S(1)}, bf16[48,384]{1,0:T(8,128)(2,1)S(1)}) custom-call(bf16[1152,384]{1,0:T(8,128)(2,1)S(1)} %get-tuple-element.167.kept.refs_0_, bf16[1152,384]{1,0:T(8,128)(2,1)S(1)} %get-tuple-element.179.refs_1_, bf16[768,384]{1,0:T(8,128)(2,1)S(1)} %copy-done.2, bf16[768,384]{1,0:T(8,128)(2,1)S(1)} %copy-done.3, ...), custom_call_target="tpu_custom_call" | custom-call | tf_op jit(solution)/shard_map/pallas_call | solution.py:91
  55.1 1.2 %collective-permute-done.21.refs_1_ = bf16[48,384]{1,0:T(8,128)(2,1)S(1)} collective-permute-done((bf16[48,384]{1,0:T(8,128)(2,1)S(1)}, bf16[48,384]{1,0:T(8,128)(2,1)S(1)}, u32[]{:S(2)}, u32[]{:S(2)}) %collective-permute-start.21) | collective-permute-done | bytes 36896 | tf_op jit(solution)/shard_map/ppermute | solution.py:753
  56.2 0.2 shard_map.377
  56.5 2.0 %collective-permute-start.26 = (bf16[288,384]{1,0:T(8,128)(2,1)S(1)}, bf16[288,384]{1,0:T(8,128)(2,1)S(1)}, u32[]{:S(2)}, u32[]{:S(2)}) collective-permute-start(bf16[288,384]{1,0:T(8,128)(2,1)S(1)} %get-tuple-element.199), channel_id=1, source_target_pairs={{0,2},{2,0},{4,6},{6,4},{8,10},{10,8},{12,14},{14,12},{16,18},{18,... | collective-permute-start | bytes 663560 | tf_op jit(solution)/shard_map/ppermute | solution.py:756
  58.5 2.6 %collective-permute-start.22 = (bf16[336,384]{1,0:T(8,128)(2,1)S(1)}, bf16[336,384]{1,0:T(8,128)(2,1)S(1)}, u32[]{:S(2)}, u32[]{:S(2)}) collective-permute-start(bf16[336,384]{1,0:T(8,128)(2,1)S(1)} %get-tuple-element.197), channel_id=1, source_target_pairs={{0,4},{2,6},{4,0},{6,2},{8,12},{10,14},{12,8},{14,10},{16,20},{18,... | collective-permute-start | bytes 774152 | tf_op jit(solution)/shard_map/ppermute | solution.py:756
  61.2 3.0 %collective-permute-start.37 = (bf16[144,384]{1,0:T(8,128)(2,1)S(1)}, bf16[144,384]{1,0:T(8,128)(2,1)S(1)}, u32[]{:S(2)}, u32[]{:S(2)}) collective-permute-start(bf16[144,384]{1,0:T(8,128)(2,1)S(1)} %get-tuple-element.203), channel_id=1, source_target_pairs={{0,24},{2,26},{4,28},{6,30},{8,16},{10,18},{12,20},{14,22},{16,8},... | collective-permute-start | bytes 331784 | tf_op jit(solution)/shard_map/ppermute | solution.py:759
  64.2 0.3 collective-permute-start.36
  64.5 1.1 collective-permute-start.35
  65.7 1.7 %collective-permute-done.22.first_got = bf16[336,384]{1,0:T(8,128)(2,1)S(1)} collective-permute-done((bf16[336,384]{1,0:T(8,128)(2,1)S(1)}, bf16[336,384]{1,0:T(8,128)(2,1)S(1)}, u32[]{:S(2)}, u32[]{:S(2)}) %collective-permute-start.22) | collective-permute-done | bytes 258080 | tf_op jit(solution)/shard_map/ppermute | solution.py:756
  67.5 1.8 %collective-permute-start.27 = (bf16[192,384]{1,0:T(8,128)(2,1)S(1)}, bf16[192,384]{1,0:T(8,128)(2,1)S(1)}, u32[]{:S(2)}, u32[]{:S(2)}) collective-permute-start(bf16[192,384]{1,0:T(8,128)(2,1)S(1)} %get-tuple-element.207.near), channel_id=1, source_target_pairs={{0,8},{2,10},{4,12},{6,14},{8,0},{10,2},{12,4},{14,6},{16,24},{18,... | collective-permute-start | bytes 442376 | tf_op jit(solution)/shard_map/ppermute | solution.py:759
  69.4 1.7 %collective-permute-start.28 = (bf16[144,384]{1,0:T(8,128)(2,1)S(1)}, bf16[144,384]{1,0:T(8,128)(2,1)S(1)}, u32[]{:S(2)}, u32[]{:S(2)}) collective-permute-start(bf16[144,384]{1,0:T(8,128)(2,1)S(1)} %get-tuple-element.208), channel_id=1, source_target_pairs={{0,16},{2,18},{4,20},{6,22},{8,24},{10,26},{12,28},{14,30},{16,0},... | collective-permute-start | bytes 331784 | tf_op jit(solution)/shard_map/ppermute | solution.py:759
  71.1 0.9 collective-permute-start.29
  72.0 3.9 %collective-permute-done.36.middle = bf16[160,384]{1,0:T(8,128)(2,1)S(1)} collective-permute-done((bf16[160,384]{1,0:T(8,128)(2,1)S(1)}, bf16[160,384]{1,0:T(8,128)(2,1)S(1)}, u32[]{:S(2)}, u32[]{:S(2)}) %collective-permute-start.36) | collective-permute-done | bytes 122912 | tf_op jit(solution)/shard_map/ppermute | solution.py:759
  75.9 0.8 shard_map.383
  76.8 1.4 %collective-permute-start.40 = (bf16[576,384]{1,0:T(8,128)(2,1)S(1)}, bf16[576,384]{1,0:T(8,128)(2,1)S(1)}, u32[]{:S(2)}, u32[]{:S(2)}) collective-permute-start(bf16[576,384]{1,0:T(8,128)(2,1)S(1)} %get-tuple-element.228.refs_0_), channel_id=1, source_target_pairs={{0,4},{2,6},{4,0},{6,2},{8,12},{10,14},{12,8},{14,10},{16,20},{18,... | collective-permute-start | bytes 1327112 | tf_op jit(solution)/shard_map/ppermute | solution.py:756
  78.1 4.5 %collective-permute-done.28.middle_got = bf16[144,384]{1,0:T(8,128)(2,1)S(1)} collective-permute-done((bf16[144,384]{1,0:T(8,128)(2,1)S(1)}, bf16[144,384]{1,0:T(8,128)(2,1)S(1)}, u32[]{:S(2)}, u32[]{:S(2)}) %collective-permute-start.28) | collective-permute-done | bytes 110624 | tf_op jit(solution)/shard_map/ppermute | solution.py:759
  82.7 3.2 %collective-permute-start.31 = (bf16[192,384]{1,0:T(8,128)(2,1)S(1)}, bf16[192,384]{1,0:T(8,128)(2,1)S(1)}, u32[]{:S(2)}, u32[]{:S(2)}) collective-permute-start(bf16[192,384]{1,0:T(8,128)(2,1)S(1)} %get-tuple-element.210.own), channel_id=1, source_target_pairs={{0,16},{2,18},{4,20},{6,22},{8,24},{10,26},{12,28},{14,30},{16,0},... | collective-permute-start | bytes 442376 | tf_op jit(solution)/shard_map/ppermute | solution.py:759
  85.9 1.4 %collective-permute-start.32 = (bf16[144,384]{1,0:T(8,128)(2,1)S(1)}, bf16[144,384]{1,0:T(8,128)(2,1)S(1)}, u32[]{:S(2)}, u32[]{:S(2)}) collective-permute-start(bf16[144,384]{1,0:T(8,128)(2,1)S(1)} %get-tuple-element.211), channel_id=1, source_target_pairs={{0,24},{2,26},{4,28},{6,30},{8,16},{10,18},{12,20},{14,22},{16,8},... | collective-permute-start | bytes 331784 | tf_op jit(solution)/shard_map/ppermute | solution.py:759
  87.3 0.4 collective-permute-start.41
  87.8 1.1 collective-permute-start.42
  88.9 5.1 %collective-permute-done.32.far = bf16[144,384]{1,0:T(8,128)(2,1)S(1)} collective-permute-done((bf16[144,384]{1,0:T(8,128)(2,1)S(1)}, bf16[144,384]{1,0:T(8,128)(2,1)S(1)}, u32[]{:S(2)}, u32[]{:S(2)}) %collective-permute-start.32) | collective-permute-done | bytes 110624 | tf_op jit(solution)/shard_map/ppermute | solution.py:759
  94.0 1.5 %collective-permute-done.31.middle = bf16[192,384]{1,0:T(8,128)(2,1)S(1)} collective-permute-done((bf16[192,384]{1,0:T(8,128)(2,1)S(1)}, bf16[192,384]{1,0:T(8,128)(2,1)S(1)}, u32[]{:S(2)}, u32[]{:S(2)}) %collective-permute-start.31) | collective-permute-done | bytes 147488 | tf_op jit(solution)/shard_map/ppermute | solution.py:759
  95.8 0.5 collective-permute-start.34
  96.2 0.7 collective-permute-start.33
  96.9 2.3 %shard_map.382 = bf16[384,768]{1,0:T(8,128)(2,1)} custom-call(f32[384,768]{1,0:T(8,128)S(1)} %get-tuple-element.140.middle, bf16[384,768]{1,0:T(8,128)(2,1)S(1)} %get-tuple-element.141.active, bf16[384,768]{1,0:T(8,128)(2,1)S(1)} %copy-done.5, bf16[384,768]{1,0:T(8,128)(2,1)S(1)} %collective-permute-done.8.wd, bf16[6,128]{1,0:T(8,128)(2,1)} %bitcast.35), custom_call_target="tpu_custom_call" | custom-call | tf_op jit(solution)/shard_map/pallas_call | solution.py:91
  99.2 0.6 shard_map.384
  99.9 2.1 %shard_map.385 = (f32[768,384]{1,0:T(8,128)}, f32[384,768]{1,0:T(8,128)}, f32[384,768]{1,0:T(8,128)}) custom-call(bf16[576,384]{1,0:T(8,128)(2,1)S(1)} %get-tuple-element.228.refs_0_, bf16[576,384]{1,0:T(8,128)(2,1)S(1)} %collective-permute-done.39.refs_1_, bf16[576,384]{1,0:T(8,128)(2,1)S(1)} %collective-permute-done.40.refs_2_, ...), custom_call_target="tpu_custom_call" | custom-call | flops 10000000000 | tf_op jit(solution)/shard_map/pallas_call | solution.py:91
  101.9 6.4 %collective-permute-done.34.refs_2_ = bf16[576,384]{1,0:T(8,128)(2,1)S(1)} collective-permute-done((bf16[576,384]{1,0:T(8,128)(2,1)S(1)}, bf16[576,384]{1,0:T(8,128)(2,1)S(1)}, u32[]{:S(2)}, u32[]{:S(2)}) %collective-permute-start.34) | collective-permute-done | bytes 442400 | tf_op jit(solution)/shard_map/ppermute | solution.py:756
  108.3 0.9 collective-permute-done.33.refs_1_
  109.3 1.7 %collective-permute-start.45 = (bf16[288,384]{1,0:T(8,128)(2,1)S(1)}, bf16[288,384]{1,0:T(8,128)(2,1)S(1)}, u32[]{:S(2)}, u32[]{:S(2)}) collective-permute-start(bf16[288,384]{1,0:T(8,128)(2,1)S(1)} %slice.19), channel_id=1, source_target_pairs={{0,4},{2,6},{4,0},{6,2},{8,12},{10,14},{12,8},{14,10},{16,20},{18,... | collective-permute-start | bytes 663560 | tf_op jit(solution)/shard_map/ppermute | solution.py:756
  111.0 0.5 collective-permute-start.44
  111.6 2.0 %shard_map.387 = (f32[768,384]{1,0:T(8,128)}, f32[768,384]{1,0:T(8,128)}, f32[768,384]{1,0:T(8,128)}) custom-call(bf16[576,384]{1,0:T(8,128)(2,1)S(1)} %get-tuple-element.212.refs_0_, bf16[624,384]{1,0:T(8,128)(2,1)S(1)} %collective-permute-done.33.refs_1_, bf16[576,384]{1,0:T(8,128)(2,1)S(1)} %collective-permute-done.34.refs_2_), custom_call_target="tpu_custom_call" | custom-call | tf_op jit(solution)/shard_map/pallas_call | solution.py:91
  113.6 0.7 shard_map.386
  114.3 1.8 %collective-permute-done.45.second = bf16[288,384]{1,0:T(8,128)(2,1)S(1)} collective-permute-done((bf16[288,384]{1,0:T(8,128)(2,1)S(1)}, bf16[288,384]{1,0:T(8,128)(2,1)S(1)}, u32[]{:S(2)}, u32[]{:S(2)}) %collective-permute-start.45) | collective-permute-done | bytes 221216 | tf_op jit(solution)/shard_map/ppermute | solution.py:756
  116.1 1.3 %collective-permute-done.44.first = bf16[288,384]{1,0:T(8,128)(2,1)S(1)} collective-permute-done((bf16[288,384]{1,0:T(8,128)(2,1)S(1)}, bf16[288,384]{1,0:T(8,128)(2,1)S(1)}, u32[]{:S(2)}, u32[]{:S(2)}) %collective-permute-start.44) | collective-permute-done | bytes 221216 | tf_op jit(solution)/shard_map/ppermute | solution.py:756
  117.4 1.0 shard_map.388
  (71 shorter events, 2.4 us)
Async XLA Ops:
  0.7 8.0 %collective-permute-start = (bf16[768,384]{1,0:T(8,128)(2,1)}, bf16[768,384]{1,0:T(8,128)(2,1)S(1)}, u32[]{:S(2)}, u32[]{:S(2)}) collective-permute-start(bf16[768,384]{1,0:T(8,128)(2,1)} %refs_2_.1), channel_id=1, source_target_pairs={{0,1},{1,0},{2,3},{3,2},{4,5},{5,4},{6,7},{7,6},{8,9},{9,8},{10,11... | collective-permute-start | bytes 1769480 | tf_op jit(solution)/shard_map/ppermute | solution.py:753
  1.2 1.8 %collective-permute-start.5 = (bf16[384]{0:T(512)(128)(2,1)}, bf16[384]{0:T(512)(128)(2,1)S(1)}, u32[]{:S(2)}, u32[]{:S(2)}) collective-permute-start(bf16[384]{0:T(512)(128)(2,1)} %param.35), channel_id=1, source_target_pairs={{0,1},{1,0},{2,3},{3,2},{4,5},{5,4},{6,7},{7,6},{8,9},{9,8},{10,11... | collective-permute-start | bytes 2312 | tf_op jit(solution)/shard_map/ppermute | solution.py:753
  1.3 2.1 %collective-permute-start.6 = (bf16[384]{0:T(512)(128)(2,1)}, bf16[384]{0:T(512)(128)(2,1)S(1)}, u32[]{:S(2)}, u32[]{:S(2)}) collective-permute-start(bf16[384]{0:T(512)(128)(2,1)} %param.36), channel_id=1, source_target_pairs={{0,1},{1,0},{2,3},{3,2},{4,5},{5,4},{6,7},{7,6},{8,9},{9,8},{10,11... | collective-permute-start | bytes 2312 | tf_op jit(solution)/shard_map/ppermute | solution.py:753
  1.7 1.8 %collective-permute-start.7 = (bf16[384]{0:T(512)(128)(2,1)}, bf16[384]{0:T(512)(128)(2,1)S(1)}, u32[]{:S(2)}, u32[]{:S(2)}) collective-permute-start(bf16[384]{0:T(512)(128)(2,1)} %param.42), channel_id=1, source_target_pairs={{0,1},{1,0},{2,3},{3,2},{4,5},{5,4},{6,7},{7,6},{8,9},{9,8},{10,11... | collective-permute-start | bytes 2312 | tf_op jit(solution)/shard_map/ppermute | solution.py:753
  1.8 7.1 %collective-permute-start.1 = (bf16[768,384]{1,0:T(8,128)(2,1)}, bf16[768,384]{1,0:T(8,128)(2,1)S(1)}, u32[]{:S(2)}, u32[]{:S(2)}) collective-permute-start(bf16[768,384]{1,0:T(8,128)(2,1)} %refs_3_.1), channel_id=1, source_target_pairs={{0,1},{1,0},{2,3},{3,2},{4,5},{5,4},{6,7},{7,6},{8,9},{9,8},{10,11... | collective-permute-start | bytes 1769480 | tf_op jit(solution)/shard_map/ppermute | solution.py:753
  3.0 5.9 %collective-permute-start.2 = (bf16[768,384]{1,0:T(8,128)(2,1)}, bf16[768,384]{1,0:T(8,128)(2,1)S(1)}, u32[]{:S(2)}, u32[]{:S(2)}) collective-permute-start(bf16[768,384]{1,0:T(8,128)(2,1)} %refs_4_.1), channel_id=1, source_target_pairs={{0,1},{1,0},{2,3},{3,2},{4,5},{5,4},{6,7},{7,6},{8,9},{9,8},{10,11... | collective-permute-start | bytes 1769480 | tf_op jit(solution)/shard_map/ppermute | solution.py:753
  3.4 5.5 %collective-permute-start.3 = (bf16[384,768]{1,0:T(8,128)(2,1)}, bf16[384,768]{1,0:T(8,128)(2,1)S(1)}, u32[]{:S(2)}, u32[]{:S(2)}) collective-permute-start(bf16[384,768]{1,0:T(8,128)(2,1)} %wo_own.3), channel_id=1, source_target_pairs={{0,1},{1,0},{2,3},{3,2},{4,5},{5,4},{6,7},{7,6},{8,9},{9,8},{10,11... | collective-permute-start | bytes 1769480 | tf_op jit(solution)/shard_map/ppermute | solution.py:753
  3.5 5.4 %collective-permute-start.4 = (bf16[768,384]{1,0:T(8,128)(2,1)}, bf16[768,384]{1,0:T(8,128)(2,1)S(1)}, u32[]{:S(2)}, u32[]{:S(2)}) collective-permute-start(bf16[768,384]{1,0:T(8,128)(2,1)} %wu_own.3), channel_id=1, source_target_pairs={{0,1},{1,0},{2,3},{3,2},{4,5},{5,4},{6,7},{7,6},{8,9},{9,8},{10,11... | collective-permute-start | bytes 1769480 | tf_op jit(solution)/shard_map/ppermute | solution.py:753
  3.9 4.8 %copy-start.5 = (bf16[384,768]{1,0:T(8,128)(2,1)S(1)}, bf16[384,768]{1,0:T(8,128)(2,1)}, u32[]{:S(2)}) copy-start(bf16[384,768]{1,0:T(8,128)(2,1)} %wd_own.3) | copy-start | bytes 1769476
  3.9 5.0 %copy-start.1 = (bf16[768,384]{1,0:T(8,128)(2,1)S(1)}, bf16[768,384]{1,0:T(8,128)(2,1)}, u32[]{:S(2)}) copy-start(bf16[768,384]{1,0:T(8,128)(2,1)} %wu_own.3) | copy-start | bytes 1769476
  3.9 5.0 %copy-start.6 = (bf16[384,768]{1,0:T(8,128)(2,1)S(1)}, bf16[384,768]{1,0:T(8,128)(2,1)}, u32[]{:S(2)}) copy-start(bf16[384,768]{1,0:T(8,128)(2,1)} %wo_own.3) | copy-start | bytes 1769476
  8.7 8.0 %collective-permute-start.8 = (bf16[384,768]{1,0:T(8,128)(2,1)S(1)}, bf16[384,768]{1,0:T(8,128)(2,1)S(1)}, u32[]{:S(2)}, u32[]{:S(2)}) collective-permute-start(bf16[384,768]{1,0:T(8,128)(2,1)S(1)} %copy-done.5), channel_id=1, source_target_pairs={{0,1},{1,0},{2,3},{3,2},{4,5},{5,4},{6,7},{7,6},{8,9},{9,8},{10,11... | collective-permute-start | bytes 1769480 | tf_op jit(solution)/shard_map/ppermute | solution.py:753
  8.9 7.7 %copy-start = (bf16[768,768]{1,0:T(8,128)(2,1)S(1)}, bf16[768,768]{1,0:T(8,128)(2,1)}, u32[]{:S(2)}) copy-start(bf16[768,768]{1,0:T(8,128)(2,1)} %cots.3) | copy-start | bytes 3538948
  16.2 3.6 %collective-permute-start.9 = (bf16[1536,384]{1,0:T(8,128)(2,1)S(1)}, bf16[1536,384]{1,0:T(8,128)(2,1)S(1)}, u32[]{:S(2)}, u32[]{:S(2)}) collective-permute-start(bf16[1536,384]{1,0:T(8,128)(2,1)S(1)} %get-tuple-element.149), channel_id=1, source_target_pairs={{0,1},{1,0},{2,3},{3,2},{4,5},{5,4},{6,7},{7,6},{8,9},{9,8},{10,11... | collective-permute-start | bytes 3538952 | tf_op jit(solution)/shard_map/ppermute | solution.py:753
  19.6 6.0 %collective-permute-start.10 = (bf16[1168,384]{1,0:T(8,128)(2,1)S(1)}, bf16[1168,384]{1,0:T(8,128)(2,1)S(1)}, u32[]{:S(2)}, u32[]{:S(2)}) collective-permute-start(bf16[1168,384]{1,0:T(8,128)(2,1)S(1)} %get-tuple-element.153), channel_id=1, source_target_pairs={{0,1},{1,0},{2,3},{3,2},{4,5},{5,4},{6,7},{7,6},{8,9},{9,8},{10,11... | collective-permute-start | bytes 2691080 | tf_op jit(solution)/shard_map/ppermute | solution.py:753
  21.0 7.3 %collective-permute-start.13 = (bf16[192,384]{1,0:T(8,128)(2,1)S(1)}, bf16[192,384]{1,0:T(8,128)(2,1)S(1)}, u32[]{:S(2)}, u32[]{:S(2)}) collective-permute-start(bf16[192,384]{1,0:T(8,128)(2,1)S(1)} %get-tuple-element.158), channel_id=1, source_target_pairs={{0,4},{2,6},{4,0},{6,2},{8,12},{10,14},{12,8},{14,10},{16,20},{18,... | collective-permute-start | bytes 442376 | tf_op jit(solution)/shard_map/ppermute | solution.py:756
  24.1 5.7 %collective-permute-start.12 = (bf16[192,384]{1,0:T(8,128)(2,1)S(1)}, bf16[192,384]{1,0:T(8,128)(2,1)S(1)}, u32[]{:S(2)}, u32[]{:S(2)}) collective-permute-start(bf16[192,384]{1,0:T(8,128)(2,1)S(1)} %get-tuple-element.156), channel_id=1, source_target_pairs={{0,2},{2,0},{4,6},{6,4},{8,10},{10,8},{12,14},{14,12},{16,18},{18,... | collective-permute-start | bytes 442376 | tf_op jit(solution)/shard_map/ppermute | solution.py:756
  27.3 9.0 %collective-permute-start.11 = (bf16[400,384]{1,0:T(8,128)(2,1)S(1)}, bf16[400,384]{1,0:T(8,128)(2,1)S(1)}, u32[]{:S(2)}, u32[]{:S(2)}) collective-permute-start(bf16[400,384]{1,0:T(8,128)(2,1)S(1)} %get-tuple-element.155), channel_id=1, source_target_pairs={{0,2},{2,0},{4,6},{6,4},{8,10},{10,8},{12,14},{14,12},{16,18},{18,... | collective-permute-start | bytes 921608 | tf_op jit(solution)/shard_map/ppermute | solution.py:756
  27.9 8.2 %collective-permute-start.14 = (bf16[384,384]{1,0:T(8,128)(2,1)S(1)}, bf16[384,384]{1,0:T(8,128)(2,1)S(1)}, u32[]{:S(2)}, u32[]{:S(2)}) collective-permute-start(bf16[384,384]{1,0:T(8,128)(2,1)S(1)} %get-tuple-element.170), channel_id=1, source_target_pairs={{0,4},{2,6},{4,0},{6,2},{8,12},{10,14},{12,8},{14,10},{16,20},{18,... | collective-permute-start | bytes 884744 | tf_op jit(solution)/shard_map/ppermute | solution.py:756
  34.9 3.7 %collective-permute-start.16 = (bf16[1152,384]{1,0:T(8,128)(2,1)S(1)}, bf16[1152,384]{1,0:T(8,128)(2,1)S(1)}, u32[]{:S(2)}, u32[]{:S(2)}) collective-permute-start(bf16[1152,384]{1,0:T(8,128)(2,1)S(1)} %get-tuple-element.179.refs_1_), channel_id=1, source_target_pairs={{0,1},{1,0},{2,3},{3,2},{4,5},{5,4},{6,7},{7,6},{8,9},{9,8},{10,11... | collective-permute-start | bytes 2654216 | tf_op jit(solution)/shard_map/ppermute | solution.py:753
  35.0 3.7 %collective-permute-start.15 = (bf16[768,384]{1,0:T(8,128)(2,1)S(1)}, bf16[768,384]{1,0:T(8,128)(2,1)S(1)}, u32[]{:S(2)}, u32[]{:S(2)}) collective-permute-start(bf16[768,384]{1,0:T(8,128)(2,1)S(1)} %get-tuple-element.178.normed_t), channel_id=1, source_target_pairs={{0,1},{1,0},{2,3},{3,2},{4,5},{5,4},{6,7},{7,6},{8,9},{9,8},{10,11... | collective-permute-start | bytes 1769480 | tf_op jit(solution)/shard_map/ppermute | solution.py:753
  36.6 7.4 %collective-permute-start.19 = (bf16[304,384]{1,0:T(8,128)(2,1)S(1)}, bf16[304,384]{1,0:T(8,128)(2,1)S(1)}, u32[]{:S(2)}, u32[]{:S(2)}) collective-permute-start(bf16[304,384]{1,0:T(8,128)(2,1)S(1)} %get-tuple-element.174), channel_id=1, source_target_pairs={{0,4},{2,6},{4,0},{6,2},{8,12},{10,14},{12,8},{14,10},{16,20},{18,... | collective-permute-start | bytes 700424 | tf_op jit(solution)/shard_map/ppermute | solution.py:756
  37.3 6.7 %collective-permute-start.20 = (bf16[288,384]{1,0:T(8,128)(2,1)S(1)}, bf16[288,384]{1,0:T(8,128)(2,1)S(1)}, u32[]{:S(2)}, u32[]{:S(2)}) collective-permute-start(bf16[288,384]{1,0:T(8,128)(2,1)S(1)} %get-tuple-element.176), channel_id=1, source_target_pairs={{0,2},{2,0},{4,6},{6,4},{8,10},{10,8},{12,14},{14,12},{16,18},{18,... | collective-permute-start | bytes 663560 | tf_op jit(solution)/shard_map/ppermute | solution.py:756
  40.9 14.1 %collective-permute-start.17 = (bf16[576,384]{1,0:T(8,128)(2,1)S(1)}, bf16[576,384]{1,0:T(8,128)(2,1)S(1)}, u32[]{:S(2)}, u32[]{:S(2)}) collective-permute-start(bf16[576,384]{1,0:T(8,128)(2,1)S(1)} %get-tuple-element.181), channel_id=1, source_target_pairs={{0,2},{2,0},{4,6},{6,4},{8,10},{10,8},{12,14},{14,12},{16,18},{18,... | collective-permute-start | bytes 1327112 | tf_op jit(solution)/shard_map/ppermute | solution.py:756
  43.0 12.1 %collective-permute-start.18 = (bf16[576,384]{1,0:T(8,128)(2,1)S(1)}, bf16[576,384]{1,0:T(8,128)(2,1)S(1)}, u32[]{:S(2)}, u32[]{:S(2)}) collective-permute-start(bf16[576,384]{1,0:T(8,128)(2,1)S(1)} %get-tuple-element.183), channel_id=1, source_target_pairs={{0,4},{2,6},{4,0},{6,2},{8,12},{10,14},{12,8},{14,10},{16,20},{18,... | collective-permute-start | bytes 1327112 | tf_op jit(solution)/shard_map/ppermute | solution.py:756
  44.0 4.4 %copy-start.2 = (bf16[768,384]{1,0:T(8,128)(2,1)S(1)}, bf16[768,384]{1,0:T(8,128)(2,1)}, u32[]{:S(2)}) copy-start(bf16[768,384]{1,0:T(8,128)(2,1)} %refs_2_.1) | copy-start | bytes 1769476
  44.0 4.4 %copy-start.3 = (bf16[768,384]{1,0:T(8,128)(2,1)S(1)}, bf16[768,384]{1,0:T(8,128)(2,1)}, u32[]{:S(2)}) copy-start(bf16[768,384]{1,0:T(8,128)(2,1)} %refs_3_.1) | copy-start | bytes 1769476
  44.0 4.4 %copy-start.4 = (bf16[768,384]{1,0:T(8,128)(2,1)S(1)}, bf16[768,384]{1,0:T(8,128)(2,1)}, u32[]{:S(2)}) copy-start(bf16[768,384]{1,0:T(8,128)(2,1)} %refs_4_.1) | copy-start | bytes 1769476
  44.1 17.0 %collective-permute-start.23 = (bf16[160,384]{1,0:T(8,128)(2,1)S(1)}, bf16[160,384]{1,0:T(8,128)(2,1)S(1)}, u32[]{:S(2)}, u32[]{:S(2)}) collective-permute-start(bf16[160,384]{1,0:T(8,128)(2,1)S(1)} %get-tuple-element.189.near), channel_id=1, source_target_pairs={{0,8},{2,10},{4,12},{6,14},{8,0},{10,2},{12,4},{14,6},{16,24},{18,... | collective-permute-start | bytes 368648 | tf_op jit(solution)/shard_map/ppermute | solution.py:759
  45.8 15.4 %collective-permute-start.25 = (bf16[144,384]{1,0:T(8,128)(2,1)S(1)}, bf16[144,384]{1,0:T(8,128)(2,1)S(1)}, u32[]{:S(2)}, u32[]{:S(2)}) collective-permute-start(bf16[144,384]{1,0:T(8,128)(2,1)S(1)} %get-tuple-element.191), channel_id=1, source_target_pairs={{0,24},{2,26},{4,28},{6,30},{8,16},{10,18},{12,20},{14,22},{16,8},... | collective-permute-start | bytes 331784 | tf_op jit(solution)/shard_map/ppermute | solution.py:759
  48.2 12.9 %collective-permute-start.24 = (bf16[144,384]{1,0:T(8,128)(2,1)S(1)}, bf16[144,384]{1,0:T(8,128)(2,1)S(1)}, u32[]{:S(2)}, u32[]{:S(2)}) collective-permute-start(bf16[144,384]{1,0:T(8,128)(2,1)S(1)} %get-tuple-element.190), channel_id=1, source_target_pairs={{0,16},{2,18},{4,20},{6,22},{8,24},{10,26},{12,28},{14,30},{16,0},... | collective-permute-start | bytes 331784 | tf_op jit(solution)/shard_map/ppermute | solution.py:759
  55.0 1.3 %collective-permute-start.21 = (bf16[48,384]{1,0:T(8,128)(2,1)S(1)}, bf16[48,384]{1,0:T(8,128)(2,1)S(1)}, u32[]{:S(2)}, u32[]{:S(2)}) collective-permute-start(bf16[48,384]{1,0:T(8,128)(2,1)S(1)} %get-tuple-element.194), channel_id=1, source_target_pairs={{0,1},{1,0},{2,3},{3,2},{4,5},{5,4},{6,7},{7,6},{8,9},{9,8},{10,11... | collective-permute-start | bytes 110600 | tf_op jit(solution)/shard_map/ppermute | solution.py:753
  56.5 9.2 %collective-permute-start.26 = (bf16[288,384]{1,0:T(8,128)(2,1)S(1)}, bf16[288,384]{1,0:T(8,128)(2,1)S(1)}, u32[]{:S(2)}, u32[]{:S(2)}) collective-permute-start(bf16[288,384]{1,0:T(8,128)(2,1)S(1)} %get-tuple-element.199), channel_id=1, source_target_pairs={{0,2},{2,0},{4,6},{6,4},{8,10},{10,8},{12,14},{14,12},{16,18},{18,... | collective-permute-start | bytes 663560 | tf_op jit(solution)/shard_map/ppermute | solution.py:756
  58.5 8.9 %collective-permute-start.22 = (bf16[336,384]{1,0:T(8,128)(2,1)S(1)}, bf16[336,384]{1,0:T(8,128)(2,1)S(1)}, u32[]{:S(2)}, u32[]{:S(2)}) collective-permute-start(bf16[336,384]{1,0:T(8,128)(2,1)S(1)} %get-tuple-element.197), channel_id=1, source_target_pairs={{0,4},{2,6},{4,0},{6,2},{8,12},{10,14},{12,8},{14,10},{16,20},{18,... | collective-permute-start | bytes 774152 | tf_op jit(solution)/shard_map/ppermute | solution.py:756
  61.2 9.9 %collective-permute-start.37 = (bf16[144,384]{1,0:T(8,128)(2,1)S(1)}, bf16[144,384]{1,0:T(8,128)(2,1)S(1)}, u32[]{:S(2)}, u32[]{:S(2)}) collective-permute-start(bf16[144,384]{1,0:T(8,128)(2,1)S(1)} %get-tuple-element.203), channel_id=1, source_target_pairs={{0,24},{2,26},{4,28},{6,30},{8,16},{10,18},{12,20},{14,22},{16,8},... | collective-permute-start | bytes 331784 | tf_op jit(solution)/shard_map/ppermute | solution.py:759
  64.2 11.7 %collective-permute-start.36 = (bf16[160,384]{1,0:T(8,128)(2,1)S(1)}, bf16[160,384]{1,0:T(8,128)(2,1)S(1)}, u32[]{:S(2)}, u32[]{:S(2)}) collective-permute-start(bf16[160,384]{1,0:T(8,128)(2,1)S(1)} %get-tuple-element.217.own), channel_id=1, source_target_pairs={{0,16},{2,18},{4,20},{6,22},{8,24},{10,26},{12,28},{14,30},{16,0},... | collective-permute-start | bytes 368648 | tf_op jit(solution)/shard_map/ppermute | solution.py:759
  64.5 11.4 %collective-permute-start.35 = (bf16[144,384]{1,0:T(8,128)(2,1)S(1)}, bf16[144,384]{1,0:T(8,128)(2,1)S(1)}, u32[]{:S(2)}, u32[]{:S(2)}) collective-permute-start(bf16[144,384]{1,0:T(8,128)(2,1)S(1)} %get-tuple-element.203), channel_id=1, source_target_pairs={{0,8},{2,10},{4,12},{6,14},{8,0},{10,2},{12,4},{14,6},{16,24},{18,... | collective-permute-start | bytes 331784 | tf_op jit(solution)/shard_map/ppermute | solution.py:759
  67.5 15.1 %collective-permute-start.27 = (bf16[192,384]{1,0:T(8,128)(2,1)S(1)}, bf16[192,384]{1,0:T(8,128)(2,1)S(1)}, u32[]{:S(2)}, u32[]{:S(2)}) collective-permute-start(bf16[192,384]{1,0:T(8,128)(2,1)S(1)} %get-tuple-element.207.near), channel_id=1, source_target_pairs={{0,8},{2,10},{4,12},{6,14},{8,0},{10,2},{12,4},{14,6},{16,24},{18,... | collective-permute-start | bytes 442376 | tf_op jit(solution)/shard_map/ppermute | solution.py:759
  69.4 13.2 %collective-permute-start.28 = (bf16[144,384]{1,0:T(8,128)(2,1)S(1)}, bf16[144,384]{1,0:T(8,128)(2,1)S(1)}, u32[]{:S(2)}, u32[]{:S(2)}) collective-permute-start(bf16[144,384]{1,0:T(8,128)(2,1)S(1)} %get-tuple-element.208), channel_id=1, source_target_pairs={{0,16},{2,18},{4,20},{6,22},{8,24},{10,26},{12,28},{14,30},{16,0},... | collective-permute-start | bytes 331784 | tf_op jit(solution)/shard_map/ppermute | solution.py:759
  71.1 11.5 %collective-permute-start.29 = (bf16[144,384]{1,0:T(8,128)(2,1)S(1)}, bf16[144,384]{1,0:T(8,128)(2,1)S(1)}, u32[]{:S(2)}, u32[]{:S(2)}) collective-permute-start(bf16[144,384]{1,0:T(8,128)(2,1)S(1)} %get-tuple-element.209), channel_id=1, source_target_pairs={{0,24},{2,26},{4,28},{6,30},{8,16},{10,18},{12,20},{14,22},{16,8},... | collective-permute-start | bytes 331784 | tf_op jit(solution)/shard_map/ppermute | solution.py:759
  76.8 10.6 %collective-permute-start.40 = (bf16[576,384]{1,0:T(8,128)(2,1)S(1)}, bf16[576,384]{1,0:T(8,128)(2,1)S(1)}, u32[]{:S(2)}, u32[]{:S(2)}) collective-permute-start(bf16[576,384]{1,0:T(8,128)(2,1)S(1)} %get-tuple-element.228.refs_0_), channel_id=1, source_target_pairs={{0,4},{2,6},{4,0},{6,2},{8,12},{10,14},{12,8},{14,10},{16,20},{18,... | collective-permute-start | bytes 1327112 | tf_op jit(solution)/shard_map/ppermute | solution.py:756
  78.1 9.7 %collective-permute-start.39 = (bf16[576,384]{1,0:T(8,128)(2,1)S(1)}, bf16[576,384]{1,0:T(8,128)(2,1)S(1)}, u32[]{:S(2)}, u32[]{:S(2)}) collective-permute-start(bf16[576,384]{1,0:T(8,128)(2,1)S(1)} %get-tuple-element.228.refs_0_), channel_id=1, source_target_pairs={{0,2},{2,0},{4,6},{6,4},{8,10},{10,8},{12,14},{14,12},{16,18},{18,... | collective-permute-start | bytes 1327112 | tf_op jit(solution)/shard_map/ppermute | solution.py:756
  82.7 12.9 %collective-permute-start.31 = (bf16[192,384]{1,0:T(8,128)(2,1)S(1)}, bf16[192,384]{1,0:T(8,128)(2,1)S(1)}, u32[]{:S(2)}, u32[]{:S(2)}) collective-permute-start(bf16[192,384]{1,0:T(8,128)(2,1)S(1)} %get-tuple-element.210.own), channel_id=1, source_target_pairs={{0,16},{2,18},{4,20},{6,22},{8,24},{10,26},{12,28},{14,30},{16,0},... | collective-permute-start | bytes 442376 | tf_op jit(solution)/shard_map/ppermute | solution.py:759
  85.9 8.1 %collective-permute-start.32 = (bf16[144,384]{1,0:T(8,128)(2,1)S(1)}, bf16[144,384]{1,0:T(8,128)(2,1)S(1)}, u32[]{:S(2)}, u32[]{:S(2)}) collective-permute-start(bf16[144,384]{1,0:T(8,128)(2,1)S(1)} %get-tuple-element.211), channel_id=1, source_target_pairs={{0,24},{2,26},{4,28},{6,30},{8,16},{10,18},{12,20},{14,22},{16,8},... | collective-permute-start | bytes 331784 | tf_op jit(solution)/shard_map/ppermute | solution.py:759
  87.3 6.7 %collective-permute-start.30 = (bf16[144,384]{1,0:T(8,128)(2,1)S(1)}, bf16[144,384]{1,0:T(8,128)(2,1)S(1)}, u32[]{:S(2)}, u32[]{:S(2)}) collective-permute-start(bf16[144,384]{1,0:T(8,128)(2,1)S(1)} %get-tuple-element.211), channel_id=1, source_target_pairs={{0,8},{2,10},{4,12},{6,14},{8,0},{10,2},{12,4},{14,6},{16,24},{18,... | collective-permute-start | bytes 331784 | tf_op jit(solution)/shard_map/ppermute | solution.py:759
  87.3 12.5 %collective-permute-start.41 = (bf16[288,384]{1,0:T(8,128)(2,1)S(1)}, bf16[288,384]{1,0:T(8,128)(2,1)S(1)}, u32[]{:S(2)}, u32[]{:S(2)}) collective-permute-start(bf16[288,384]{1,0:T(8,128)(2,1)S(1)} %slice.20), channel_id=1, source_target_pairs={{0,2},{2,0},{4,6},{6,4},{8,10},{10,8},{12,14},{14,12},{16,18},{18,... | collective-permute-start | bytes 663560 | tf_op jit(solution)/shard_map/ppermute | solution.py:756
  87.8 12.0 %collective-permute-start.42 = (bf16[288,384]{1,0:T(8,128)(2,1)S(1)}, bf16[288,384]{1,0:T(8,128)(2,1)S(1)}, u32[]{:S(2)}, u32[]{:S(2)}) collective-permute-start(bf16[288,384]{1,0:T(8,128)(2,1)S(1)} %slice.21), channel_id=1, source_target_pairs={{0,4},{2,6},{4,0},{6,2},{8,12},{10,14},{12,8},{14,10},{16,20},{18,... | collective-permute-start | bytes 663560 | tf_op jit(solution)/shard_map/ppermute | solution.py:756
  95.7 3.5 %collective-permute-start.38 = (f32[16,384]{1,0:T(8,128)S(1)}, f32[16,384]{1,0:T(8,128)S(1)}, u32[]{:S(2)}, u32[]{:S(2)}) collective-permute-start(f32[16,384]{1,0:T(8,128)S(1)} %get-tuple-element.222.small), channel_id=1, source_target_pairs={{0,1},{1,0},{2,3},{3,2},{4,5},{5,4},{6,7},{7,6},{8,9},{9,8},{10,11... | collective-permute-start | bytes 73736 | tf_op jit(solution)/shard_map/ppermute | solution.py:753
  95.8 12.6 %collective-permute-start.34 = (bf16[576,384]{1,0:T(8,128)(2,1)S(1)}, bf16[576,384]{1,0:T(8,128)(2,1)S(1)}, u32[]{:S(2)}, u32[]{:S(2)}) collective-permute-start(bf16[576,384]{1,0:T(8,128)(2,1)S(1)} %get-tuple-element.212.refs_0_), channel_id=1, source_target_pairs={{0,4},{2,6},{4,0},{6,2},{8,12},{10,14},{12,8},{14,10},{16,20},{18,... | collective-permute-start | bytes 1327112 | tf_op jit(solution)/shard_map/ppermute | solution.py:756
  96.2 13.0 %collective-permute-start.33 = (bf16[624,384]{1,0:T(8,128)(2,1)S(1)}, bf16[624,384]{1,0:T(8,128)(2,1)S(1)}, u32[]{:S(2)}, u32[]{:S(2)}) collective-permute-start(bf16[624,384]{1,0:T(8,128)(2,1)S(1)} %get-tuple-element.216), channel_id=1, source_target_pairs={{0,2},{2,0},{4,6},{6,4},{8,10},{10,8},{12,14},{14,12},{16,18},{18,... | collective-permute-start | bytes 1437704 | tf_op jit(solution)/shard_map/ppermute | solution.py:756
  109.3 6.7 %collective-permute-start.45 = (bf16[288,384]{1,0:T(8,128)(2,1)S(1)}, bf16[288,384]{1,0:T(8,128)(2,1)S(1)}, u32[]{:S(2)}, u32[]{:S(2)}) collective-permute-start(bf16[288,384]{1,0:T(8,128)(2,1)S(1)} %slice.19), channel_id=1, source_target_pairs={{0,4},{2,6},{4,0},{6,2},{8,12},{10,14},{12,8},{14,10},{16,20},{18,... | collective-permute-start | bytes 663560 | tf_op jit(solution)/shard_map/ppermute | solution.py:756
  111.0 6.4 %collective-permute-start.44 = (bf16[288,384]{1,0:T(8,128)(2,1)S(1)}, bf16[288,384]{1,0:T(8,128)(2,1)S(1)}, u32[]{:S(2)}, u32[]{:S(2)}) collective-permute-start(bf16[288,384]{1,0:T(8,128)(2,1)S(1)} %slice.18), channel_id=1, source_target_pairs={{0,2},{2,0},{4,6},{6,4},{8,10},{10,8},{12,14},{14,12},{16,18},{18,... | collective-permute-start | bytes 663560 | tf_op jit(solution)/shard_map/ppermute | solution.py:756
  111.5 2.1 %collective-permute-start.43 = (f32[48,384]{1,0:T(8,128)S(1)}, f32[48,384]{1,0:T(8,128)S(1)}, u32[]{:S(2)}, u32[]{:S(2)}) collective-permute-start(f32[48,384]{1,0:T(8,128)S(1)} %convert_add_fusion), channel_id=1, source_target_pairs={{0,1},{1,0},{2,3},{3,2},{4,5},{5,4},{6,7},{7,6},{8,9},{9,8},{10,11... | collective-permute-start | bytes 221192 | tf_op jit(solution)/shard_map/ppermute | solution.py:753
